TPU v7x, 32 devices: a whole 2x2x4 slice. The times are simulated.
32 devices in a mesh: items: 2 (over core), height: 4 (over y, x), tensor: 4 (over z).
Axes of the slice: x: 2, y: 2, z: 4, core: 2. Of those that a mesh axis runs over, the one named last changes fastest.
Arguments:
- hidden: float32 [2, 1024, 1280], P('items', 'height'), may hold values from -48 to 48
- text_states: float32 [2, 77, 2048], P('items'), may hold values from -6 to 6
- bucket: int32 [2], P('items'), may hold values from 0 to 2
- timestep: int32 [2], P('items'), may hold values from 0 to 999
- gain_in: float32 [1280], P(('items', 'height')), may hold values from 0.5 to 1.5
- conv_first: float32 [3, 3, 1280, 1280], P(None, None, ('items', 'height'), 'tensor'), may hold values from -0.0546875 to 0.0546875
- time_weight: float32 [1280, 1280], P(('items', 'height'), 'tensor'), may hold values from -0.15625 to 0.15625
- gain_mid: float32 [1280], P('tensor'), may hold values from 0.5 to 1.5
- conv_second: float32 [3, 3, 1280, 1280], P(None, None, 'tensor', ('items', 'height')), may hold values from -0.0546875 to 0.0546875
- gain_attn_norm: float32 [1280], P('tensor'), may hold values from 0.5 to 1.5
- proj_in: float32 [1280, 1280], P('tensor', ('items', 'height')), may hold values from -0.15625 to 0.15625
- gain_self: float32 [1280], P(('items', 'height')), may hold values from 0.5 to 1.5
- query_self: float32 [1280, 1280], P(('items', 'height'), 'tensor'), may hold values from -0.15625 to 0.15625
- key_self: float32 [1280, 1280], P(('items', 'height'), 'tensor'), may hold values from -0.25 to 0.25
- value_self: float32 [1280, 1280], P(('items', 'height'), 'tensor'), may hold values from -0.15625 to 0.15625
- out_self: float32 [1280, 1280], P('tensor', ('items', 'height')), may hold values from -2 to 2
- gain_cross: float32 [1280], P(('items', 'height')), may hold values from 0.5 to 1.5
- query_cross: float32 [1280, 1280], P(('items', 'height'), 'tensor'), may hold values from -0.25 to 0.25
- key_cross: float32 [2048, 1280], P(('items', 'height'), 'tensor'), may hold values from -0.125 to 0.125
- value_cross: float32 [2048, 1280], P(('items', 'height'), 'tensor'), may hold values from -0.125 to 0.125
- out_cross: float32 [1280, 1280], P('tensor', ('items', 'height')), may hold values from -0.5 to 0.5
- gain_ff: float32 [1280], P(('items', 'height')), may hold values from 0.5 to 1.5
- ff_in: float32 [1280, 2, 5120], P(('items', 'height'), None, 'tensor'), may hold values from -0.15625 to 0.15625
- ff_out: float32 [5120, 1280], P('tensor', ('items', 'height')), may hold values from -0.078125 to 0.078125
- proj_out: float32 [1280, 1280], P(('items', 'height'), 'tensor'), may hold values from -0.15625 to 0.15625
- cotangent: float32 [2, 1024, 1280], P('items', 'height', 'tensor'), may hold values from -6 to 6
Outputs:
- output: float32 [2, 1024, 1280], P('items', 'height', 'tensor')
- grad_hidden: float32 [2, 1024, 1280], P('items', 'height')
- grad_gain_in: float32 [1280], P(('items', 'height'))
- grad_conv_first: float32 [3, 3, 1280, 1280], P(None, None, ('items', 'height'), 'tensor')
- grad_time_weight: float32 [1280, 1280], P(('items', 'height'), 'tensor')
- grad_gain_mid: float32 [1280], P('tensor')
- grad_conv_second: float32 [3, 3, 1280, 1280], P(None, None, 'tensor', ('items', 'height'))
- grad_gain_attn_norm: float32 [1280], P('tensor')
- grad_proj_in: float32 [1280, 1280], P('tensor', ('items', 'height'))
- grad_gain_self: float32 [1280], P(('items', 'height'))
- grad_query_self: float32 [1280, 1280], P(('items', 'height'), 'tensor')
- grad_key_self: float32 [1280, 1280], P(('items', 'height'), 'tensor')
- grad_value_self: float32 [1280, 1280], P(('items', 'height'), 'tensor')
- grad_out_self: float32 [1280, 1280], P('tensor', ('items', 'height'))
- grad_gain_cross: float32 [1280], P(('items', 'height'))
- grad_query_cross: float32 [1280, 1280], P(('items', 'height'), 'tensor')
- grad_key_cross: float32 [2048, 1280], P(('items', 'height'), 'tensor')
- grad_value_cross: float32 [2048, 1280], P(('items', 'height'), 'tensor')
- grad_out_cross: float32 [1280, 1280], P('tensor', ('items', 'height'))
- grad_gain_ff: float32 [1280], P(('items', 'height'))
- grad_ff_in: float32 [1280, 2, 5120], P(('items', 'height'), None, 'tensor')
- grad_ff_out: float32 [5120, 1280], P('tensor', ('items', 'height'))
- grad_proj_out: float32 [1280, 1280], P(('items', 'height'), 'tensor')
Inputs may be any that keep to these rules, and one draw needn't show every extreme that they name: bucket 0 is a 32 by 32 image, 1 is 24 by 40, 2 is 20 by 48.
All inputs are finite; a program needn't handle non-finite values.
Results may differ from a plain program's by a relative error of at most 0.0003.
Values sent between devices are 32-bit elements; how exact they have to be, the bound alone decides.
No kernel may reach another device: no remote copies, remote signals or barrier semaphores. Data moves between devices by JAX's collectives and lax.ppermute only.
A program may use at most 384 MiB of HBM per device.

v0:
```python
import functools
import math

import jax
import jax.numpy as jnp
from jax import lax
from jax.experimental import pallas as pl
from jax.experimental.pallas import tpu as pltpu
from jax.sharding import PartitionSpec as P

HEAD_DIM = 64
GROUPS = 32
EDGE = 48


highest = lax.Precision.HIGHEST
norm_eps = 1e-05
masked_score = -1e30
edge_margin = 56
high = lax.Precision.HIGH
margin = 64
I, H, T = "items", "height", "tensor"
IH = (I, H)
E0 = "bc,bn->cn"
E1 = "bhqk,bkhd->bqhd"
E2 = "bhqk,bqhd->bkhd"
E3 = "bqhd,bkhd->bhqk"
E4 = "bqhd,bqhd->bhq"
E5 = "bsc,bsjf->cjf"
E6 = "bsc,cjf->bsjf"
E7 = "bsjf,cjf->bsc"
E8 = "bsk,bsn->kn"
E9 = "bsk,kn->bsn"
E10 = "bsn,kn->bsk"
QK, PV, PQ = "qhd,khd->hqk", "hqk,khd->qhd", "hqk,qhd->khd"


def padded_2(block, sides, width):
    for axis, dim in sides:
        count = lax.axis_size(axis)
        forward = [(i, i + 1) for i in range(count - 1)]
        backward = [(target, source) for source, target in forward]
        low = lax.ppermute(
            lax.slice_in_dim(block, block.shape[dim] - width, None, axis=dim), axis, forward
        )
        high = lax.ppermute(lax.slice_in_dim(block, 0, width, axis=dim), axis, backward)
        block = jnp.concatenate([low, block, high], axis=dim)
    return block


def grid_shape(bucket):
    strip_rows = jnp.where(bucket == 0, 8, jnp.where(bucket == 1, 6, 5)).astype(jnp.int32)
    strip_width = jnp.where(bucket == 0, 32, jnp.where(bucket == 1, 40, 48)).astype(jnp.int32)
    return (strip_rows, strip_width)


def tokens_dot(values, weight):
    return jnp.einsum(E9, values, weight, precision=highest)


def tokens_back(grad_values, weight):
    return jnp.einsum(E10, grad_values, weight, precision=highest)


def tokens_grad(values, grad_values):
    return jnp.einsum(E8, values, grad_values, precision=highest)


def tensor_sum(values):
    return lax.psum(values, T)


def expand_groups(stat, size_group):
    return jnp.repeat(stat, size_group, axis=1)[:, None, :]


def group_stats(values, valid_col, group_count, counts):
    item_count, slot_count, channels = values.shape
    size_group = channels // group_count
    grouped = (values * valid_col).reshape(item_count, slot_count, group_count, size_group)
    sum_values = jnp.sum(grouped, axis=(1, 3))
    sum_squares = jnp.sum(grouped * grouped, axis=(1, 3))
    sum_values, sum_squares = lax.psum((sum_values, sum_squares), H)
    mean_val = sum_values / counts[:, None]
    var_val = sum_squares / counts[:, None] - mean_val * mean_val
    return (
        expand_groups(mean_val, size_group),
        expand_groups(lax.rsqrt(var_val + norm_eps), size_group),
    )


def group_back(grad_out, centred, inv_std, gain_vector, valid_col, group_count, counts):
    item_count, slot_count, channels = grad_out.shape
    size_group = channels // group_count
    scaled = grad_out * gain_vector * valid_col
    sum_first = jnp.sum(
        scaled.reshape(item_count, slot_count, group_count, size_group), axis=(1, 3)
    )
    sum_second = jnp.sum(
        (scaled * centred).reshape(item_count, slot_count, group_count, size_group), axis=(1, 3)
    )
    sum_first, sum_second = lax.psum((sum_first, sum_second), H)
    mean_first = expand_groups(sum_first / counts[:, None], size_group)
    mean_second = expand_groups(sum_second / counts[:, None], size_group)
    grad_in = inv_std * (scaled - mean_first - centred * mean_second) * valid_col
    return (grad_in, jnp.sum(grad_out * centred, axis=(0, 1)))


def layer_norm(values, gain_vector):
    mean_val = jnp.mean(values, axis=-1, keepdims=True)
    var_val = jnp.mean(values * values, axis=-1, keepdims=True) - mean_val * mean_val
    inv_std = lax.rsqrt(var_val + norm_eps)
    centred = (values - mean_val) * inv_std
    return (centred * gain_vector, centred, inv_std)


def layer_back(grad_out, centred, inv_std, gain_vector):
    scaled = grad_out * gain_vector
    grad_in = inv_std * (
        scaled
        - jnp.mean(scaled, axis=-1, keepdims=True)
        - centred * jnp.mean(scaled * centred, axis=-1, keepdims=True)
    )
    return (grad_in, jnp.sum(grad_out * centred, axis=(0, 1)))


def edge_rows(values, strip_rows, strip_width):
    item_count, slot_count, channels = values.shape
    position = jnp.arange(EDGE, dtype=jnp.int32)

    def edge_one_item(item_vals, rows_here, width_here):
        keep_mask = (position < width_here)[:, None].astype(jnp.float32)
        padded = jnp.concatenate([item_vals, jnp.zeros((EDGE, channels), jnp.float32)], axis=0)
        top_row = item_vals[:EDGE] * keep_mask
        bottom_row = (
            lax.dynamic_slice_in_dim(padded, (rows_here - 1) * width_here, EDGE, 0) * keep_mask
        )
        return jnp.stack([top_row, bottom_row])

    return jax.vmap(edge_one_item)(values, strip_rows, strip_width)


def neighbour_stack(values, strip_rows, strip_width):
    edge_pair = edge_rows(values, strip_rows, strip_width)
    beside_all = padded_2(edge_pair, ((H, 1),), 1)
    item_count, slot_count, channels = values.shape
    position = jnp.arange(slot_count, dtype=jnp.int32)

    def neighbour_one_item(item_vals, item_around, rows_here, width_here):
        cell_span = rows_here * width_here
        extended = jnp.zeros((2 * edge_margin + slot_count, channels), jnp.float32)
        extended = lax.dynamic_update_slice_in_dim(
            extended, item_around[0], edge_margin - width_here, 0
        )
        extended = lax.dynamic_update_slice_in_dim(extended, item_vals, edge_margin, 0)
        extended = lax.dynamic_update_slice_in_dim(
            extended, item_around[3], edge_margin + cell_span, 0
        )
        column = position % width_here
        shifted_list = []
        for row_step in (-1, 0, 1):
            for col_step in (-1, 0, 1):
                shifted = lax.dynamic_slice_in_dim(
                    extended, edge_margin + row_step * width_here + col_step, slot_count, 0
                )
                keep_mask = (
                    (column + col_step >= 0)
                    & (column + col_step < width_here)
                    & (position < cell_span)
                )
                shifted_list.append(shifted * keep_mask[:, None].astype(jnp.float32))
        return jnp.stack(shifted_list, axis=1)

    return jax.vmap(neighbour_one_item)(values, beside_all, strip_rows, strip_width)


def conv_apply(neighbours, weight):
    item_count, slot_count = (neighbours.shape[0], neighbours.shape[1])
    flattened = neighbours.reshape(item_count, slot_count, -1)
    return tokens_dot(flattened, weight.reshape(-1, weight.shape[3]))


def conv_input_grad(neighbours_grad, weight):
    flipped = jnp.transpose(weight[::-1, ::-1], (0, 1, 3, 2))
    return conv_apply(neighbours_grad, flipped)


def conv_weight_grad(neighbours, grad_out, weight_shape):
    flattened = neighbours.reshape(neighbours.shape[0], neighbours.shape[1], -1)
    return tokens_grad(flattened, grad_out).reshape(weight_shape)


def time_features(timestep, channels):
    half_width = channels // 2
    frequency = jnp.exp(-math.log(10000.0) * jnp.arange(half_width, dtype=jnp.float32) / half_width)
    angles = timestep.astype(jnp.float32)[:, None] * frequency[None, :]
    return jnp.concatenate([jnp.cos(angles), jnp.sin(angles)], axis=1)


def exact_gelu(values):
    return jax.nn.gelu(values, approximate=False)


def head_split(values, heads_here):
    return values.reshape(
        values.shape[0], values.shape[1], heads_here, values.shape[2] // heads_here
    )


def score_block(queries, keys_all, key_valid, heads_here):
    head_size = queries.shape[2] // heads_here
    scores = jnp.einsum(
        E3,
        head_split(queries, heads_here),
        head_split(keys_all, heads_here),
        precision=highest,
    ) * (1.0 / math.sqrt(head_size))
    return jnp.where(key_valid[:, None, None, :], scores, masked_score)


def attend(queries, keys_all, values_all, key_valid, heads_here):
    scores = score_block(queries, keys_all, key_valid, heads_here)
    row_peak = jnp.max(scores, axis=-1, keepdims=True)
    exponent = jnp.exp(scores - row_peak)
    row_total = jnp.sum(exponent, axis=-1, keepdims=True)
    soft_weights = exponent / row_total
    attended = jnp.einsum(
        E1, soft_weights, head_split(values_all, heads_here), precision=highest
    )
    return (attended.reshape(queries.shape), row_peak + jnp.log(row_total))


def attend_back(
    queries, keys_all, values_all, key_valid, heads_here, attended, log_total, grad_attended
):
    head_size = queries.shape[2] // heads_here
    scaling = 1.0 / math.sqrt(head_size)
    soft_weights = jnp.exp(score_block(queries, keys_all, key_valid, heads_here) - log_total)
    grad_heads = head_split(grad_attended, heads_here)
    grad_soft = jnp.einsum(
        E3, grad_heads, head_split(values_all, heads_here), precision=highest
    )
    row_delta = jnp.einsum(
        E4, grad_heads, head_split(attended, heads_here), precision=highest
    )
    grad_scores = soft_weights * (grad_soft - row_delta[..., None])
    grad_query = (
        jnp.einsum(
            E1, grad_scores, head_split(keys_all, heads_here), precision=highest
        )
        * scaling
    )
    grad_key = (
        jnp.einsum(
            E2, grad_scores, head_split(queries, heads_here), precision=highest
        )
        * scaling
    )
    grad_value = jnp.einsum(E2, soft_weights, grad_heads, precision=highest)
    return (
        grad_query.reshape(queries.shape),
        grad_key.reshape(keys_all.shape),
        grad_value.reshape(values_all.shape),
    )


def shards(
    hidden,
    text_states,
    bucket,
    timestep,
    gain_in,
    conv_first,
    time_weight,
    gain_mid,
    conv_second,
    gain_attn_norm,
    proj_in,
    gain_self,
    query_self,
    key_self,
    value_self,
    out_self,
    gain_cross,
    query_cross,
    key_cross,
    value_cross,
    out_cross,
    gain_ff,
    ff_in,
    ff_out,
    proj_out,
    cotangent,
):
    item_count, slot_count, channels = hidden.shape
    local_width = gain_mid.shape[0]
    local_groups = GROUPS * local_width // channels
    heads_here = local_width // HEAD_DIM
    height_count = lax.axis_size(H)
    width_ih = lax.axis_size(I) * lax.axis_size(H)
    offset = lax.axis_index(T) * local_width
    strip_rows, strip_width = grid_shape(bucket)
    cell_span = strip_rows * strip_width
    position = jnp.arange(slot_count, dtype=jnp.int32)
    valid_mask = position[None, :] < cell_span[:, None]
    valid_col = valid_mask[:, :, None].astype(jnp.float32)
    full_counts = (height_count * cell_span * (channels // GROUPS)).astype(jnp.float32)
    key_valid = jnp.tile(valid_mask, (1, height_count))
    text_valid = jnp.ones((item_count, text_states.shape[1]), dtype=bool)
    resnet_full = (
        lax.all_gather(gain_in, IH, axis=0, tiled=True),
        lax.all_gather(conv_first, IH, axis=2, tiled=True),
        lax.all_gather(time_weight, IH, axis=0, tiled=True),
        lax.all_gather(conv_second, IH, axis=3, tiled=True),
    )
    block_full = (
        lax.all_gather(proj_in, IH, axis=1, tiled=True),
        lax.all_gather(gain_self, IH, axis=0, tiled=True),
        lax.all_gather(query_self, IH, axis=0, tiled=True),
        lax.all_gather(key_self, IH, axis=0, tiled=True),
        lax.all_gather(value_self, IH, axis=0, tiled=True),
        lax.all_gather(out_self, IH, axis=1, tiled=True),
        lax.all_gather(gain_cross, IH, axis=0, tiled=True),
        lax.all_gather(query_cross, IH, axis=0, tiled=True),
        lax.all_gather(key_cross, IH, axis=0, tiled=True),
        lax.all_gather(value_cross, IH, axis=0, tiled=True),
        lax.all_gather(out_cross, IH, axis=1, tiled=True),
        lax.all_gather(gain_ff, IH, axis=0, tiled=True),
        lax.all_gather(ff_in, IH, axis=0, tiled=True),
        lax.all_gather(ff_out, IH, axis=1, tiled=True),
        lax.all_gather(proj_out, IH, axis=0, tiled=True),
    )
    gain_in_full, conv_first_full, time_full, conv_second_full = resnet_full
    (
        proj_in_full,
        gain_self_full,
        query_self_full,
        key_self_full,
        value_self_full,
        out_self_full,
        gain_cross_full,
        query_cross_full,
        key_cross_full,
        value_cross_full,
        out_cross_full,
        gain_ff_full,
        ff_in_full,
        ff_out_full,
        proj_out_full,
    ) = block_full
    source = hidden * valid_col
    mean_one, inv_one = group_stats(source, valid_col, GROUPS, full_counts)
    centred_one = (source - mean_one) * inv_one * valid_col
    norm_one = centred_one * gain_in_full
    act_one, silu_pull_one = jax.vjp(jax.nn.silu, norm_one)
    stack_one = neighbour_stack(act_one, strip_rows, strip_width)
    silu_features = jax.nn.silu(time_features(timestep, channels))
    time_term = jnp.dot(
        silu_features, time_full, precision=highest, preferred_element_type=jnp.float32
    )
    conv_one = (conv_apply(stack_one, conv_first_full) + time_term[:, None, :]) * valid_col
    mean_two, inv_two = group_stats(conv_one, valid_col, local_groups, full_counts)
    centred_two = (conv_one - mean_two) * inv_two * valid_col
    norm_two = centred_two * gain_mid
    act_two, silu_pull_two = jax.vjp(jax.nn.silu, norm_two)
    stack_two = neighbour_stack(act_two, strip_rows, strip_width)
    conv_two = tensor_sum(conv_apply(stack_two, conv_second_full)) * valid_col
    residual = source + conv_two
    residual_local = lax.dynamic_slice_in_dim(residual, offset, local_width, 2)
    mean_three, inv_three = group_stats(residual_local, valid_col, local_groups, full_counts)
    centred_three = (residual_local - mean_three) * inv_three * valid_col
    norm_three = centred_three * gain_attn_norm
    projected = tensor_sum(tokens_dot(norm_three, proj_in_full))
    normed_self, centred_self, inv_self = layer_norm(projected, gain_self_full)
    queries = tokens_dot(normed_self, query_self_full)
    keys_here = tokens_dot(normed_self, key_self_full)
    values_here = tokens_dot(normed_self, value_self_full)
    keys_all, values_all = (
        lax.all_gather(keys_here, H, axis=1, tiled=True),
        lax.all_gather(values_here, H, axis=1, tiled=True),
    )
    attn_self, total_self = attend(queries, keys_all, values_all, key_valid, heads_here)
    after_self = projected + tensor_sum(tokens_dot(attn_self, out_self_full))
    normed_cross, centred_cross, inv_cross = layer_norm(after_self, gain_cross_full)
    queries_cross = tokens_dot(normed_cross, query_cross_full)
    keys_text = tokens_dot(text_states, key_cross_full)
    values_text = tokens_dot(text_states, value_cross_full)
    attn_cross, total_cross = attend(queries_cross, keys_text, values_text, text_valid, heads_here)
    after_cross = after_self + tensor_sum(tokens_dot(attn_cross, out_cross_full))
    normed_ff, centred_ff, inv_ff = layer_norm(after_cross, gain_ff_full)
    hidden_ff = jnp.einsum(E6, normed_ff, ff_in_full, precision=highest)
    value_half = hidden_ff[:, :, 0]
    gate_act, gelu_pull = jax.vjp(exact_gelu, hidden_ff[:, :, 1])
    ff_act = value_half * gate_act
    after_ff = after_cross + tensor_sum(tokens_dot(ff_act, ff_out_full))
    output = (residual_local + tokens_dot(after_ff, proj_out_full)) * valid_col
    (
        proj_in_back,
        gain_self_back,
        query_self_back,
        key_self_back,
        value_self_back,
        out_self_back,
        gain_cross_back,
        query_cross_back,
        key_cross_back,
        value_cross_back,
        out_cross_back,
        gain_ff_back,
        ff_in_back,
        ff_out_back,
        proj_out_back,
    ) = block_full
    grad_local = cotangent * valid_col
    grad_proj_out = tokens_grad(after_ff, grad_local)
    grad_after_ff = tensor_sum(tokens_back(grad_local, proj_out_back))
    grad_ff_out = tokens_grad(ff_act, grad_after_ff)
    grad_ff_act = tokens_back(grad_after_ff, ff_out_back)
    grad_value_half = grad_ff_act * gate_act
    grad_gate_half = gelu_pull(grad_ff_act * value_half)[0]
    grad_hidden_ff = jnp.stack([grad_value_half, grad_gate_half], axis=2)
    grad_ff_in = jnp.einsum(E5, normed_ff, grad_hidden_ff, precision=highest)
    grad_normed_ff = tensor_sum(
        jnp.einsum(E7, grad_hidden_ff, ff_in_back, precision=highest)
    )
    back_ff, grad_gain_ff = layer_back(grad_normed_ff, centred_ff, inv_ff, gain_ff_back)
    grad_after_cross = grad_after_ff + back_ff
    grad_out_cross = tokens_grad(attn_cross, grad_after_cross)
    grad_attn_cross = tokens_back(grad_after_cross, out_cross_back)
    grad_queries_cross, grad_keys_text, grad_values_text = attend_back(
        queries_cross,
        keys_text,
        values_text,
        text_valid,
        heads_here,
        attn_cross,
        total_cross,
        grad_attn_cross,
    )
    grad_query_cross = tokens_grad(normed_cross, grad_queries_cross)
    grad_key_cross = tokens_grad(text_states, grad_keys_text)
    grad_value_cross = tokens_grad(text_states, grad_values_text)
    grad_normed_cross = tensor_sum(tokens_back(grad_queries_cross, query_cross_back))
    back_cross, grad_gain_cross = layer_back(
        grad_normed_cross, centred_cross, inv_cross, gain_cross_back
    )
    grad_after_self = grad_after_cross + back_cross
    grad_out_self = tokens_grad(attn_self, grad_after_self)
    grad_attn_self = tokens_back(grad_after_self, out_self_back)
    grad_queries, grad_keys_all, grad_values_all = attend_back(
        queries, keys_all, values_all, key_valid, heads_here, attn_self, total_self, grad_attn_self
    )
    grad_keys_here, grad_values_here = (
        lax.psum_scatter(grad_keys_all, H, scatter_dimension=1, tiled=True),
        lax.psum_scatter(grad_values_all, H, scatter_dimension=1, tiled=True),
    )
    grad_query_self = tokens_grad(normed_self, grad_queries)
    grad_key_self = tokens_grad(normed_self, grad_keys_here)
    grad_value_self = tokens_grad(normed_self, grad_values_here)
    grad_normed_self = tensor_sum(
        tokens_back(grad_queries, query_self_back)
        + tokens_back(grad_keys_here, key_self_back)
        + tokens_back(grad_values_here, value_self_back)
    )
    back_self, grad_gain_self = layer_back(grad_normed_self, centred_self, inv_self, gain_self_back)
    grad_projected = grad_after_self + back_self
    grad_proj_in = tokens_grad(norm_three, grad_projected)
    grad_norm_three = tokens_back(grad_projected, proj_in_back)
    back_three, grad_gain_attn = group_back(
        grad_norm_three,
        centred_three,
        inv_three,
        gain_attn_norm,
        valid_col,
        local_groups,
        full_counts,
    )
    grad_residual_local = grad_local + back_three
    block_grads = (
        lax.psum_scatter(grad_proj_in, IH, scatter_dimension=1, tiled=True),
        lax.psum_scatter(
            jnp.tile(grad_gain_attn, width_ih), IH, scatter_dimension=0, tiled=True
        ),
        lax.psum_scatter(grad_gain_self, IH, scatter_dimension=0, tiled=True),
        lax.psum_scatter(grad_query_self, IH, scatter_dimension=0, tiled=True),
        lax.psum_scatter(grad_key_self, IH, scatter_dimension=0, tiled=True),
        lax.psum_scatter(grad_value_self, IH, scatter_dimension=0, tiled=True),
        lax.psum_scatter(grad_out_self, IH, scatter_dimension=1, tiled=True),
        lax.psum_scatter(grad_gain_cross, IH, scatter_dimension=0, tiled=True),
        lax.psum_scatter(grad_query_cross, IH, scatter_dimension=0, tiled=True),
        lax.psum_scatter(grad_key_cross, IH, scatter_dimension=0, tiled=True),
        lax.psum_scatter(grad_value_cross, IH, scatter_dimension=0, tiled=True),
        lax.psum_scatter(grad_out_cross, IH, scatter_dimension=1, tiled=True),
        lax.psum_scatter(grad_gain_ff, IH, scatter_dimension=0, tiled=True),
        lax.psum_scatter(grad_ff_in, IH, scatter_dimension=0, tiled=True),
        lax.psum_scatter(grad_ff_out, IH, scatter_dimension=1, tiled=True),
        lax.psum_scatter(grad_proj_out, IH, scatter_dimension=0, tiled=True),
    )
    gain_in_back, conv_first_back, time_back, conv_second_back = resnet_full
    grad_residual = lax.all_gather(grad_residual_local, T, axis=2, tiled=True)
    grad_conv_second = conv_weight_grad(stack_two, grad_residual, conv_second_back.shape)
    stack_grad_two = neighbour_stack(grad_residual, strip_rows, strip_width)
    grad_act_two = conv_input_grad(stack_grad_two, conv_second_back)
    grad_norm_two = silu_pull_two(grad_act_two)[0]
    grad_conv_one, grad_gain_mid = group_back(
        grad_norm_two, centred_two, inv_two, gain_mid, valid_col, local_groups, full_counts
    )
    grad_time_term = jnp.sum(grad_conv_one, axis=1)
    grad_time_weight = jnp.einsum(E0, silu_features, grad_time_term, precision=highest)
    grad_conv_first = conv_weight_grad(stack_one, grad_conv_one, conv_first_back.shape)
    stack_grad_one = neighbour_stack(grad_conv_one, strip_rows, strip_width)
    grad_act_one = tensor_sum(conv_input_grad(stack_grad_one, conv_first_back))
    grad_norm_one = silu_pull_one(grad_act_one)[0]
    back_one, grad_gain_in = group_back(
        grad_norm_one, centred_one, inv_one, gain_in_back, valid_col, GROUPS, full_counts
    )
    grad_hidden = (grad_residual + back_one) * valid_col
    resnet_grads = (
        lax.psum_scatter(grad_gain_in, IH, scatter_dimension=0, tiled=True),
        lax.psum_scatter(grad_conv_first, IH, scatter_dimension=2, tiled=True),
        lax.psum_scatter(grad_time_weight, IH, scatter_dimension=0, tiled=True),
        lax.psum_scatter(
            jnp.tile(grad_gain_mid, width_ih), IH, scatter_dimension=0, tiled=True
        ),
        lax.psum_scatter(grad_conv_second, IH, scatter_dimension=3, tiled=True),
    )
    return (
        output,
        grad_hidden,
        resnet_grads[0],
        resnet_grads[1],
        resnet_grads[2],
        resnet_grads[3],
        resnet_grads[4],
        block_grads[1],
        block_grads[0],
        block_grads[2],
        block_grads[3],
        block_grads[4],
        block_grads[5],
        block_grads[6],
        block_grads[7],
        block_grads[8],
        block_grads[9],
        block_grads[10],
        block_grads[11],
        block_grads[12],
        block_grads[13],
        block_grads[14],
        block_grads[15],
    )


def mm(left, right, left_dim, right_dim):
    return lax.dot_general(
        left,
        right,
        (((left_dim,), (right_dim,)), ((), ())),
        precision=high,
        preferred_element_type=jnp.float32,
    )


def swap(values):
    return lax.ppermute(values, I, [(0, 1), (1, 0)])


def flip(values, step):
    return lax.ppermute(values, H, [(s, s ^ step) for s in range(4)])


def turn(values, step):
    return lax.ppermute(values, T, [(s, (s + step) % 4) for s in range(4)])


def z_pieces(values):
    return [values] + [turn(values, 4 - j) for j in (1, 2, 3)]


def z_collect(pieces):
    total = pieces[0]
    for j in (1, 2, 3):
        total = total + turn(pieces[j], j)
    return total


def z_exchange(pieces):
    return [pieces[0]] + [turn(pieces[4 - j], 4 - j) for j in (1, 2, 3)]


def z_order(pieces, axis):
    t = lax.axis_index(T)
    shape = list(pieces[0].shape)
    shape.insert(axis, 4)
    whole = jnp.zeros(shape, pieces[0].dtype)
    for j in range(4):
        whole = lax.dynamic_update_index_in_dim(whole, pieces[j], lax.rem(t + j, 4), axis)
    return whole


def z_sum(values):
    return jnp.sum(z_order(z_pieces(values), 0), axis=0)


def h_collect(pieces):
    total = pieces[0]
    for j in (1, 2, 3):
        total = total + flip(pieces[j], j)
    return total


def h_sum(values):
    h = lax.axis_index(H)
    pieces = [values] + [flip(values, j) for j in (1, 2, 3)]
    whole = jnp.zeros((4,) + values.shape, values.dtype)
    for j in range(4):
        whole = lax.dynamic_update_index_in_dim(whole, pieces[j], h ^ j, 0)
    return jnp.sum(whole, axis=0)


def pick(values, index, axis=0):
    return lax.dynamic_index_in_dim(values, index, axis, keepdims=False)


def plane_sum(own, other):
    own = own + swap(other)
    part = h_collect([own[j] for j in range(4)])
    pieces = [part] + [flip(part, j) for j in (1, 2, 3)]
    return pieces + [swap(piece) for piece in pieces]


def q_to_s(values):
    moved = lax.all_to_all(values.reshape((8,) + values.shape[2:]), IH, 0, 0)
    return jnp.moveaxis(moved, 0, 1).reshape(values.shape[2], -1)


def s_to_q(values):
    cut = jnp.moveaxis(values.reshape(values.shape[0], 8, -1), 1, 0)
    moved = lax.all_to_all(cut, IH, 0, 0)
    return moved.reshape((2, 4) + moved.shape[1:])


def group_sum(channel_sums):
    shape = channel_sums.shape
    groups = jnp.sum(channel_sums.reshape(shape[:-1] + (shape[-1] // 40, 40)), axis=-1)
    return jnp.repeat(groups, 40, axis=-1)


IMAGE_ROWS = 1152
TAP_ROWS = range(16, 1136, 160)


def halves(values):
    top = values.astype(jnp.bfloat16)
    return top, (values - top.astype(jnp.float32)).astype(jnp.bfloat16)


def dot_halves(left, right, left_dim, right_dim):
    def one(a, b):
        return lax.dot_general(
            a, b, (((left_dim,), (right_dim,)), ((), ())), preferred_element_type=jnp.float32
        )

    return one(left[0], right[0]) + (one(left[0], right[1]) + one(left[1], right[0]))


def marks_of(marks, b):
    return marks[2 * b], marks[2 * b + 1]


def row_mask(span, rows, columns):
    return (lax.broadcasted_iota(jnp.int32, (rows, columns), 0) < span).astype(jnp.float32)


def put_strip(image, b, strip, span, values):
    at = pl.multiple_of(margin + strip * span, 8)
    image[b, pl.ds(at, 240)] = values[:240]

    @pl.when(span == 256)
    def _():
        image[b, pl.ds(pl.multiple_of(at + 240, 8), 16)] = values[240:]


def widen(wide, image, b, width, sign):
    channels = image.shape[2]
    width_f = width.astype(jnp.float32)
    for base in TAP_ROWS:
        row = lax.broadcasted_iota(jnp.int32, (160, channels), 0).astype(jnp.float32)
        cell = row + float(base - margin)
        column = cell - width_f * jnp.floor((cell + 0.5) / width_f)
        for j in range(3):
            step = sign * (j - 1)
            values = image[b, base + step : base + step + 160, :]
            if step < 0:
                values = jnp.where(column > 0.5, values, 0.0)
            if step > 0:
                values = jnp.where(column < width_f - 1.5, values, 0.0)
            wide[base : base + 160, j * channels : (j + 1) * channels] = values


def split_weight(weight, top, low):
    for k in range(3):
        rows = weight.shape[0] // 3
        first, second = halves(weight[k * rows : (k + 1) * rows, :])
        top[k * rows : (k + 1) * rows, :] = first
        low[k * rows : (k + 1) * rows, :] = second


def conv_strip(wide, top, low, strip, span, width, sign):
    rows = top.shape[0] // 3
    total = None
    for i in range(3):
        at = pl.multiple_of(margin + strip * span + sign * (i - 1) * width, 8)
        taps = halves(wide[pl.ds(at, 256), :])
        part = dot_halves(
            taps, (top[i * rows : (i + 1) * rows, :], low[i * rows : (i + 1) * rows, :]), 1, 0
        )
        total = part if total is None else total + part
    return total * row_mask(span, 256, total.shape[1])


def group_rows(sums):
    channels = sums.shape[1]
    lane = lax.broadcasted_iota(jnp.int32, (1, channels), 1)
    result = jnp.zeros((1, channels), jnp.float32)
    for g in range(channels // 40):
        inside = (lane >= 40 * g) & (lane < 40 * g + 40)
        result = jnp.where(inside, jnp.sum(jnp.where(inside, sums, 0.0)), result)
    return result


def group_row_stats(total, squares, span):
    count = (span * 160).astype(jnp.float32)
    mean = group_rows(total) / count
    var = group_rows(squares) / count - mean * mean
    return mean, lax.rsqrt(var + norm_eps)


def column_sum(values):
    return jnp.sum(values, axis=0, keepdims=True)


def first_kernel(marks, source, gain, tau, weight, own, other, image, stats, wide, top, low):
    item, h = marks[4], marks[5]
    split_weight(weight, top, low)
    image[...] = jnp.zeros_like(image)
    for b, out in ((0, own), (1, other)):
        span, width = marks_of(marks, b)
        base = (item ^ b) * 4
        total = jnp.zeros((1, 160), jnp.float32)
        squares = jnp.zeros((1, 160), jnp.float32)
        for k in range(4):
            values = source[base + k]
            total = total + column_sum(values)
            squares = squares + column_sum(values * values)
        mean, inv = group_row_stats(total, squares, span)
        stats[b, 0:1, :] = mean
        stats[b, 1:2, :] = inv
        for k in range(4):
            norm = (source[base + k] - mean) * inv * row_mask(span, 256, 160) * gain[...]
            put_strip(image, b, k, span, norm * jax.nn.sigmoid(norm))
        widen(wide, image, b, width, 1)
        added = tau[b : b + 1, :]

        def step(k, _):
            conv = conv_strip(wide, top, low, k, span, width, 1)
            out[k ^ h] = conv + added * row_mask(span, 256, 320)
            return 0

        lax.fori_loop(0, 4, step, 0)


def put_quarters(outs, tile, place, t):
    for j in range(4):
        at = pl.multiple_of(lax.rem(t + j, 4) * 64, 8)
        outs[j][place] = tile[pl.ds(at, 64), :]


def second_kernel(marks, *refs):
    strips, gain, weight = refs[:8], refs[8], refs[9]
    outs, image, stats = refs[10:14], refs[14], refs[15]
    wide, top, low, tile = refs[16:]
    item, h, t = marks[4], marks[5], marks[6]
    split_weight(weight, top, low)
    image[...] = jnp.zeros_like(image)
    for b in range(2):
        span, width = marks_of(marks, b)
        total = jnp.zeros((1, 320), jnp.float32)
        squares = jnp.zeros((1, 320), jnp.float32)
        for j in range(4):
            values = strips[4 * b + j][...]
            total = total + column_sum(values)
            squares = squares + column_sum(values * values)
        mean, inv = group_row_stats(total, squares, span)
        stats[b, 0:1, :] = mean
        stats[b, 1:2, :] = inv
        for j in range(4):
            values = strips[4 * b + j][...]
            norm = (values - mean) * inv * row_mask(span, 256, 320) * gain[...]
            put_strip(image, b, h ^ j, span, norm * jax.nn.sigmoid(norm))
        widen(wide, image, b, width, 1)

        def step(k, _):
            tile[...] = conv_strip(wide, top, low, k, span, width, 1)
            put_quarters(outs, tile, (item ^ b) * 4 + k, t)
            return 0

        lax.fori_loop(0, 4, step, 0)


def second_back_kernel(marks, *refs):
    quarters, weight = refs[:4], refs[4]
    own, other, image = refs[5:8]
    wide, top, low = refs[8:]
    item, h, t = marks[4], marks[5], marks[6]
    split_weight(weight, top, low)
    image[...] = jnp.zeros_like(image)
    for b, out in ((0, own), (1, other)):
        span, width = marks_of(marks, b)

        def fill(k, _):
            for j in range(4):
                q = lax.rem(t + j, 4)
                values = quarters[j][(item ^ b) * 4 + k]
                at = pl.multiple_of(margin + k * span + q * 64, 8)
                image[b, pl.ds(at, 48)] = values[:48]

                @pl.when((q < 3) | (span == 256))
                def _():
                    image[b, pl.ds(pl.multiple_of(at + 48, 8), 16)] = values[48:]

            return 0

        lax.fori_loop(0, 4, fill, 0)
        widen(wide, image, b, width, -1)

        def step(k, _):
            out[k ^ h] = conv_strip(wide, top, low, k, span, width, -1)
            return 0

        lax.fori_loop(0, 4, step, 0)


def first_back_kernel(marks, *refs):
    grads, strips, gain, stats, weight = refs[:8], refs[8:16], refs[16], refs[17], refs[18]
    outs, image, sums, grad_gain = refs[19:23], refs[23], refs[24], refs[25]
    wide, top, low, tile, scaled_at, centred_at = refs[26:]
    item, h, t = marks[4], marks[5], marks[6]
    split_weight(weight, top, low)
    image[...] = jnp.zeros_like(image)
    gain_total = jnp.zeros((1, 320), jnp.float32)
    for b in range(2):
        span, width = marks_of(marks, b)
        mean, inv = stats[b, 0:1, :], stats[b, 1:2, :]
        first = jnp.zeros((1, 320), jnp.float32)
        second = jnp.zeros((1, 320), jnp.float32)
        for j in range(4):
            centred = (strips[4 * b + j][...] - mean) * inv * row_mask(span, 256, 320)
            norm = centred * gain[...]
            gate = jax.nn.sigmoid(norm)
            grad_norm = grads[4 * b + j][...] * gate * (1.0 + norm * (1.0 - gate))
            scaled = grad_norm * gain[...]
            first = first + column_sum(scaled)
            second = second + column_sum(scaled * centred)
            gain_total = gain_total + column_sum(grad_norm * centred)
            scaled_at[j] = scaled
            centred_at[j] = centred
        count = (span * 160).astype(jnp.float32)
        first = group_rows(first) / count
        second = group_rows(second) / count
        tau_total = jnp.zeros((1, 320), jnp.float32)
        for j in range(4):
            grad = inv * row_mask(span, 256, 320) * (
                scaled_at[j] - first - centred_at[j] * second
            )
            tau_total = tau_total + column_sum(grad)
            put_strip(image, b, h ^ j, span, grad)
        sums[b : b + 1, :] = tau_total
        widen(wide, image, b, width, -1)

        def step(k, _):
            tile[...] = conv_strip(wide, top, low, k, span, width, -1)
            put_quarters(outs, tile, (item ^ b) * 4 + k, t)
            return 0

        lax.fori_loop(0, 4, step, 0)
    grad_gain[...] = gain_total


def first_weight_kernel(marks, image, grad, out, wide):
    out[...] = jnp.zeros_like(out)
    for b in range(2):
        _, width = marks_of(marks, b)
        widen(wide, image, b, width, 1)
        for i in range(3):

            def step(c, _):
                at = pl.multiple_of(margin + c * 256 + (i - 1) * width, 8)
                taps = halves(wide[pl.ds(at, 256), :].T)
                cells = halves(grad[b, pl.ds(pl.multiple_of(margin + c * 256, 8), 256), :])
                part = dot_halves(taps, cells, 1, 0)
                for j in range(3):
                    out[3 * i + j] += part[160 * j : 160 * j + 160]
                return 0

            lax.fori_loop(0, 4, step, 0)


def second_weight_kernel(marks, image, grad, out, wide, total):
    for i in range(3):
        total[...] = jnp.zeros_like(total)
        for b in range(2):
            _, width = marks_of(marks, b)
            widen(wide, grad, b, width, -1)

            def step(c, _):
                at = pl.multiple_of(margin + c * 256 - (i - 1) * width, 8)
                cells = halves(image[b, pl.ds(pl.multiple_of(margin + c * 256, 8), 256), :].T)
                total[...] += dot_halves(cells, halves(wide[pl.ds(at, 256), :]), 1, 0)
                return 0

            lax.fori_loop(0, 4, step, 0)
        for j in range(3):
            out[3 * i + j] = total[:, 160 * j : 160 * j + 160]


def run_kernel(body, marks, inputs, outs, scratch, flops):
    in_smem = pl.BlockSpec(memory_space=pltpu.SMEM)
    in_vmem = pl.BlockSpec(memory_space=pltpu.VMEM)
    return pl.pallas_call(
        body,
        out_shape=[jax.ShapeDtypeStruct(shape, jnp.float32) for shape in outs],
        in_specs=[in_smem] + [in_vmem] * len(inputs),
        out_specs=[in_vmem] * len(outs),
        scratch_shapes=[pltpu.VMEM(shape, kind) for shape, kind in scratch],
        compiler_params=pltpu.CompilerParams(vmem_limit_bytes=56 * 1024 * 1024),
        cost_estimate=pl.CostEstimate(
            flops=flops, bytes_accessed=10 * 1024 * 1024, transcendentals=0
        ),
    )(marks, *inputs)


def weight_kernel(plan, *refs):
    count = 1 + max(which for block in plan for _, _, which in block)
    lefts, right, out = refs[:count], refs[count], refs[count + 1]
    tokens = right.shape[0]
    for number, block in enumerate(plan):

        @pl.when(pl.program_id(0) == number)
        def _():
            for begin, columns, which in block:
                top, low = halves(right[:, begin : begin + columns])
                if tokens <= 64:
                    stacked = jnp.concatenate([top, low, top], axis=0)
                for m in range(0, 1280, 256):
                    cells = lefts[which][:, m : m + 256].T
                    if tokens <= 64:
                        first, second = halves(cells)
                        first = jnp.concatenate([first, first, second], axis=1)
                        part = jnp.dot(first, stacked, preferred_element_type=jnp.float32)
                    else:
                        part = dot_halves(halves(cells), (top, low), 1, 0)
                    out[m : m + 256, begin : begin + columns] = part


def weight_grads(plan, lefts, right):
    tokens = right.shape[0]
    blocks = len(plan)
    return pl.pallas_call(
        functools.partial(weight_kernel, plan),
        out_shape=jax.ShapeDtypeStruct((1280, 1280 * blocks), jnp.float32),
        grid=(blocks,),
        in_specs=[pl.BlockSpec((tokens, 1280), lambda i: (0, 0))] * len(lefts)
        + [pl.BlockSpec((tokens, 1280), lambda i: (0, i))],
        out_specs=pl.BlockSpec((1280, 1280), lambda i: (0, i)),
        compiler_params=pltpu.CompilerParams(vmem_limit_bytes=48 * 1024 * 1024),
        cost_estimate=pl.CostEstimate(
            flops=6 * tokens * 1280 * 1280 * blocks,
            bytes_accessed=7 * 1024 * 1024 * blocks,
            transcendentals=0,
        ),
    )(*lefts, right)


def after(values, *events):
    return lax.optimization_barrier((values,) + events)[0]


def together(*values):
    return lax.optimization_barrier(values)


CONV_FLOPS = 6 * 2048 * 1440 * 320


def first_conv(marks, source, gain, tau, weight):
    f32, b16 = jnp.float32, jnp.bfloat16
    return run_kernel(
        first_kernel,
        marks,
        (source, gain, tau, weight),
        [(4, 256, 320), (4, 256, 320), (2, IMAGE_ROWS, 160), (2, 8, 160)],
        [((IMAGE_ROWS, 480), f32), ((1440, 320), b16), ((1440, 320), b16)],
        CONV_FLOPS,
    )


def second_conv(marks, strips, gain, weight):
    f32, b16 = jnp.float32, jnp.bfloat16
    return run_kernel(
        second_kernel,
        marks,
        (*strips, gain, weight),
        [(8, 64, 160)] * 4 + [(2, IMAGE_ROWS, 320), (2, 8, 320)],
        [
            ((IMAGE_ROWS, 960), f32),
            ((2880, 160), b16),
            ((2880, 160), b16),
            ((256, 160), f32),
        ],
        CONV_FLOPS,
    )


def second_conv_back(marks, quarters, weight):
    f32, b16 = jnp.float32, jnp.bfloat16
    return run_kernel(
        second_back_kernel,
        marks,
        (*quarters, weight),
        [(4, 256, 320), (4, 256, 320), (2, IMAGE_ROWS, 160)],
        [((IMAGE_ROWS, 480), f32), ((1440, 320), b16), ((1440, 320), b16)],
        CONV_FLOPS,
    )


def first_conv_back(marks, grads, strips, gain, stats, weight):
    f32, b16 = jnp.float32, jnp.bfloat16
    return run_kernel(
        first_back_kernel,
        marks,
        (*grads, *strips, gain, stats, weight),
        [(8, 64, 160)] * 4 + [(2, IMAGE_ROWS, 320), (2, 320), (1, 320)],
        [
            ((IMAGE_ROWS, 960), f32),
            ((2880, 160), b16),
            ((2880, 160), b16),
            ((256, 160), f32),
            ((4, 256, 320), f32),
            ((4, 256, 320), f32),
        ],
        CONV_FLOPS,
    )


def first_conv_weight(marks, image, grad):
    return run_kernel(
        first_weight_kernel,
        marks,
        (image, grad),
        [(9, 160, 320)],
        [((IMAGE_ROWS, 480), jnp.float32)],
        CONV_FLOPS,
    )[0]


def second_conv_weight(marks, image, grad):
    return run_kernel(
        second_weight_kernel,
        marks,
        (image, grad),
        [(9, 320, 160)],
        [((IMAGE_ROWS, 480), jnp.float32), ((320, 480), jnp.float32)],
        CONV_FLOPS,
    )[0]


def heads_of(values, count):
    return values.reshape(values.shape[0], count, HEAD_DIM)


def ein(form, left, right):
    return jnp.einsum(form, left, right, precision=high, preferred_element_type=jnp.float32)


def soft_attend(queries, keys, values, key_valid, count):
    scores = ein(QK, heads_of(queries, count), heads_of(keys, count)) * (1.0 / math.sqrt(HEAD_DIM))
    if key_valid is not None:
        scores = jnp.where(key_valid[None, None, :], scores, masked_score)
    exponent = jnp.exp(scores - jnp.max(scores, axis=-1, keepdims=True))
    weights = exponent / jnp.sum(exponent, axis=-1, keepdims=True)
    attended = ein(PV, weights, heads_of(values, count))
    return attended.reshape(queries.shape), weights


def soft_back(queries, keys, values, count, weights, attended, grad_out):
    scaling = 1.0 / math.sqrt(HEAD_DIM)
    grad_heads = heads_of(grad_out, count)
    grad_soft = ein(QK, grad_heads, heads_of(values, count))
    delta = jnp.sum(grad_heads * heads_of(attended, count), axis=-1).T
    grad_scores = weights * (grad_soft - delta[..., None])
    grad_query = ein(PV, grad_scores, heads_of(keys, count)) * scaling
    grad_key = ein(PQ, grad_scores, heads_of(queries, count)) * scaling
    grad_value = ein(PQ, weights, grad_heads)
    return (
        grad_query.reshape(queries.shape),
        grad_key.reshape(keys.shape),
        grad_value.reshape(values.shape),
    )


def layer_grad(grad_out, centred, inv_std, gain_vector):
    scaled = grad_out * gain_vector
    grad_in = inv_std * (
        scaled
        - jnp.mean(scaled, axis=-1, keepdims=True)
        - centred * jnp.mean(scaled * centred, axis=-1, keepdims=True)
    )
    return grad_in, jnp.sum(grad_out * centred, axis=0)


def layer_forward(values, gain_vector):
    mean_val = jnp.mean(values, axis=-1, keepdims=True)
    var_val = jnp.mean(values * values, axis=-1, keepdims=True) - mean_val * mean_val
    inv_std = lax.rsqrt(var_val + norm_eps)
    centred = (values - mean_val) * inv_std
    return centred * gain_vector, centred, inv_std


def gather_plane(block):
    return lax.all_gather(block, IH, axis=0, tiled=True)


def scatter_plane(block):
    return lax.psum_scatter(block, IH, scatter_dimension=0, tiled=True)


def strip_sums(values):
    return jnp.sum(values, axis=(1, 2))


def grid_cells(bucket):
    strip_rows, strip_width = grid_shape(bucket)
    return strip_rows * strip_width


def fast_shards(
    hidden,
    text_states,
    bucket,
    timestep,
    gain_in,
    conv_first,
    time_weight,
    gain_mid,
    conv_second,
    gain_attn_norm,
    proj_in,
    gain_self,
    query_self,
    key_self,
    value_self,
    out_self,
    gain_cross,
    query_cross,
    key_cross,
    value_cross,
    out_cross,
    gain_ff,
    ff_in,
    ff_out,
    proj_out,
    cotangent,
):
    item, h, t = lax.axis_index(I), lax.axis_index(H), lax.axis_index(T)
    block = item * 4 + h
    width, wide = 160, 320
    channels = 1280

    def rows_of(values):
        return [values[64 * j : 64 * j + 64] for j in range(4)]

    own_span = grid_cells(bucket[0])
    slot = jnp.arange(256, dtype=jnp.int32)
    own_valid = (slot < own_span).astype(jnp.float32)[:, None]
    source = s_to_q(hidden[0] * own_valid).reshape(8, 256, width)
    both = jnp.stack([bucket[0], timestep[0]]).astype(jnp.float32)
    both_other = swap(both)
    pair = jnp.where(item == 0, jnp.stack([both, both_other]), jnp.stack([both_other, both]))
    times = jnp.stack([both[1], both_other[1]])
    strip_rows, strip_width = grid_shape(pair[:, 0].astype(jnp.int32))
    spans = strip_rows * strip_width
    marks = jnp.stack(
        [
            own_span,
            pick(strip_width, item),
            pick(spans, 1 - item),
            pick(strip_width, 1 - item),
            item,
            h,
            t,
        ]
    ).astype(jnp.int32)
    counts = (4 * spans * 40).astype(jnp.float32)[:, None]
    quarter_slot = t * 64 + jnp.arange(64, dtype=jnp.int32)
    q_valid = (quarter_slot[None, :] < spans[:, None]).astype(jnp.float32)[:, None, :, None]
    relative_slot = jnp.mod(t * 64 + slot, 256)
    key_valid = jnp.tile(relative_slot < own_span, 4)

    def spread(stat):
        return stat[:, None, None, :]

    def quarter(values):
        return lax.dynamic_slice_in_dim(values, t * 64, 64, 2)

    gains = jnp.stack([gain_self, gain_cross, gain_ff], axis=1)
    attn_full = gather_plane(
        jnp.concatenate(
            [
                query_self,
                key_self,
                value_self,
                proj_out,
                out_self.T,
                jnp.pad(gains, ((0, 0), (0, 125))),
            ],
            axis=1,
        )
    )
    qkv_full = attn_full[:, :960]
    proj_out_full = attn_full[:, 960:1280]
    out_self_full = attn_full[:, 1280:1600]
    gain_rows = attn_full[:, 1600:1603].T
    gain_self_full, gain_cross_full, gain_ff_full = (gain_rows[k : k + 1] for k in range(3))

    own_third = jnp.concatenate([proj_in.T, query_cross, out_cross.T], axis=1)
    own_third = jnp.concatenate(
        [own_third, jnp.pad(gain_attn_norm[None, :], ((0, 7), (0, 640)))], axis=0
    )
    third_pieces = z_pieces(own_third)

    features = jax.nn.silu(time_features(times, channels))
    own_features = lax.dynamic_slice_in_dim(features, block * width, width, 1)
    tau = mm(own_features, time_weight, 1, 0)
    own_one, other_one, image_one, stats_one = first_conv(
        marks, source, gain_in[None, :], tau, conv_first.reshape(9 * width, wide)
    )
    strips_one = plane_sum(own_one, other_one)

    third = z_order(after(third_pieces, own_one), 1)
    gain_attn_full = third[160, :, :320].reshape(1, channels)
    third = third[:160].reshape(160, 4, 3, 320).transpose(0, 2, 1, 3).reshape(160, 3840)
    third_full = gather_plane(third)
    proj_in_full = third_full[:, :1280]
    query_cross_full = third_full[:, 1280:2560]
    out_cross_full = third_full[:, 2560:]

    ff_full = gather_plane(jnp.concatenate([ff_in.reshape(160, 2560), ff_out.T], axis=1))
    ff_in_full = ff_full[:, :2560]
    ff_out_full = ff_full[:, 2560:]

    cot = after(cotangent[0] * own_valid, own_one)
    cot_relative = lax.dynamic_slice_in_dim(jnp.concatenate([cot, cot], axis=0), t * 64, 256, 0)
    cot_pieces = z_exchange(rows_of(cot_relative))
    grad_ff_part = mm(cot_relative, proj_out_full, 1, 1)
    grad_after_ff = z_collect(rows_of(grad_ff_part))

    *strips_one, grad_after_ff = together(*strips_one, grad_after_ff)
    *conv_two, image_two, stats_two = second_conv(
        marks, strips_one, gain_mid[None, :], conv_second.reshape(9 * wide, width)
    )
    conv_two_sum = z_collect(conv_two)

    text_here = after(text_states[0], conv_two[0])
    text_own = lax.dynamic_slice_in_dim(text_here, block * 256, 256, 1)
    text_other = swap(lax.dynamic_slice_in_dim(text_here, ((1 - item) * 4 + h) * 256, 256, 1))
    text_weight = jnp.concatenate([key_cross, value_cross], axis=1)
    text_part = mm(text_own, text_weight, 1, 0) + swap(mm(text_other, text_weight, 1, 0))
    text_sum = h_sum(text_part)
    cot_s = z_order(after(cot_pieces, conv_two[0]), 1)
    cot_q = s_to_q(cot_s.reshape(64, channels))
    residual_q = quarter(source.reshape(2, 4, 256, width)) + conv_two_sum.reshape(2, 4, 64, width)

    sums = z_sum(jnp.stack([strip_sums(residual_q), strip_sums(residual_q * residual_q)]))
    mean_three = group_sum(sums[0]) / counts
    var_three = group_sum(sums[1]) / counts - mean_three * mean_three
    inv_three = lax.rsqrt(var_three + norm_eps)
    centred_three = (residual_q - spread(mean_three)) * spread(inv_three) * q_valid
    norm_three = q_to_s(centred_three) * gain_attn_full
    projected = mm(norm_three, proj_in_full, 1, 1)

    normed_self, centred_self, inv_self = layer_forward(projected, gain_self_full)
    normed_self_all = jnp.concatenate(z_pieces(normed_self), axis=0)
    qkv = mm(normed_self_all, qkv_full, 1, 0)
    queries = qkv[:, :wide]
    kv_pieces = [qkv[:, wide:]] + [flip(qkv[:, wide:], j) for j in (1, 2, 3)]
    text_kv = z_order(z_pieces(after(text_sum, qkv)), 1)
    keys_text = text_kv[:, :, :320].reshape(-1, channels)
    values_text = text_kv[:, :, 320:].reshape(-1, channels)
    grad_after_ff_all = jnp.concatenate(z_pieces(after(grad_after_ff, qkv)), axis=0)

    kv_all = jnp.concatenate(kv_pieces, axis=0)
    keys_all, values_all = kv_all[:, :wide], kv_all[:, wide:]
    attn_self, weights_self = soft_attend(queries, keys_all, values_all, key_valid, 5)
    self_part = mm(attn_self, out_self_full, 1, 1)
    self_sum = z_collect(rows_of(self_part))
    grad_ff_act = mm(after(grad_after_ff_all, self_part), ff_out_full, 1, 0)
    residual_s = q_to_s(after(residual_q, self_part))
    self_sum, grad_ff_act = together(self_sum, grad_ff_act)
    after_self = projected + self_sum

    normed_cross, centred_cross, inv_cross = layer_forward(after_self, gain_cross_full)
    queries_cross = mm(normed_cross, query_cross_full, 1, 0)
    attn_cross, weights_cross = soft_attend(queries_cross, keys_text, values_text, None, 20)
    after_cross = after_self + mm(attn_cross, out_cross_full, 1, 1)

    normed_ff, centred_ff, inv_ff = layer_forward(after_cross, gain_ff_full)
    normed_ff_all = jnp.concatenate(z_pieces(normed_ff), axis=0)
    hidden_ff = mm(normed_ff_all, ff_in_full, 1, 0)
    value_half, gate_half = hidden_ff[:, :channels], hidden_ff[:, channels:]
    phi = 0.5 * (1.0 + lax.erf(gate_half * math.sqrt(0.5)))
    slope = phi + gate_half * jnp.exp(-0.5 * gate_half * gate_half) * (1.0 / math.sqrt(2 * math.pi))
    gate_act = gate_half * phi
    ff_act = value_half * gate_act
    grad_value = grad_ff_act * gate_act
    grad_gate = grad_ff_act * value_half * slope
    grad_hidden_ff = jnp.concatenate([grad_value, grad_gate], axis=1)
    grad_normed_part = mm(grad_hidden_ff, ff_in_full, 1, 1)
    grad_normed_ff = z_collect(rows_of(grad_normed_part))
    ff_right = after(jnp.concatenate([grad_hidden_ff, ff_act], axis=1), grad_normed_part)
    ff_grads = weight_grads(
        (((0, 1280, 0),), ((0, 1280, 0),), ((0, 1280, 1),)),
        (normed_ff_all, grad_after_ff_all),
        ff_right,
    )
    grad_normed_ff, ff_grads = together(grad_normed_ff, ff_grads)
    ff_grads = scatter_plane(ff_grads)

    back_ff, grad_gain_ff = layer_grad(grad_normed_ff, centred_ff, inv_ff, gain_ff_full)
    grad_after_cross = grad_after_ff + back_ff
    grad_attn_cross = mm(grad_after_cross, out_cross_full, 1, 0)
    grad_queries_cross, grad_keys_text, grad_values_text = soft_back(
        queries_cross, keys_text, values_text, 20, weights_cross, attn_cross, grad_attn_cross
    )
    grad_normed_cross = mm(grad_queries_cross, query_cross_full, 1, 1)
    back_cross, grad_gain_cross = layer_grad(
        grad_normed_cross, centred_cross, inv_cross, gain_cross_full
    )
    grad_after_self = grad_after_cross + back_cross
    grad_pieces = z_pieces(grad_after_self)
    cross_right = after(
        jnp.concatenate([grad_queries_cross, attn_cross], axis=1), grad_after_self
    )
    cross_grads = weight_grads(
        (((0, 1280, 0),), ((0, 1280, 1),)), (normed_cross, grad_after_cross), cross_right
    )
    *grad_pieces, cross_grads = together(*grad_pieces, cross_grads)
    cross_grads = scatter_plane(cross_grads)
    text_grads = jnp.concatenate(
        [grad_keys_text.reshape(-1, 4, wide), grad_values_text.reshape(-1, 4, wide)], axis=2
    )

    grad_after_self_all = jnp.concatenate(grad_pieces, axis=0)
    grad_attn_self = mm(grad_after_self_all, out_self_full, 1, 0)
    grad_queries, grad_keys_all, grad_values_all = soft_back(
        queries, keys_all, values_all, 5, weights_self, attn_self, grad_attn_self
    )
    grad_kv_all = jnp.concatenate([grad_keys_all, grad_values_all], axis=1)
    grad_kv = h_collect([grad_kv_all[256 * j : 256 * j + 256] for j in range(4)])
    text_grads = after(text_grads, grad_kv_all)
    text_grads = z_collect([pick(text_grads, lax.rem(t + j, 4), 1) for j in range(4)])
    out_part = mm(after(ff_act, grad_kv_all), ff_out_full, 1, 1)
    grad_kv, out_part = together(grad_kv, out_part)

    grad_qkv = jnp.concatenate([grad_queries, grad_kv], axis=1)
    grad_normed_part = mm(grad_qkv, qkv_full, 1, 1)
    grad_normed_self = z_collect(rows_of(grad_normed_part))
    text_grads = h_sum(after(text_grads, grad_normed_part))

    back_self, grad_gain_self = layer_grad(grad_normed_self, centred_self, inv_self, gain_self_full)
    grad_projected = grad_after_self + back_self
    grad_norm_three = mm(grad_projected, proj_in_full, 1, 0)

    both_grads = s_to_q(
        jnp.concatenate([grad_norm_three * gain_attn_full, grad_norm_three], axis=0)
    )
    attn_right = jnp.concatenate(
        [
            jnp.concatenate([grad_qkv, attn_self], axis=1),
            jnp.pad(norm_three, ((0, 192), (0, 0))),
        ],
        axis=1,
    )
    attn_grads = weight_grads(
        (((0, 960, 0), (960, 320, 1)), ((0, 1280, 2),)),
        (
            normed_self_all,
            grad_after_self_all,
            jnp.pad(grad_projected, ((0, 192), (0, 0))),
        ),
        after(attn_right, grad_norm_three),
    )
    both_grads, attn_grads = together(both_grads, attn_grads)
    attn_grads = scatter_plane(attn_grads)

    scaled_three, grad_three = both_grads[:, :, :64] * q_valid, both_grads[:, :, 64:]
    sums = z_sum(
        jnp.stack(
            [
                strip_sums(scaled_three),
                strip_sums(scaled_three * centred_three),
                strip_sums(grad_three * centred_three),
            ]
        )
    )
    grad_gain_three = jnp.sum(sums[2], axis=0)
    grad_residual_q = cot_q + spread(inv_three) * q_valid * (
        scaled_three
        - spread(group_sum(sums[0]) / counts)
        - centred_three * spread(group_sum(sums[1]) / counts)
    )

    own_two, other_two, image_back = second_conv_back(
        marks,
        z_pieces(grad_residual_q.reshape(8, 64, width)),
        conv_second.transpose(0, 1, 3, 2).reshape(9 * width, wide),
    )
    grad_act_two = plane_sum(own_two, other_two)
    grad_conv_second = second_conv_weight(marks, image_two, after(image_back, own_two)).reshape(
        3, 3, wide, width
    )
    after_ff = after_cross + z_collect(rows_of(after(out_part, own_two)))
    after_ff_all = jnp.concatenate(z_pieces(after_ff), axis=0)
    residual_cut = jnp.moveaxis(after(residual_s, own_two).reshape(64, 4, wide), 1, 0)
    residual_all = jnp.concatenate(
        z_exchange([pick(residual_cut, lax.rem(t + j, 4)) for j in range(4)]), axis=0
    )
    output = residual_all + mm(after_ff_all, proj_out_full, 1, 0)
    output = jnp.concatenate([output, output], axis=0)
    output = lax.dynamic_slice_in_dim(output, lax.rem(4 - t, 4) * 64, 256, 0) * own_valid
    grad_proj_out = scatter_plane(mm(after_ff_all, cot_relative, 0, 0))
    grad_text_weight = mm(text_own, text_grads, 0, 0) + mm(text_other, swap(text_grads), 0, 0)
    gain_sums = z_sum(after(jnp.stack([grad_gain_self, grad_gain_cross, grad_gain_ff]), own_two))
    *grad_act_two, grad_conv_second, output = together(*grad_act_two, grad_conv_second, output)

    *grad_act_one, image_grad, grad_tau, grad_gain_mid = first_conv_back(
        marks,
        grad_act_two,
        strips_one,
        gain_mid[None, :],
        stats_two,
        conv_first.transpose(0, 1, 3, 2).reshape(9 * wide, width),
    )
    grad_act_one_sum = z_collect(grad_act_one)
    grad_conv_first = first_conv_weight(marks, image_one, after(image_grad, grad_act_one[0]))
    grad_act_one_sum, grad_conv_first = together(grad_act_one_sum, grad_conv_first)
    grad_conv_first = grad_conv_first.reshape(3, 3, width, wide)
    grad_time_weight = mm(own_features, grad_tau, 0, 0)

    grad_act_one_sum = grad_act_one_sum.reshape(2, 4, 64, width)
    stats_one = jnp.where(item == 0, stats_one, stats_one[::-1])
    mean_one, inv_one = stats_one[:, 0], stats_one[:, 1]
    centred_one_q = (quarter(source.reshape(2, 4, 256, width)) - spread(mean_one)) * (
        spread(inv_one) * q_valid
    )
    norm_one_q = centred_one_q * gain_in
    gate_one = jax.nn.sigmoid(norm_one_q)
    grad_norm_one = grad_act_one_sum * gate_one * (1.0 + norm_one_q * (1.0 - gate_one))
    scaled_one = grad_norm_one * gain_in
    sums = z_sum(
        jnp.stack(
            [
                strip_sums(scaled_one),
                strip_sums(scaled_one * centred_one_q),
                strip_sums(grad_norm_one * centred_one_q),
            ]
        )
    )
    grad_gain_in = jnp.sum(sums[2], axis=0)
    grad_hidden = grad_residual_q + spread(inv_one) * q_valid * (
        scaled_one
        - spread(group_sum(sums[0]) / counts)
        - centred_one_q * spread(group_sum(sums[1]) / counts)
    )
    extra = jnp.concatenate(
        [
            jnp.broadcast_to(grad_gain_three, (8, 1, width)),
            jnp.moveaxis(gain_sums.reshape(3, 8, width), 1, 0),
            jnp.zeros((8, 4, width), jnp.float32),
        ],
        axis=1,
    )
    moved = jnp.concatenate([grad_hidden.reshape(8, 64, width), extra], axis=1)
    moved = lax.all_to_all(moved, IH, 0, 0)
    grad_hidden = jnp.moveaxis(moved[:, :64], 0, 1).reshape(64, channels)
    grad_hidden = z_order(z_pieces(grad_hidden), 0).reshape(256, channels)
    grad_gain_attn = lax.dynamic_slice_in_dim(
        moved[:, 64].reshape(channels), t * wide, wide, 0
    )
    gain_sums = jnp.sum(moved[:, 65:68], axis=0)

    grad_query_cross, grad_out_cross = z_shares(cross_grads, 2)
    (grad_proj_in,) = z_shares(attn_grads[:, 1280:], 1)

    return (
        output[None],
        grad_hidden[None],
        grad_gain_in,
        grad_conv_first,
        grad_time_weight,
        grad_gain_mid[0],
        grad_conv_second,
        grad_gain_attn,
        grad_proj_in.T,
        gain_sums[0],
        attn_grads[:, :320],
        attn_grads[:, 320:640],
        attn_grads[:, 640:960],
        attn_grads[:, 960:1280].T,
        gain_sums[1],
        grad_query_cross,
        grad_text_weight[:, :wide],
        grad_text_weight[:, wide:],
        grad_out_cross.T,
        gain_sums[2],
        ff_grads[:, :2560].reshape(width, 2, channels),
        ff_grads[:, 2560:].T,
        grad_proj_out,
    )


def z_shares(columns, count):
    t = lax.axis_index(T)
    cut = columns.reshape(columns.shape[0], count, 4, 320)
    own = z_collect([pick(cut, lax.rem(t + j, 4), 2) for j in range(4)])
    return [own[:, k] for k in range(count)]


def solution(mesh):
    placed = (
        P(I, H, None),
        P(I, None, None),
        P(I),
        P(I),
        P(IH),
        P(None, None, IH, T),
        P(IH, T),
        P(T),
        P(None, None, T, IH),
        P(T),
        P(T, IH),
        P(IH),
        P(IH, T),
        P(IH, T),
        P(IH, T),
        P(T, IH),
        P(IH),
        P(IH, T),
        P(IH, T),
        P(IH, T),
        P(T, IH),
        P(IH),
        P(IH, None, T),
        P(T, IH),
        P(IH, T),
        P(I, H, T),
    )
    sizes = (mesh.shape[I], mesh.shape[H], mesh.shape[T])
    body = fast_shards if sizes == (2, 4, 4) else shards
    return jax.shard_map(
        body,
        mesh=mesh,
        in_specs=placed,
        out_specs=(
            P(I, H, T),
            P(I, H, None),
            P(IH),
            P(None, None, IH, T),
            P(IH, T),
            P(T),
            P(None, None, T, IH),
            P(T),
            P(T, IH),
            P(IH),
            P(IH, T),
            P(IH, T),
            P(IH, T),
            P(T, IH),
            P(IH),
            P(IH, T),
            P(IH, T),
            P(IH, T),
            P(T, IH),
            P(IH),
            P(IH, None, T),
            P(T, IH),
            P(IH, T),
        ),
        check_vma=False,
    )
```

profile of v0, /device:TPU:0, one launch (start us, length us, event | category | flops | bytes accessed | tf_op | source)
XLA Modules:
  0.0 1246.0 jit_solution(5662514722865085597)
XLA Ops:
  34.6 16.5 %all-to-all-done = f32[8,256,160]{1,2,0:T(8,128)S(1)} async-done(((f32[8,256,160]{1,2,0:T(8,128)}), f32[8,256,160]{1,2,0:T(8,128)S(1)}, u32[]{:S(2)}, u32[]{:S(2)}) %all-to-all-start) | async-done | bytes 1310752 | tf_op jit(solution)/shard_map/all_to_all | solution.py:639
  52.9 19.0 %shard_map.425 = (f32[4,256,320]{2,1,0:T(8,128)}, f32[4,256,320]{2,1,0:T(8,128)}, f32[2,1152,160]{2,1,0:T(8,128)}, f32[2,8,160]{2,1,0:T(8,128)}) custom-call(s32[7]{0:T(128)} %stack.107.marks, f32[8,256,160]{2,1,0:T(8,128)} %copy.176.source, f32[1,160]{1,0:T(1,128)} %bitcast.418, f32[2,320]{1,0:T(2,128)} %fusion.113.tau, f32[1440,320]{1,0:T(8,128)} %bitcast.341), custom_call_target="tpu_custom_call" | custom-call | flops 5662310400 | bytes 10485760 | tf_op jit(solution)/shard_map/pallas_call | solution.py:930
  114.6 15.4 %collective-permute-done.5 = f32[256,320]{1,0:T(8,128)} collective-permute-done((f32[256,320]{1,0:T(8,128)}, f32[256,320]{1,0:T(8,128)}, u32[]{:S(2)}, u32[]{:S(2)}) %collective-permute-start.5) | collective-permute-done | bytes 327712 | tf_op jit(solution)/shard_map/ppermute | solution.py:569
  130.0 16.5 %collective-permute-done.7 = f32[256,320]{1,0:T(8,128)} collective-permute-done((f32[256,320]{1,0:T(8,128)}, f32[256,320]{1,0:T(8,128)}, u32[]{:S(2)}, u32[]{:S(2)}) %collective-permute-start.7) | collective-permute-done | bytes 327712 | tf_op jit(solution)/shard_map/ppermute | solution.py:569
  190.9 20.6 %shard_map.426 = (f32[8,64,160]{2,1,0:T(8,128)}, f32[8,64,160]{2,1,0:T(8,128)}, f32[8,64,160]{2,1,0:T(8,128)}, f32[8,64,160]{2,1,0:T(8,128)}, f32[2,1152,320]{2,1,0:T(8,128)}, /*index=5*/f32[2,8,320]{2,1,0:T(8,128)}) custom-call(s32[7]{0:T(128)} %stack.107.marks, f32[256,320]{1,0:T(8,128)} %fusion.77.refs_0_.refs_8_, ...), custom_call_target="tpu_custom_call" | custom-call | flops 5662310400 | bytes 10485760 | tf_op jit(solution)/shard_map/pallas_call | solution.py:930
  229.4 21.6 %collective-permute-done.19 = f32[8,64,160]{2,1,0:T(8,128)S(1)} collective-permute-done((f32[8,64,160]{2,1,0:T(8,128)}, f32[8,64,160]{2,1,0:T(8,128)S(1)}, u32[]{:S(2)}, u32[]{:S(2)}) %collective-permute-start.19) | collective-permute-done | bytes 327712 | tf_op jit(solution)/shard_map/ppermute | solution.py:573
  252.1 10.4 collective-permute-start.22
  282.0 10.5 all-to-all-done.2
  312.0 13.1 %collective-permute-done.28 = f32[64,1280]{1,0:T(8,128)S(1)} collective-permute-done((f32[64,1280]{1,0:T(8,128)S(1)}, f32[64,1280]{1,0:T(8,128)S(1)}, u32[]{:S(2)}, u32[]{:S(2)}) %collective-permute-start.28) | collective-permute-done | bytes 327712 | tf_op jit(solution)/shard_map/ppermute | solution.py:573
  350.0 14.1 %collective-permute-done.45 = f32[77,640]{1,0:T(8,128)S(1)} collective-permute-done((f32[77,640]{1,0:T(8,128)S(1)}, f32[77,640]{1,0:T(8,128)S(1)}, u32[]{:S(2)}, u32[]{:S(2)}) %collective-permute-start.45) | collective-permute-done | bytes 197152 | tf_op jit(solution)/shard_map/ppermute | solution.py:573
  405.4 11.5 collective-permute-start.33
  474.9 11.9 collective-permute-done.48
  520.2 12.5 %shard_map.427 = f32[1280,3840]{1,0:T(8,128)} custom-call(f32[256,1280]{1,0:T(8,128)S(1)} %pad_maximum_fusion.5.refs_0_, f32[256,1280]{1,0:T(8,128)S(1)} %constant_dynamic-update-slice_fusion.refs_1_, f32[256,3840]{1,0:T(8,128)} %pad_maximum_fusion.1.refs_2_), custom_call_target="tpu_custom_call" | custom-call | flops 7549747200 | bytes 22020096 | tf_op jit(solution)/shard_map/pallas_call | solution.py:969
  573.8 12.8 %collective-permute-done.54 = f32[64,1280]{1,0:T(8,128)S(1)} collective-permute-done((f32[64,1280]{1,0:T(8,128)S(1)}, f32[64,1280]{1,0:T(8,128)S(1)}, u32[]{:S(2)}, u32[]{:S(2)}) %collective-permute-start.54) | collective-permute-done | bytes 327712 | tf_op jit(solution)/shard_map/ppermute | solution.py:573
  636.2 12.5 %collective-permute-done.56 = f32[256,640]{1,0:T(8,128)} collective-permute-done((f32[256,640]{1,0:T(8,128)}, f32[256,640]{1,0:T(8,128)}, u32[]{:S(2)}, u32[]{:S(2)}) %collective-permute-start.56) | collective-permute-done | bytes 655392 | tf_op jit(solution)/shard_map/ppermute | solution.py:569
  654.3 20.8 %collective-permute-done.58 = f32[256,640]{1,0:T(8,128)} collective-permute-done((f32[256,640]{1,0:T(8,128)}, f32[256,640]{1,0:T(8,128)}, u32[]{:S(2)}, u32[]{:S(2)}) %collective-permute-start.58) | collective-permute-done | bytes 655392 | tf_op jit(solution)/shard_map/ppermute | solution.py:569
  682.1 10.0 collective-permute-start.59
  736.3 10.3 shard_map.429
  817.2 19.9 %collective-permute-done.109 = f32[77,640]{1,0:T(8,128)S(1)} collective-permute-done((f32[77,640]{1,0:T(8,128)}, f32[77,640]{1,0:T(8,128)S(1)}, u32[]{:S(2)}, u32[]{:S(2)}) %collective-permute-start.109) | collective-permute-done | bytes 197152 | tf_op jit(solution)/shard_map/ppermute | solution.py:569
  858.1 10.3 collective-permute-done.67.refs_3_
  868.3 19.9 %collective-permute-done.66.refs_2_ = f32[8,64,160]{2,1,0:T(8,128)S(1)} collective-permute-done((f32[8,64,160]{2,1,0:T(8,128)S(1)}, f32[8,64,160]{2,1,0:T(8,128)S(1)}, u32[]{:S(2)}, u32[]{:S(2)}) %collective-permute-start.66) | collective-permute-done | bytes 327712 | tf_op jit(solution)/shard_map/ppermute | solution.py:573
  889.0 18.5 %shard_map.430 = (f32[4,256,320]{2,1,0:T(8,128)}, f32[4,256,320]{2,1,0:T(8,128)}, f32[2,1152,160]{2,1,0:T(8,128)}) custom-call(s32[7]{0:T(128)} %stack.107.marks, f32[8,64,160]{2,1,0:T(8,128)} %bitcast.350, f32[8,64,160]{2,1,0:T(8,128)} %collective-permute-done.65.refs_1_, f32[8,64,160]{2,1,0:T(8,128)} %copy-done.95, f32[8,64,160]{2,1,0:T(8,128)} %copy-done.94, ...), custom_call_target="tpu_custom_call" | custom-call | flops 5662310400 | bytes 10485760 | tf_op jit(solution)/shard_map/pallas_call | solution.py:930
  940.7 13.3 %collective-permute-done.83 = f32[64,1280]{1,0:T(8,128)} collective-permute-done((f32[64,1280]{1,0:T(8,128)}, f32[64,1280]{1,0:T(8,128)}, u32[]{:S(2)}, u32[]{:S(2)}) %collective-permute-start.83) | collective-permute-done | bytes 327712 | tf_op jit(solution)/shard_map/ppermute | solution.py:573
  961.5 13.4 %collective-permute-done.71 = f32[256,320]{1,0:T(8,128)} collective-permute-done((f32[256,320]{1,0:T(8,128)}, f32[256,320]{1,0:T(8,128)}, u32[]{:S(2)}, u32[]{:S(2)}) %collective-permute-start.71) | collective-permute-done | bytes 327712 | tf_op jit(solution)/shard_map/ppermute | solution.py:569
  989.4 20.2 %shard_map.431 = f32[9,320,160]{2,1,0:T(8,128)} custom-call(s32[7]{0:T(128)} %stack.107.marks, f32[2,1152,320]{2,1,0:T(8,128)} %get-tuple-element.145.image, f32[2,1152,160]{2,1,0:T(8,128)} %get-tuple-element.147.grad), custom_call_target="tpu_custom_call" | custom-call | flops 5662310400 | bytes 10485760 | tf_op jit(solution)/shard_map/pallas_call | solution.py:930
  1028.7 23.8 %shard_map.432 = (f32[8,64,160]{2,1,0:T(8,128)}, f32[8,64,160]{2,1,0:T(8,128)}, f32[8,64,160]{2,1,0:T(8,128)}, f32[8,64,160]{2,1,0:T(8,128)}, f32[2,1152,320]{2,...) custom-call(s32[7]{0:T(128)} %stack.107.marks, f32[256,320]{1,0:T(8,128)} %fusion.74.refs_0_, ...), custom_call_target="tpu_custom_call" | custom-call | flops 5662310400 | bytes 10485760 | tf_op jit(solution)/shard_map/pallas_call | solution.py:930
  1057.9 20.1 %shard_map.433 = f32[9,160,320]{2,1,0:T(8,128)} custom-call(s32[7]{0:T(128)} %stack.107.marks, f32[2,1152,160]{2,1,0:T(8,128)} %get-tuple-element.167.image, f32[2,1152,320]{2,1,0:T(8,128)} %get-tuple-element.169.grad), custom_call_target="tpu_custom_call" | custom-call | flops 5662310400 | bytes 10485760 | tf_op jit(solution)/shard_map/pallas_call | solution.py:930
  1078.0 13.7 %collective-permute-done.89 = f32[8,64,160]{2,1,0:T(8,128)S(1)} collective-permute-done((f32[8,64,160]{2,1,0:T(8,128)}, f32[8,64,160]{2,1,0:T(8,128)S(1)}, u32[]{:S(2)}, u32[]{:S(2)}) %collective-permute-start.89) | collective-permute-done | bytes 327712 | tf_op jit(solution)/shard_map/ppermute | solution.py:573
  1092.2 10.9 collective-permute-start.92
  1135.5 16.6 %collective-permute-done.97 = f32[64,1280]{1,0:T(8,128)S(1)} collective-permute-done((f32[64,1280]{1,0:T(8,128)}, f32[64,1280]{1,0:T(8,128)S(1)}, u32[]{:S(2)}, u32[]{:S(2)}) %collective-permute-start.97) | collective-permute-done | bytes 327712 | tf_op jit(solution)/shard_map/ppermute | solution.py:573
  1179.2 18.2 %collective-permute-done.104 = f32[160,2,320]{2,0,1:T(8,128)S(1)} collective-permute-done((f32[160,2,320]{2,0,1:T(8,128)S(1)}, f32[160,2,320]{2,0,1:T(8,128)S(1)}, u32[]{:S(2)}, u32[]{:S(2)}) %collective-permute-start.104) | collective-permute-done | bytes 409632 | tf_op jit(solution)/shard_map/ppermute | solution.py:573
  1202.6 10.8 collective-permute-start.100
  (789 shorter events, 738.0 us)
Async XLA Ops:
  7.2 144.8 %all-gather.4.cloned.1.call-start = ((), (), s32[]{:S(2)}) async-start(), calls=%async_computation.10 | async-start | bytes 10321920 | tf_op jit(solution)/shard_map/all_gather | solution.py:1131
  10.8 61.1 %collective-permute-start.26 = (f32[168,960]{1,0:T(8,128)S(1)}, f32[168,960]{1,0:T(8,128)}, u32[]{:S(2)}, u32[]{:S(2)}) collective-permute-start(f32[168,960]{1,0:T(8,128)S(1)} %select_maximum_fusion), channel_id=1, source_target_pairs={{0,1},{1,2},{2,3},{3,0},{4,5},{5,6},{6,7},{7,4},{8,9},{9,10},{10,1... | collective-permute-start | bytes 1935368 | tf_op jit(solution)/shard_map/ppermute | solution.py:573
  13.9 58.1 %collective-permute-start.25 = (f32[168,960]{1,0:T(8,128)S(1)}, f32[168,960]{1,0:T(8,128)}, u32[]{:S(2)}, u32[]{:S(2)}) collective-permute-start(f32[168,960]{1,0:T(8,128)S(1)} %select_maximum_fusion), channel_id=1, source_target_pairs={{0,2},{1,3},{2,0},{3,1},{4,6},{5,7},{6,4},{7,5},{8,10},{9,11},{10,... | collective-permute-start | bytes 1935368 | tf_op jit(solution)/shard_map/ppermute | solution.py:573
  16.5 55.5 %collective-permute-start.24 = (f32[168,960]{1,0:T(8,128)S(1)}, f32[168,960]{1,0:T(8,128)}, u32[]{:S(2)}, u32[]{:S(2)}) collective-permute-start(f32[168,960]{1,0:T(8,128)S(1)} %select_maximum_fusion), channel_id=1, source_target_pairs={{0,3},{1,0},{2,1},{3,2},{4,7},{5,4},{6,5},{7,6},{8,11},{9,8},{10,9... | collective-permute-start | bytes 1935368 | tf_op jit(solution)/shard_map/ppermute | solution.py:573
  25.2 267.9 %all-gather.6.cloned.1.call-start = ((), (), s32[]{:S(2)}) async-start(), calls=%async_computation.11 | async-start | bytes 22118400 | tf_op jit(solution)/shard_map/all_gather | solution.py:1131
  88.2 330.5 %all-gather.8.cloned.1.call-start = ((), (), s32[]{:S(2)}) async-start(), calls=%async_computation.12 | async-start | bytes 22118400 | tf_op jit(solution)/shard_map/all_gather | solution.py:1131
  109.4 37.1 %collective-permute-start.7 = (f32[256,320]{1,0:T(8,128)}, f32[256,320]{1,0:T(8,128)}, u32[]{:S(2)}, u32[]{:S(2)}) collective-permute-start(f32[256,320]{1,0:T(8,128)} %get-tuple-element.328), channel_id=1, source_target_pairs={{0,12},{4,8},{8,4},{12,0},{1,13},{5,9},{9,5},{13,1},{2,14},{6,10},... | collective-permute-start | bytes 983048 | tf_op jit(solution)/shard_map/ppermute | solution.py:569
  111.1 35.4 %collective-permute-start.6 = (f32[256,320]{1,0:T(8,128)}, f32[256,320]{1,0:T(8,128)}, u32[]{:S(2)}, u32[]{:S(2)}) collective-permute-start(f32[256,320]{1,0:T(8,128)} %get-tuple-element.329), channel_id=1, source_target_pairs={{0,8},{4,12},{8,0},{12,4},{1,9},{5,13},{9,1},{13,5},{2,10},{6,14},... | collective-permute-start | bytes 983048 | tf_op jit(solution)/shard_map/ppermute | solution.py:569
  150.6 33.3 %collective-permute-start.8 = (f32[256,320]{1,0:T(8,128)}, f32[256,320]{1,0:T(8,128)}, u32[]{:S(2)}, u32[]{:S(2)}) collective-permute-start(f32[256,320]{1,0:T(8,128)} %fusion.77.refs_0_.refs_8_), channel_id=1, source_target_pairs={{0,4},{4,0},{8,12},{12,8},{1,5},{5,1},{9,13},{13,9},{2,6},{6,2},{1... | collective-permute-start | bytes 983048 | tf_op jit(solution)/shard_map/ppermute | solution.py:569
  212.5 38.4 %collective-permute-start.19 = (f32[8,64,160]{2,1,0:T(8,128)}, f32[8,64,160]{2,1,0:T(8,128)S(1)}, u32[]{:S(2)}, u32[]{:S(2)}) collective-permute-start(f32[8,64,160]{2,1,0:T(8,128)} %get-tuple-element.119), channel_id=1, source_target_pairs={{0,2},{1,3},{2,0},{3,1},{4,6},{5,7},{6,4},{7,5},{8,10},{9,11},{10,... | collective-permute-start | bytes 983048 | tf_op jit(solution)/shard_map/ppermute | solution.py:573
  214.9 36.0 %collective-permute-start.20 = (f32[8,64,160]{2,1,0:T(8,128)}, f32[8,64,160]{2,1,0:T(8,128)S(1)}, u32[]{:S(2)}, u32[]{:S(2)}) collective-permute-start(f32[8,64,160]{2,1,0:T(8,128)} %get-tuple-element.120), channel_id=1, source_target_pairs={{0,3},{1,0},{2,1},{3,2},{4,7},{5,4},{6,5},{7,6},{8,11},{9,8},{10,9... | collective-permute-start | bytes 983048 | tf_op jit(solution)/shard_map/ppermute | solution.py:573
  219.5 46.3 %collective-permute-start.40 = (f32[77,640]{1,0:T(8,128)S(1)}, f32[77,640]{1,0:T(8,128)S(1)}, u32[]{:S(2)}, u32[]{:S(2)}) collective-permute-start(f32[77,640]{1,0:T(8,128)S(1)} %fusion.140), channel_id=1, source_target_pairs={{0,16},{16,0},{1,17},{17,1},{2,18},{18,2},{3,19},{19,3},{4,20},{20... | collective-permute-start | bytes 591368 | tf_op jit(solution)/shard_map/ppermute | solution.py:565
  277.4 878.4 %reduce-scatter.7.cloned.1.call-start = ((), (), s32[]{:S(2)}) async-start(), calls=%async_computation.14 | async-start | bytes 14745600 | tf_op jit(solution)/shard_map/reduce_scatter | solution.py:1135
  342.7 35.0 %collective-permute-start.38 = (f32[64,1280]{1,0:T(8,128)S(1)}, f32[64,1280]{1,0:T(8,128)}, u32[]{:S(2)}, u32[]{:S(2)}) collective-permute-start(f32[64,1280]{1,0:T(8,128)S(1)} %fusion.88), channel_id=1, source_target_pairs={{0,1},{1,2},{2,3},{3,0},{4,5},{5,6},{6,7},{7,4},{8,9},{9,10},{10,1... | collective-permute-start | bytes 983048 | tf_op jit(solution)/shard_map/ppermute | solution.py:573
  342.7 33.9 %collective-permute-start.37 = (f32[64,1280]{1,0:T(8,128)S(1)}, f32[64,1280]{1,0:T(8,128)}, u32[]{:S(2)}, u32[]{:S(2)}) collective-permute-start(f32[64,1280]{1,0:T(8,128)S(1)} %fusion.88), channel_id=1, source_target_pairs={{0,2},{1,3},{2,0},{3,1},{4,6},{5,7},{6,4},{7,5},{8,10},{9,11},{10,... | collective-permute-start | bytes 983048 | tf_op jit(solution)/shard_map/ppermute | solution.py:573
  618.3 36.0 %collective-permute-start.57 = (f32[256,640]{1,0:T(8,128)}, f32[256,640]{1,0:T(8,128)}, u32[]{:S(2)}, u32[]{:S(2)}) collective-permute-start(f32[256,640]{1,0:T(8,128)} %get-tuple-element.311), channel_id=1, source_target_pairs={{0,8},{4,12},{8,0},{12,4},{1,9},{5,13},{9,1},{13,5},{2,10},{6,14},... | collective-permute-start | bytes 1966088 | tf_op jit(solution)/shard_map/ppermute | solution.py:569
  618.3 56.8 %collective-permute-start.58 = (f32[256,640]{1,0:T(8,128)}, f32[256,640]{1,0:T(8,128)}, u32[]{:S(2)}, u32[]{:S(2)}) collective-permute-start(f32[256,640]{1,0:T(8,128)} %get-tuple-element.312), channel_id=1, source_target_pairs={{0,12},{4,8},{8,4},{12,0},{1,13},{5,9},{9,5},{13,1},{2,14},{6,10},... | collective-permute-start | bytes 1966088 | tf_op jit(solution)/shard_map/ppermute | solution.py:569
  727.4 472.5 %reduce-scatter.5.cloned.1.call-start = ((), (), s32[]{:S(2)}) async-start(), calls=%async_computation.13 | async-start | bytes 14745600 | tf_op jit(solution)/shard_map/reduce_scatter | solution.py:1135
  746.6 486.3 %reduce-scatter.9.cloned.1.call-start = ((), (), s32[]{:S(2)}) async-start(), calls=%async_computation.15 | async-start | bytes 22118400 | tf_op jit(solution)/shard_map/reduce_scatter | solution.py:1135
  800.6 49.5 %all-to-all-start.1 = ((f32[8,64,160]{2,1,0:T(8,128)}), f32[8,64,160]{2,1,0:T(8,128)}, u32[]{:S(2)}, u32[]{:S(2)}) async-start(f32[8,64,160]{2,1,0:T(8,128)} %copy.185), calls=%async_computation.1 | async-start | bytes 1048576 | tf_op jit(solution)/shard_map/all_to_all | solution.py:639
  812.7 43.6 %collective-permute-start.111 = (f32[77,640]{1,0:T(8,128)}, f32[77,640]{1,0:T(8,128)}, u32[]{:S(2)}, u32[]{:S(2)}) collective-permute-start(f32[77,640]{1,0:T(8,128)} %fusion.97), channel_id=1, source_target_pairs={{0,12},{4,8},{8,4},{12,0},{1,13},{5,9},{9,5},{13,1},{2,14},{6,10},... | collective-permute-start | bytes 591368 | tf_op jit(solution)/shard_map/ppermute | solution.py:569
  815.2 40.2 %collective-permute-start.110 = (f32[77,640]{1,0:T(8,128)}, f32[77,640]{1,0:T(8,128)}, u32[]{:S(2)}, u32[]{:S(2)}) collective-permute-start(f32[77,640]{1,0:T(8,128)} %fusion.97), channel_id=1, source_target_pairs={{0,8},{4,12},{8,0},{12,4},{1,9},{5,13},{9,1},{13,5},{2,10},{6,14},... | collective-permute-start | bytes 591368 | tf_op jit(solution)/shard_map/ppermute | solution.py:569
  851.6 36.6 %collective-permute-start.66 = (f32[8,64,160]{2,1,0:T(8,128)S(1)}, f32[8,64,160]{2,1,0:T(8,128)S(1)}, u32[]{:S(2)}, u32[]{:S(2)}) collective-permute-start(f32[8,64,160]{2,1,0:T(8,128)S(1)} %bitcast.348), channel_id=1, source_target_pairs={{0,2},{1,3},{2,0},{3,1},{4,6},{5,7},{6,4},{7,5},{8,10},{9,11},{10,... | collective-permute-start | bytes 983048 | tf_op jit(solution)/shard_map/ppermute | solution.py:573
  852.3 35.9 %collective-permute-start.65 = (f32[8,64,160]{2,1,0:T(8,128)S(1)}, f32[8,64,160]{2,1,0:T(8,128)}, u32[]{:S(2)}, u32[]{:S(2)}) collective-permute-start(f32[8,64,160]{2,1,0:T(8,128)S(1)} %bitcast.349), channel_id=1, source_target_pairs={{0,3},{1,0},{2,1},{3,2},{4,7},{5,4},{6,5},{7,6},{8,11},{9,8},{10,9... | collective-permute-start | bytes 983048 | tf_op jit(solution)/shard_map/ppermute | solution.py:573
  858.1 52.6 %collective-permute-start.112 = (f32[77,640]{1,0:T(8,128)}, f32[77,640]{1,0:T(8,128)S(1)}, u32[]{:S(2)}, u32[]{:S(2)}) collective-permute-start(f32[77,640]{1,0:T(8,128)} %reduce_sum.419), channel_id=1, source_target_pairs={{0,16},{16,0},{1,17},{17,1},{2,18},{18,2},{3,19},{19,3},{4,20},{20... | collective-permute-start | bytes 591368 | tf_op jit(solution)/shard_map/ppermute | solution.py:565
  939.0 36.0 %collective-permute-start.71 = (f32[256,320]{1,0:T(8,128)}, f32[256,320]{1,0:T(8,128)}, u32[]{:S(2)}, u32[]{:S(2)}) collective-permute-start(f32[256,320]{1,0:T(8,128)} %get-tuple-element.325), channel_id=1, source_target_pairs={{0,12},{4,8},{8,4},{12,0},{1,13},{5,9},{9,5},{13,1},{2,14},{6,10},... | collective-permute-start | bytes 983048 | tf_op jit(solution)/shard_map/ppermute | solution.py:569
  984.4 37.8 %collective-permute-start.85 = (f32[64,1280]{1,0:T(8,128)S(1)}, f32[64,1280]{1,0:T(8,128)S(1)}, u32[]{:S(2)}, u32[]{:S(2)}) collective-permute-start(f32[64,1280]{1,0:T(8,128)S(1)} %add_add_fusion.2), channel_id=1, source_target_pairs={{0,3},{1,0},{2,1},{3,2},{4,7},{5,4},{6,5},{7,6},{8,11},{9,8},{10,9... | collective-permute-start | bytes 983048 | tf_op jit(solution)/shard_map/ppermute | solution.py:573
  988.9 33.4 %collective-permute-start.72 = (f32[256,320]{1,0:T(8,128)}, f32[256,320]{1,0:T(8,128)}, u32[]{:S(2)}, u32[]{:S(2)}) collective-permute-start(f32[256,320]{1,0:T(8,128)} %fusion.74.refs_0_), channel_id=1, source_target_pairs={{0,4},{4,0},{8,12},{12,8},{1,5},{5,1},{9,13},{13,9},{2,6},{6,2},{1... | collective-permute-start | bytes 983048 | tf_op jit(solution)/shard_map/ppermute | solution.py:569
  1054.0 37.6 %collective-permute-start.89 = (f32[8,64,160]{2,1,0:T(8,128)}, f32[8,64,160]{2,1,0:T(8,128)S(1)}, u32[]{:S(2)}, u32[]{:S(2)}) collective-permute-start(f32[8,64,160]{2,1,0:T(8,128)} %get-tuple-element.165), channel_id=1, source_target_pairs={{0,2},{1,3},{2,0},{3,1},{4,6},{5,7},{6,4},{7,5},{8,10},{9,11},{10,... | collective-permute-start | bytes 983048 | tf_op jit(solution)/shard_map/ppermute | solution.py:573
  1056.8 34.8 %collective-permute-start.90 = (f32[8,64,160]{2,1,0:T(8,128)}, f32[8,64,160]{2,1,0:T(8,128)S(1)}, u32[]{:S(2)}, u32[]{:S(2)}) collective-permute-start(f32[8,64,160]{2,1,0:T(8,128)} %get-tuple-element.166), channel_id=1, source_target_pairs={{0,3},{1,0},{2,1},{3,2},{4,7},{5,4},{6,5},{7,6},{8,11},{9,8},{10,9... | collective-permute-start | bytes 983048 | tf_op jit(solution)/shard_map/ppermute | solution.py:573
  1118.4 120.2 %reduce-scatter.11.cloned.1.call-start = ((), (), s32[]{:S(2)}) async-start(), calls=%async_computation.16 | async-start | bytes 2211840 | tf_op jit(solution)/shard_map/reduce_scatter | solution.py:1135
  1129.9 40.1 %collective-permute-start.99 = (f32[64,1280]{1,0:T(8,128)}, f32[64,1280]{1,0:T(8,128)}, u32[]{:S(2)}, u32[]{:S(2)}) collective-permute-start(f32[64,1280]{1,0:T(8,128)} %reshape.549), channel_id=1, source_target_pairs={{0,1},{1,2},{2,3},{3,0},{4,5},{5,6},{6,7},{7,4},{8,9},{9,10},{10,1... | collective-permute-start | bytes 983048 | tf_op jit(solution)/shard_map/ppermute | solution.py:573
  (202 other events, 3436.9 us)
Sparse Core Ops, SparseCore 0:
  10.8 74.4 all-gather.3
  88.3 135.6 all-gather.5
  226.0 117.2 all-gather.7
  586.8 126.8 reduce-scatter.6
  746.7 119.1 reduce-scatter.4
  869.4 163.0 reduce-scatter.8
  1123.2 38.9 reduce-scatter.10
where the time goes:
time: 1260 us; the launch traced here: 1250 us
  waiting for transfers between devices  476 us (38%)
  starting transfers between devices  246 us (20%)
  local copies, waits for them, and re-layouts  156 us (12%)
  Pallas kernels  151 us (12%)
  matrix products  146 us (12%)
  other arithmetic  52.4 us (4%)
  between operations  18.5 us (1%)
    ppermute x75, waiting for transfers between devices, turn(): return lax.ppermute(values, T, [(s, (s + step) % 4) for s in range(4)])  302 us
    ppermute x75, starting transfers between devices, turn(): return lax.ppermute(values, T, [(s, (s + step) % 4) for s in range(4)])  194 us
    ppermute x24, waiting for transfers between devices, flip(): return lax.ppermute(values, H, [(s, s ^ step) for s in range(4)])  145 us
    pallas_call x6, Pallas kernels, run_kernel(): pl.pallas_call(body, out_shape=[jax.ShapeDtypeStruct(shape, jnp.float32)...  122 us
    dot_general x23, matrix products, mm(): lax.dot_general(left, right, (((left_dim,), (right_dim,)), ((), ())), pre...  109 us
    dot_general x12, matrix products, ein(): jnp.einsum(form, left, right, precision=high, preferred_element_type=jnp....  36.7 us
    pallas_call x3, Pallas kernels, weight_grads(): pl.pallas_call(functools.partial(weight_kernel, plan), out_shape=jax.Shap...  29 us
    unnamed x233, local copies, waits for them, and re-layouts  26.6 us
  transfers between devices with their start and end apart: 126, of which 58 were waited for; matrix products, arithmetic and copies ran while one was open for 22% of the time, Pallas kernels for 12%

commit v1 on v0

--- a/solution.py
+++ b/solution.py
@@ -577,29 +577,29 @@
     return [values] + [turn(values, 4 - j) for j in (1, 2, 3)]
 
 
-def z_collect(pieces):
-    total = pieces[0]
-    for j in (1, 2, 3):
-        total = total + turn(pieces[j], j)
-    return total
-
-
-def z_exchange(pieces):
-    return [pieces[0]] + [turn(pieces[4 - j], 4 - j) for j in (1, 2, 3)]
-
-
-def z_order(pieces, axis):
-    t = lax.axis_index(T)
-    shape = list(pieces[0].shape)
-    shape.insert(axis, 4)
-    whole = jnp.zeros(shape, pieces[0].dtype)
-    for j in range(4):
-        whole = lax.dynamic_update_index_in_dim(whole, pieces[j], lax.rem(t + j, 4), axis)
-    return whole
-
-
-def z_sum(values):
-    return jnp.sum(z_order(z_pieces(values), 0), axis=0)
+def total_of(pieces):
+    return (pieces[0] + pieces[1]) + (pieces[2] + pieces[3])
+
+
+def z_received(pieces):
+    return [pieces[0]] + [turn(pieces[j], j) for j in (1, 2, 3)]
+
+
+def z_all(values):
+    return lax.all_to_all(values, T, 0, 0)
+
+
+def z_spread(values):
+    return z_all(jnp.broadcast_to(values[None], (4,) + values.shape))
+
+
+def folded(values):
+    values = jnp.pad(values, ((0, 3), (0, 0)))
+    return jnp.concatenate([values[:40], values[40:]], axis=1)
+
+
+def unfolded(values):
+    return jnp.concatenate([values[:, :640], values[:37, 640:]], axis=0)
 
 
 def h_collect(pieces):
@@ -610,40 +610,22 @@
 
 
 def h_sum(values):
-    h = lax.axis_index(H)
-    pieces = [values] + [flip(values, j) for j in (1, 2, 3)]
-    whole = jnp.zeros((4,) + values.shape, values.dtype)
-    for j in range(4):
-        whole = lax.dynamic_update_index_in_dim(whole, pieces[j], h ^ j, 0)
-    return jnp.sum(whole, axis=0)
+    pair = values + flip(values, 1)
+    return pair + flip(pair, 2)
 
 
 def pick(values, index, axis=0):
     return lax.dynamic_index_in_dim(values, index, axis, keepdims=False)
 
 
-def plane_sum(own, other):
-    own = own + swap(other)
+def plane_sum(own):
     part = h_collect([own[j] for j in range(4)])
     pieces = [part] + [flip(part, j) for j in (1, 2, 3)]
-    return pieces + [swap(piece) for piece in pieces]
-
-
-def q_to_s(values):
-    moved = lax.all_to_all(values.reshape((8,) + values.shape[2:]), IH, 0, 0)
-    return jnp.moveaxis(moved, 0, 1).reshape(values.shape[2], -1)
-
-
-def s_to_q(values):
-    cut = jnp.moveaxis(values.reshape(values.shape[0], 8, -1), 1, 0)
-    moved = lax.all_to_all(cut, IH, 0, 0)
-    return moved.reshape((2, 4) + moved.shape[1:])
-
-
-def group_sum(channel_sums):
-    shape = channel_sums.shape
-    groups = jnp.sum(channel_sums.reshape(shape[:-1] + (shape[-1] // 40, 40)), axis=-1)
-    return jnp.repeat(groups, 40, axis=-1)
+    return pieces + [swap(piece) for piece in pieces], part
+
+
+def plane_exchange(packed):
+    return lax.all_to_all(packed, IH, 0, 0)
 
 
 IMAGE_ROWS = 1152
@@ -672,6 +654,30 @@
     return (lax.broadcasted_iota(jnp.int32, (rows, columns), 0) < span).astype(jnp.float32)
 
 
+def unpack_quarter(packed):
+    rest = jnp.concatenate([packed[64:80, 32 * g : 32 * g + 32] for g in range(4)], axis=0)
+    return jnp.concatenate([packed[:64], rest], axis=1)
+
+
+def put_quarter(out, place, values, row=0):
+    out[place, row : row + 64, :] = values[:, :128]
+    for g in range(4):
+        out[place, row + 64 : row + 80, 32 * g : 32 * g + 32] = values[
+            16 * g : 16 * g + 16, 128:160
+        ]
+
+
+def unpack_strip(packed):
+    rest = jnp.concatenate([packed[256:320, 64 * g : 64 * g + 64] for g in range(4)], axis=0)
+    return jnp.concatenate([packed[:256], rest], axis=1)
+
+
+def put_packed_strip(out, place, values):
+    out[place, 0:256, :] = values[:, :256]
+    for g in range(4):
+        out[place, 256:320, 64 * g : 64 * g + 64] = values[64 * g : 64 * g + 64, 256:320]
+
+
 def put_strip(image, b, strip, span, values):
     at = pl.multiple_of(margin + strip * span, 8)
     image[b, pl.ds(at, 240)] = values[:240]
@@ -679,6 +685,20 @@
     @pl.when(span == 256)
     def _():
         image[b, pl.ds(pl.multiple_of(at + 240, 8), 16)] = values[240:]
+
+
+def put_cells(image, b, strip, span, q, values):
+    at = pl.multiple_of(margin + strip * span + q * 64, 8)
+    image[b, pl.ds(at, 48)] = values[:48]
+
+    @pl.when((q < 3) | (span == 256))
+    def _():
+        image[b, pl.ds(pl.multiple_of(at + 48, 8), 16)] = values[48:]
+
+
+def quarter_mask(span, q):
+    row = lax.broadcasted_iota(jnp.int32, (64, 160), 0) + q * 64
+    return (row < span).astype(jnp.float32)
 
 
 def widen(wide, image, b, width, sign):
@@ -706,6 +726,13 @@
         low[k * rows : (k + 1) * rows, :] = second
 
 
+def split_weight_turned(weight, top, low):
+    for tap in range(9):
+        first, second = halves(weight[160 * tap : 160 * tap + 160, :].T)
+        top[320 * tap : 320 * tap + 320, :] = first
+        low[320 * tap : 320 * tap + 320, :] = second
+
+
 def conv_strip(wide, top, low, strip, span, width, sign):
     rows = top.shape[0] // 3
     total = None
@@ -740,7 +767,9 @@
     return jnp.sum(values, axis=0, keepdims=True)
 
 
-def first_kernel(marks, source, gain, tau, weight, own, other, image, stats, wide, top, low):
+def first_kernel(
+    marks, source, gain, tau, weight, own, other, image, stats, wide, top, low, cells
+):
     item, h = marks[4], marks[5]
     split_weight(weight, top, low)
     image[...] = jnp.zeros_like(image)
@@ -750,21 +779,23 @@
         total = jnp.zeros((1, 160), jnp.float32)
         squares = jnp.zeros((1, 160), jnp.float32)
         for k in range(4):
-            values = source[base + k]
-            total = total + column_sum(values)
-            squares = squares + column_sum(values * values)
+            for q in range(4):
+                values = unpack_quarter(source[base + k, 80 * q : 80 * q + 80, :])
+                cells[k, 64 * q : 64 * q + 64, :] = values
+                total = total + column_sum(values)
+                squares = squares + column_sum(values * values)
         mean, inv = group_row_stats(total, squares, span)
         stats[b, 0:1, :] = mean
         stats[b, 1:2, :] = inv
         for k in range(4):
-            norm = (source[base + k] - mean) * inv * row_mask(span, 256, 160) * gain[...]
+            norm = (cells[k] - mean) * inv * row_mask(span, 256, 160) * gain[...]
             put_strip(image, b, k, span, norm * jax.nn.sigmoid(norm))
         widen(wide, image, b, width, 1)
         added = tau[b : b + 1, :]
 
         def step(k, _):
             conv = conv_strip(wide, top, low, k, span, width, 1)
-            out[k ^ h] = conv + added * row_mask(span, 256, 320)
+            put_packed_strip(out, k ^ h, conv + added * row_mask(span, 256, 320))
             return 0
 
         lax.fori_loop(0, 4, step, 0)
@@ -773,7 +804,7 @@
 def put_quarters(outs, tile, place, t):
     for j in range(4):
         at = pl.multiple_of(lax.rem(t + j, 4) * 64, 8)
-        outs[j][place] = tile[pl.ds(at, 64), :]
+        put_quarter(outs[j], place, tile[pl.ds(at, 64), :])
 
 
 def second_kernel(marks, *refs):
@@ -781,21 +812,21 @@
     outs, image, stats = refs[10:14], refs[14], refs[15]
     wide, top, low, tile = refs[16:]
     item, h, t = marks[4], marks[5], marks[6]
-    split_weight(weight, top, low)
+    split_weight_turned(weight, top, low)
     image[...] = jnp.zeros_like(image)
     for b in range(2):
         span, width = marks_of(marks, b)
         total = jnp.zeros((1, 320), jnp.float32)
         squares = jnp.zeros((1, 320), jnp.float32)
         for j in range(4):
-            values = strips[4 * b + j][...]
+            values = unpack_strip(strips[4 * b + j][...])
             total = total + column_sum(values)
             squares = squares + column_sum(values * values)
         mean, inv = group_row_stats(total, squares, span)
         stats[b, 0:1, :] = mean
         stats[b, 1:2, :] = inv
         for j in range(4):
-            values = strips[4 * b + j][...]
+            values = unpack_strip(strips[4 * b + j][...])
             norm = (values - mean) * inv * row_mask(span, 256, 320) * gain[...]
             put_strip(image, b, h ^ j, span, norm * jax.nn.sigmoid(norm))
         widen(wide, image, b, width, 1)
@@ -820,22 +851,15 @@
 
         def fill(k, _):
             for j in range(4):
-                q = lax.rem(t + j, 4)
-                values = quarters[j][(item ^ b) * 4 + k]
-                at = pl.multiple_of(margin + k * span + q * 64, 8)
-                image[b, pl.ds(at, 48)] = values[:48]
-
-                @pl.when((q < 3) | (span == 256))
-                def _():
-                    image[b, pl.ds(pl.multiple_of(at + 48, 8), 16)] = values[48:]
-
+                values = unpack_quarter(quarters[j][(item ^ b) * 4 + k])
+                put_cells(image, b, k, span, lax.rem(t + j, 4), values)
             return 0
 
         lax.fori_loop(0, 4, fill, 0)
         widen(wide, image, b, width, -1)
 
         def step(k, _):
-            out[k ^ h] = conv_strip(wide, top, low, k, span, width, -1)
+            put_packed_strip(out, k ^ h, conv_strip(wide, top, low, k, span, width, -1))
             return 0
 
         lax.fori_loop(0, 4, step, 0)
@@ -846,7 +870,7 @@
     outs, image, sums, grad_gain = refs[19:23], refs[23], refs[24], refs[25]
     wide, top, low, tile, scaled_at, centred_at = refs[26:]
     item, h, t = marks[4], marks[5], marks[6]
-    split_weight(weight, top, low)
+    split_weight_turned(weight, top, low)
     image[...] = jnp.zeros_like(image)
     gain_total = jnp.zeros((1, 320), jnp.float32)
     for b in range(2):
@@ -855,10 +879,11 @@
         first = jnp.zeros((1, 320), jnp.float32)
         second = jnp.zeros((1, 320), jnp.float32)
         for j in range(4):
-            centred = (strips[4 * b + j][...] - mean) * inv * row_mask(span, 256, 320)
+            values = unpack_strip(strips[4 * b + j][...])
+            centred = (values - mean) * inv * row_mask(span, 256, 320)
             norm = centred * gain[...]
             gate = jax.nn.sigmoid(norm)
-            grad_norm = grads[4 * b + j][...] * gate * (1.0 + norm * (1.0 - gate))
+            grad_norm = unpack_strip(grads[4 * b + j][...]) * gate * (1.0 + norm * (1.0 - gate))
             scaled = grad_norm * gain[...]
             first = first + column_sum(scaled)
             second = second + column_sum(scaled * centred)
@@ -887,18 +912,18 @@
     grad_gain[...] = gain_total
 
 
-def first_weight_kernel(marks, image, grad, out, wide):
+def conv_weight_kernel(sign, marks, image, cells, out, wide):
     out[...] = jnp.zeros_like(out)
     for b in range(2):
         _, width = marks_of(marks, b)
-        widen(wide, image, b, width, 1)
+        widen(wide, image, b, width, sign)
         for i in range(3):
 
             def step(c, _):
-                at = pl.multiple_of(margin + c * 256 + (i - 1) * width, 8)
+                at = pl.multiple_of(margin + c * 256 + sign * (i - 1) * width, 8)
                 taps = halves(wide[pl.ds(at, 256), :].T)
-                cells = halves(grad[b, pl.ds(pl.multiple_of(margin + c * 256, 8), 256), :])
-                part = dot_halves(taps, cells, 1, 0)
+                values = halves(cells[b, pl.ds(pl.multiple_of(margin + c * 256, 8), 256), :])
+                part = dot_halves(taps, values, 1, 0)
                 for j in range(3):
                     out[3 * i + j] += part[160 * j : 160 * j + 160]
                 return 0
@@ -906,22 +931,306 @@
             lax.fori_loop(0, 4, step, 0)
 
 
-def second_weight_kernel(marks, image, grad, out, wide, total):
-    for i in range(3):
-        total[...] = jnp.zeros_like(total)
-        for b in range(2):
-            _, width = marks_of(marks, b)
-            widen(wide, grad, b, width, -1)
-
-            def step(c, _):
-                at = pl.multiple_of(margin + c * 256 - (i - 1) * width, 8)
-                cells = halves(image[b, pl.ds(pl.multiple_of(margin + c * 256, 8), 256), :].T)
-                total[...] += dot_halves(cells, halves(wide[pl.ds(at, 256), :]), 1, 0)
-                return 0
-
-            lax.fori_loop(0, 4, step, 0)
-        for j in range(3):
-            out[3 * i + j] = total[:, 160 * j : 160 * j + 160]
+def wide_halves(values):
+    top, low = halves(values)
+    return jnp.concatenate([top, top, low], axis=1)
+
+
+def other_halves(values):
+    top, low = halves(values)
+    return jnp.concatenate([top, low, top], axis=1)
+
+
+def dot_last(left, right):
+    return lax.dot_general(
+        left, right, (((1,), (1,)), ((), ())), preferred_element_type=jnp.float32
+    )
+
+
+def dot_pair(left, values):
+    top, low = halves(values)
+    both = jnp.dot(left[0], jnp.concatenate([top, low], axis=1), preferred_element_type=jnp.float32)
+    return (both[:, :64] + both[:, 64:]) + jnp.dot(
+        left[1], top, preferred_element_type=jnp.float32
+    )
+
+
+def scores_turned(marks, queries, pieces, head, j):
+    at = 64 * head
+    keys = pieces[j][:, at : at + 64]
+    scores = dot_last(wide_halves(keys), other_halves(queries[:, at : at + 64])) * 0.125
+    slot = lax.broadcasted_iota(jnp.int32, (256, 256), 0) + marks[6] * 64
+    slot = jnp.where(slot >= 256, slot - 256, slot)
+    return jnp.where(slot < marks[0], scores, masked_score)
+
+
+def attend_kernel(marks, qkv, *refs):
+    pieces, out, totals, held = refs[:4], refs[4], refs[5], refs[6]
+    totals[...] = jnp.zeros_like(totals)
+    for head in range(5):
+        peak = None
+        for j in range(4):
+            scores = scores_turned(marks, qkv, pieces, head, j)
+            held[256 * j : 256 * j + 256, :] = scores
+            here = jnp.max(scores, axis=0, keepdims=True)
+            peak = here if peak is None else jnp.maximum(peak, here)
+        total = jnp.zeros((1, 256), jnp.float32)
+        attended = jnp.zeros((64, 256), jnp.float32)
+        for j in range(4):
+            exponent = jnp.exp(held[256 * j : 256 * j + 256, :] - peak)
+            total = total + column_sum(exponent)
+            values = halves(pieces[j][:, 320 + 64 * head : 384 + 64 * head].T)
+            first, second = halves(exponent)
+            both = jnp.dot(
+                jnp.concatenate(values, axis=0), first, preferred_element_type=jnp.float32
+            )
+            attended = attended + (
+                (both[:64] + both[64:])
+                + jnp.dot(values[0], second, preferred_element_type=jnp.float32)
+            )
+        out[:, 64 * head : 64 * head + 64] = (attended / total).T
+        totals[head : head + 1, :] = peak + jnp.log(total)
+
+
+def attend_back_kernel(marks, qkv, *refs):
+    pieces, totals, attended, grad = refs[:4], refs[4], refs[5], refs[6]
+    grad_query, outs = refs[7], refs[8:12]
+    for head in range(5):
+        at = 64 * head
+        grad_out = grad[:, at : at + 64]
+        queries = qkv[:, at : at + 64]
+        delta = column_sum((grad_out * attended[:, at : at + 64]).T)
+        total = totals[head : head + 1, :]
+        grad_other = other_halves(grad_out)
+        query_grad = jnp.zeros((64, 256), jnp.float32)
+        for j in range(4):
+            weights = jnp.exp(scores_turned(marks, qkv, pieces, head, j) - total)
+            values = pieces[j][:, 320 + at : 384 + at]
+            grad_scores = weights * (dot_last(wide_halves(values), grad_other) - delta)
+            outs[j][:, 320 + at : 384 + at] = dot_pair(halves(weights), grad_out)
+            first, second = halves(grad_scores)
+            outs[j][:, at : at + 64] = dot_pair((first, second), queries) * 0.125
+            keys = halves(pieces[j][:, at : at + 64].T)
+            both = jnp.dot(
+                jnp.concatenate(keys, axis=0), first, preferred_element_type=jnp.float32
+            )
+            query_grad = query_grad + (
+                (both[:64] + both[64:])
+                + jnp.dot(keys[0], second, preferred_element_type=jnp.float32)
+            )
+        grad_query[:, at : at + 64] = query_grad.T * 0.125
+
+
+def pack_kernel(marks, values, out):
+    for q in range(values.shape[0] // 64):
+        for k in range(8):
+            part = values[64 * q : 64 * q + 64, 160 * k : 160 * k + 160]
+            put_quarter(out, k, part, 80 * q)
+
+
+def unpack_kernel(marks, packed, plain):
+    for k in range(8):
+        plain[:, 160 * k : 160 * k + 160] = unpack_quarter(packed[k, 0:80, :])
+
+
+def unpack_norm_kernel(marks, packed, gain, scaled, plain):
+    for k in range(8):
+        centred = unpack_quarter(packed[k, 0:80, :])
+        mean = jnp.concatenate([packed[k, 80:81, :], packed[k, 81:82, 0:32]], axis=1)
+        inv = jnp.concatenate([packed[k, 82:83, :], packed[k, 83:84, 0:32]], axis=1)
+        at = slice(160 * k, 160 * k + 160)
+        scaled[:, at] = centred * gain[:, at]
+        plain[:, at] = centred * (1.0 / inv) + mean
+
+
+def cotangent_kernel(marks, pieces, total, out, whole):
+    total[...] = (pieces[0, :, :1280] + pieces[1, :, :1280]) + (
+        pieces[2, :, :1280] + pieces[3, :, :1280]
+    )
+    for part in range(4):
+        whole[:, 320 * part : 320 * part + 320] = pieces[part, :, 1280:1600]
+    for k in range(8):
+        put_quarter(out, k, whole[:, 160 * k : 160 * k + 160])
+
+
+def third_kernel(marks, *refs):
+    pieces, out, gain = refs[:4], refs[4], refs[5]
+    for first in range(4):
+
+        @pl.when(marks[6] == first)
+        def _():
+            for j in range(4):
+                at = (first + j) % 4 * 320
+                gain[:, at : at + 320] = pieces[j][160:161, 0:320]
+                for m in range(3):
+                    out[:, 1280 * m + at : 1280 * m + at + 320] = pieces[j][
+                        0:160, 320 * m : 320 * m + 320
+                    ]
+
+
+def text_kernel(marks, pieces, rows, keys, values):
+    for part in range(4):
+        at = pl.multiple_of(lax.rem(part - marks[6] + 4, 4) * 64, 8)
+        rows[pl.ds(at, 64), :] = pieces[part, 0:64, :]
+        lanes = slice(320 * part, 320 * part + 320)
+        keys[0:40, lanes] = pieces[part, 64:104, 0:320]
+        values[0:40, lanes] = pieces[part, 64:104, 320:640]
+        keys[40:77, lanes] = pieces[part, 64:101, 640:960]
+        values[40:77, lanes] = pieces[part, 64:101, 960:1280]
+
+
+def text_grad_kernel(marks, rows, keys, values, out):
+    for part in range(4):
+        at = pl.multiple_of(lax.rem(part - marks[6] + 4, 4) * 64, 8)
+        out[part, 0:64, :] = rows[pl.ds(at, 64), :]
+        lanes = slice(320 * part, 320 * part + 320)
+        out[part, 64:104, 0:320] = keys[0:40, lanes]
+        out[part, 64:104, 320:640] = values[0:40, lanes]
+        out[part, 64:101, 640:960] = keys[40:77, lanes]
+        out[part, 64:101, 960:1280] = values[40:77, lanes]
+        out[part, 101:104, 640:1280] = jnp.zeros((3, 640), jnp.float32)
+
+
+def rows_kernel(marks, *refs):
+    pieces, out = refs[:4], refs[4]
+    for j in range(4):
+        at = pl.multiple_of(lax.rem(marks[6] + j, 4) * 64, 8)
+        out[pl.ds(at, 64), :] = pieces[j][...]
+
+
+def residual_kernel(marks, source, first, second, third, fourth, out, sums):
+    t = marks[6]
+    at = pl.multiple_of(t * 80, 8)
+    sums[...] = jnp.zeros_like(sums)
+    for b in range(2):
+        for k in range(4):
+            place = 4 * b + k
+            packed = source[place, pl.ds(at, 80), :] + (
+                (first[place] + second[place]) + (third[place] + fourth[place])
+            )
+            out[place] = packed
+            values = unpack_quarter(packed)
+            sums[2 * b : 2 * b + 1, :] += column_sum(values)
+            sums[2 * b + 1 : 2 * b + 2, :] += column_sum(values * values)
+
+
+def span_of_item(marks, b):
+    return jnp.where(marks[4] == b, marks[0], marks[2])
+
+
+def norm_kernel(marks, residual, first, second, third, fourth, out, stats):
+    total = (first[...] + second[...]) + (third[...] + fourth[...])
+    for b in range(2):
+        span = span_of_item(marks, b)
+        mean, inv = group_row_stats(
+            total[2 * b : 2 * b + 1, :], total[2 * b + 1 : 2 * b + 2, :], span
+        )
+        stats[2 * b : 2 * b + 1, :] = mean
+        stats[2 * b + 1 : 2 * b + 2, :] = inv
+        for k in range(4):
+            values = unpack_quarter(residual[4 * b + k])
+            centred = (values - mean) * inv * quarter_mask(span, marks[6])
+            put_quarter(out, 4 * b + k, centred)
+            out[4 * b + k, 80:88, :] = jnp.zeros((8, 128), jnp.float32)
+            for row, value in ((80, mean), (82, inv)):
+                out[4 * b + k, row : row + 1, :] = value[:, :128]
+                out[4 * b + k, row + 1 : row + 2, 0:32] = value[:, 128:]
+
+
+def centred_of(marks, residual, stats, b, k):
+    values = unpack_quarter(residual[4 * b + k])
+    mean, inv = stats[2 * b : 2 * b + 1, :], stats[2 * b + 1 : 2 * b + 2, :]
+    return (values - mean) * inv * quarter_mask(span_of_item(marks, b), marks[6])
+
+
+def norm_sums_kernel(marks, grad, residual, stats, gain, sums):
+    sums[...] = jnp.zeros_like(sums)
+    for b in range(2):
+        for k in range(4):
+            centred = centred_of(marks, residual, stats, b, k)
+            values = unpack_quarter(grad[4 * b + k])
+            scaled = values * gain[...]
+            sums[3 * b : 3 * b + 1, :] += column_sum(scaled)
+            sums[3 * b + 1 : 3 * b + 2, :] += column_sum(scaled * centred)
+            sums[3 * b + 2 : 3 * b + 3, :] += column_sum(values * centred)
+
+
+def sum_in_order(pieces, t):
+    total = None
+    for part in range(4):
+        j = lax.rem(part - t + 4, 4)
+        value = jnp.where(
+            j < 2,
+            jnp.where(j == 0, pieces[0][...], pieces[1][...]),
+            jnp.where(j == 2, pieces[2][...], pieces[3][...]),
+        )
+        total = value if total is None else total + value
+    return total
+
+
+def norm_back_kernel(marks, *refs):
+    grad, residual, stats, gain, base = refs[:5]
+    pieces, out, grad_gain = refs[5:9], refs[9], refs[10]
+    total = sum_in_order(pieces, marks[6])
+    grad_gain[...] = jnp.zeros_like(grad_gain)
+    grad_gain[0:1, :] = total[2:3, :] + total[5:6, :]
+    for b in range(2):
+        span = span_of_item(marks, b)
+        count = (span * 160).astype(jnp.float32)
+        first = group_rows(total[3 * b : 3 * b + 1, :]) / count
+        second = group_rows(total[3 * b + 1 : 3 * b + 2, :]) / count
+        inv = stats[2 * b + 1 : 2 * b + 2, :]
+        for k in range(4):
+            centred = centred_of(marks, residual, stats, b, k)
+            scaled = unpack_quarter(grad[4 * b + k]) * gain[...]
+            values = inv * quarter_mask(span, marks[6]) * (scaled - first - centred * second)
+            put_quarter(out, 4 * b + k, values + unpack_quarter(base[4 * b + k]))
+
+
+def input_sums_kernel(marks, source, gain, stats, *refs):
+    pieces, out, sums = refs[:4], refs[4], refs[5]
+    at = pl.multiple_of(marks[6] * 80, 8)
+    sums[...] = jnp.zeros_like(sums)
+    for b in range(2):
+        span = span_of_item(marks, b)
+        mine = marks[4] ^ b
+        mean, inv = stats[mine, 0:1, :], stats[mine, 1:2, :]
+        for k in range(4):
+            place = 4 * b + k
+            values = unpack_quarter(source[place, pl.ds(at, 80), :])
+            centred = (values - mean) * inv * quarter_mask(span, marks[6])
+            norm = centred * gain[...]
+            gate = jax.nn.sigmoid(norm)
+            packed = (pieces[0][place] + pieces[1][place]) + (pieces[2][place] + pieces[3][place])
+            grad = unpack_quarter(packed) * gate * (1.0 + norm * (1.0 - gate))
+            put_quarter(out, place, grad)
+            scaled = grad * gain[...]
+            sums[3 * b : 3 * b + 1, :] += column_sum(scaled)
+            sums[3 * b + 1 : 3 * b + 2, :] += column_sum(scaled * centred)
+            sums[3 * b + 2 : 3 * b + 3, :] += column_sum(grad * centred)
+
+
+def input_back_kernel(marks, grad, source, gain, stats, base, extra, *refs):
+    pieces, out, grad_gain = refs[:4], refs[4], refs[5]
+    at = pl.multiple_of(marks[6] * 80, 8)
+    total = sum_in_order(pieces, marks[6])
+    grad_gain[...] = jnp.zeros_like(grad_gain)
+    grad_gain[0:1, :] = total[2:3, :] + total[5:6, :]
+    for b in range(2):
+        span = span_of_item(marks, b)
+        count = (span * 160).astype(jnp.float32)
+        first = group_rows(total[3 * b : 3 * b + 1, :]) / count
+        second = group_rows(total[3 * b + 1 : 3 * b + 2, :]) / count
+        mine = marks[4] ^ b
+        mean, inv = stats[mine, 0:1, :], stats[mine, 1:2, :]
+        for k in range(4):
+            place = 4 * b + k
+            keep = quarter_mask(span, marks[6])
+            centred = (unpack_quarter(source[place, pl.ds(at, 80), :]) - mean) * inv * keep
+            scaled = unpack_quarter(grad[place]) * gain[...]
+            values = inv * keep * (scaled - first - centred * second)
+            put_quarter(out, place, values + unpack_quarter(base[place]))
+            out[place, 80:88, :] = extra[place]
 
 
 def run_kernel(body, marks, inputs, outs, scratch, flops):
@@ -942,7 +1251,7 @@
 
 def weight_kernel(plan, *refs):
     count = 1 + max(which for block in plan for _, _, which in block)
-    lefts, right, out = refs[:count], refs[count], refs[count + 1]
+    lefts, right, out = refs[:count], refs[count], refs[-1]
     tokens = right.shape[0]
     for number, block in enumerate(plan):
 
@@ -963,23 +1272,30 @@
                     out[m : m + 256, begin : begin + columns] = part
 
 
-def weight_grads(plan, lefts, right):
+def weight_grads(plan, lefts, right, first=0, blocks=None, into=None):
     tokens = right.shape[0]
-    blocks = len(plan)
+    blocks = blocks or len(plan)
+    in_specs = [pl.BlockSpec((tokens, 1280), lambda i: (0, 0))] * len(lefts)
+    in_specs.append(pl.BlockSpec((tokens, 1280), lambda i: (0, i)))
+    inputs, alias = (*lefts, right), {}
+    if into is not None:
+        in_specs.append(pl.BlockSpec(memory_space=pl.ANY))
+        alias = {len(inputs): 0}
+        inputs = (*inputs, into)
     return pl.pallas_call(
         functools.partial(weight_kernel, plan),
         out_shape=jax.ShapeDtypeStruct((1280, 1280 * blocks), jnp.float32),
-        grid=(blocks,),
-        in_specs=[pl.BlockSpec((tokens, 1280), lambda i: (0, 0))] * len(lefts)
-        + [pl.BlockSpec((tokens, 1280), lambda i: (0, i))],
-        out_specs=pl.BlockSpec((1280, 1280), lambda i: (0, i)),
+        grid=(len(plan),),
+        in_specs=in_specs,
+        out_specs=pl.BlockSpec((1280, 1280), lambda i: (0, i + first)),
+        input_output_aliases=alias,
         compiler_params=pltpu.CompilerParams(vmem_limit_bytes=48 * 1024 * 1024),
         cost_estimate=pl.CostEstimate(
-            flops=6 * tokens * 1280 * 1280 * blocks,
-            bytes_accessed=7 * 1024 * 1024 * blocks,
+            flops=6 * tokens * 1280 * 1280 * len(plan),
+            bytes_accessed=7 * 1024 * 1024 * len(plan),
             transcendentals=0,
         ),
-    )(*lefts, right)
+    )(*inputs)
 
 
 def after(values, *events):
@@ -988,6 +1304,10 @@
 
 def together(*values):
     return lax.optimization_barrier(values)
+
+
+def small(body, marks, inputs, outs, scratch=()):
+    return run_kernel(body, marks, inputs, outs, scratch, 4 * 1024 * 1024)
 
 
 CONV_FLOPS = 6 * 2048 * 1440 * 320
@@ -999,8 +1319,13 @@
         first_kernel,
         marks,
         (source, gain, tau, weight),
-        [(4, 256, 320), (4, 256, 320), (2, IMAGE_ROWS, 160), (2, 8, 160)],
-        [((IMAGE_ROWS, 480), f32), ((1440, 320), b16), ((1440, 320), b16)],
+        [(4, 320, 256), (4, 320, 256), (2, IMAGE_ROWS, 160), (2, 8, 160)],
+        [
+            ((IMAGE_ROWS, 480), f32),
+            ((1440, 320), b16),
+            ((1440, 320), b16),
+            ((4, 256, 160), f32),
+        ],
         CONV_FLOPS,
     )
 
@@ -1011,7 +1336,7 @@
         second_kernel,
         marks,
         (*strips, gain, weight),
-        [(8, 64, 160)] * 4 + [(2, IMAGE_ROWS, 320), (2, 8, 320)],
+        [(8, 80, 128)] * 4 + [(2, IMAGE_ROWS, 320), (2, 8, 320)],
         [
             ((IMAGE_ROWS, 960), f32),
             ((2880, 160), b16),
@@ -1028,7 +1353,7 @@
         second_back_kernel,
         marks,
         (*quarters, weight),
-        [(4, 256, 320), (4, 256, 320), (2, IMAGE_ROWS, 160)],
+        [(4, 320, 256), (4, 320, 256), (2, IMAGE_ROWS, 160)],
         [((IMAGE_ROWS, 480), f32), ((1440, 320), b16), ((1440, 320), b16)],
         CONV_FLOPS,
     )
@@ -1040,7 +1365,7 @@
         first_back_kernel,
         marks,
         (*grads, *strips, gain, stats, weight),
-        [(8, 64, 160)] * 4 + [(2, IMAGE_ROWS, 320), (2, 320), (1, 320)],
+        [(8, 80, 128)] * 4 + [(2, IMAGE_ROWS, 320), (2, 320), (1, 320)],
         [
             ((IMAGE_ROWS, 960), f32),
             ((2880, 160), b16),
@@ -1053,24 +1378,13 @@
     )
 
 
-def first_conv_weight(marks, image, grad):
+def conv_weight(marks, image, cells, sign):
     return run_kernel(
-        first_weight_kernel,
+        functools.partial(conv_weight_kernel, sign),
         marks,
-        (image, grad),
+        (image, cells),
         [(9, 160, 320)],
         [((IMAGE_ROWS, 480), jnp.float32)],
-        CONV_FLOPS,
-    )[0]
-
-
-def second_conv_weight(marks, image, grad):
-    return run_kernel(
-        second_weight_kernel,
-        marks,
-        (image, grad),
-        [(9, 320, 160)],
-        [((IMAGE_ROWS, 480), jnp.float32), ((320, 480), jnp.float32)],
         CONV_FLOPS,
     )[0]
 
@@ -1133,10 +1447,6 @@
 
 def scatter_plane(block):
     return lax.psum_scatter(block, IH, scatter_dimension=0, tiled=True)
-
-
-def strip_sums(values):
-    return jnp.sum(values, axis=(1, 2))
 
 
 def grid_cells(bucket):
@@ -1183,36 +1493,17 @@
     own_span = grid_cells(bucket[0])
     slot = jnp.arange(256, dtype=jnp.int32)
     own_valid = (slot < own_span).astype(jnp.float32)[:, None]
-    source = s_to_q(hidden[0] * own_valid).reshape(8, 256, width)
     both = jnp.stack([bucket[0], timestep[0]]).astype(jnp.float32)
     both_other = swap(both)
-    pair = jnp.where(item == 0, jnp.stack([both, both_other]), jnp.stack([both_other, both]))
     times = jnp.stack([both[1], both_other[1]])
-    strip_rows, strip_width = grid_shape(pair[:, 0].astype(jnp.int32))
-    spans = strip_rows * strip_width
+    other_rows, other_width = grid_shape(both_other[0].astype(jnp.int32))
+    own_rows, own_width = grid_shape(bucket[0])
     marks = jnp.stack(
-        [
-            own_span,
-            pick(strip_width, item),
-            pick(spans, 1 - item),
-            pick(strip_width, 1 - item),
-            item,
-            h,
-            t,
-        ]
+        [own_span, own_width, other_rows * other_width, other_width, item, h, t]
     ).astype(jnp.int32)
-    counts = (4 * spans * 40).astype(jnp.float32)[:, None]
-    quarter_slot = t * 64 + jnp.arange(64, dtype=jnp.int32)
-    q_valid = (quarter_slot[None, :] < spans[:, None]).astype(jnp.float32)[:, None, :, None]
-    relative_slot = jnp.mod(t * 64 + slot, 256)
-    key_valid = jnp.tile(relative_slot < own_span, 4)
-
-    def spread(stat):
-        return stat[:, None, None, :]
-
-    def quarter(values):
-        return lax.dynamic_slice_in_dim(values, t * 64, 64, 2)
-
+
+    (source,) = small(pack_kernel, marks, (hidden[0] * own_valid,), [(8, 320, 128)])
+    source = plane_exchange(source)
     gains = jnp.stack([gain_self, gain_cross, gain_ff], axis=1)
     attn_full = gather_plane(
         jnp.concatenate(
@@ -1242,71 +1533,95 @@
     features = jax.nn.silu(time_features(times, channels))
     own_features = lax.dynamic_slice_in_dim(features, block * width, width, 1)
     tau = mm(own_features, time_weight, 1, 0)
+    second_weight = conv_second.transpose(0, 1, 3, 2).reshape(9 * width, wide)
     own_one, other_one, image_one, stats_one = first_conv(
         marks, source, gain_in[None, :], tau, conv_first.reshape(9 * width, wide)
     )
-    strips_one = plane_sum(own_one, other_one)
-
-    third = z_order(after(third_pieces, own_one), 1)
-    gain_attn_full = third[160, :, :320].reshape(1, channels)
-    third = third[:160].reshape(160, 4, 3, 320).transpose(0, 2, 1, 3).reshape(160, 3840)
+    own_one, other_one, *third_pieces = together(own_one, other_one, *third_pieces)
+    own_one = own_one + swap(other_one)
+    strips_one, part = plane_sum(own_one)
+    third, gain_attn_full = small(
+        third_kernel, marks, after(third_pieces, part), [(160, 3840), (1, channels)]
+    )
     third_full = gather_plane(third)
     proj_in_full = third_full[:, :1280]
     query_cross_full = third_full[:, 1280:2560]
     out_cross_full = third_full[:, 2560:]
-
-    ff_full = gather_plane(jnp.concatenate([ff_in.reshape(160, 2560), ff_out.T], axis=1))
+    ff_block = jnp.concatenate([ff_in.reshape(160, 2560), ff_out.T], axis=1)
+    ff_full = gather_plane(after(ff_block, part))
     ff_in_full = ff_full[:, :2560]
     ff_out_full = ff_full[:, 2560:]
-
     cot = after(cotangent[0] * own_valid, own_one)
-    cot_relative = lax.dynamic_slice_in_dim(jnp.concatenate([cot, cot], axis=0), t * 64, 256, 0)
-    cot_pieces = z_exchange(rows_of(cot_relative))
-    grad_ff_part = mm(cot_relative, proj_out_full, 1, 1)
-    grad_after_ff = z_collect(rows_of(grad_ff_part))
-
-    *strips_one, grad_after_ff = together(*strips_one, grad_after_ff)
+    grad_ff_part = mm(cot, proj_out_full, 1, 1)
+    cot_pieces = z_all(jnp.concatenate([grad_ff_part, cot], axis=1).reshape(4, 64, channels + wide))
+    *strips_one, cot_pieces = together(*strips_one, cot_pieces)
+
     *conv_two, image_two, stats_two = second_conv(
-        marks, strips_one, gain_mid[None, :], conv_second.reshape(9 * wide, width)
-    )
-    conv_two_sum = z_collect(conv_two)
-
-    text_here = after(text_states[0], conv_two[0])
+        marks, strips_one, gain_mid[None, :], second_weight
+    )
+    conv_two_pieces = z_received(conv_two)
+
+    event = conv_two[0]
+    grad_after_ff, cot_packed = small(
+        cotangent_kernel,
+        marks,
+        (after(cot_pieces, event),),
+        [(64, channels), (8, 80, 128)],
+        [((64, channels), jnp.float32)],
+    )
+    cot_q = plane_exchange(cot_packed)
+    text_here = after(text_states[0], event)
     text_own = lax.dynamic_slice_in_dim(text_here, block * 256, 256, 1)
     text_other = swap(lax.dynamic_slice_in_dim(text_here, ((1 - item) * 4 + h) * 256, 256, 1))
     text_weight = jnp.concatenate([key_cross, value_cross], axis=1)
     text_part = mm(text_own, text_weight, 1, 0) + swap(mm(text_other, text_weight, 1, 0))
-    text_sum = h_sum(text_part)
-    cot_s = z_order(after(cot_pieces, conv_two[0]), 1)
-    cot_q = s_to_q(cot_s.reshape(64, channels))
-    residual_q = quarter(source.reshape(2, 4, 256, width)) + conv_two_sum.reshape(2, 4, 64, width)
-
-    sums = z_sum(jnp.stack([strip_sums(residual_q), strip_sums(residual_q * residual_q)]))
-    mean_three = group_sum(sums[0]) / counts
-    var_three = group_sum(sums[1]) / counts - mean_three * mean_three
-    inv_three = lax.rsqrt(var_three + norm_eps)
-    centred_three = (residual_q - spread(mean_three)) * spread(inv_three) * q_valid
-    norm_three = q_to_s(centred_three) * gain_attn_full
+
+    residual_q, sums = small(
+        residual_kernel, marks, (source, *conv_two_pieces), [(8, 80, 128), (8, width)]
+    )
+    centred_three, stats_three = small(
+        norm_kernel, marks, (residual_q, *z_pieces(sums)), [(8, 88, 128), (8, width)]
+    )
+    norm_three, residual_s = small(
+        unpack_norm_kernel,
+        marks,
+        (plane_exchange(centred_three), gain_attn_full),
+        [(64, channels), (64, channels)],
+    )
     projected = mm(norm_three, proj_in_full, 1, 1)
 
     normed_self, centred_self, inv_self = layer_forward(projected, gain_self_full)
-    normed_self_all = jnp.concatenate(z_pieces(normed_self), axis=0)
+    normed_pieces = z_pieces(normed_self)
+    text_sum = h_sum(after(text_part, normed_self))
+    *normed_pieces, text_sum, cot_q = together(*normed_pieces, text_sum, cot_q)
+    normed_self_all = jnp.concatenate(normed_pieces, axis=0)
     qkv = mm(normed_self_all, qkv_full, 1, 0)
-    queries = qkv[:, :wide]
-    kv_pieces = [qkv[:, wide:]] + [flip(qkv[:, wide:], j) for j in (1, 2, 3)]
-    text_kv = z_order(z_pieces(after(text_sum, qkv)), 1)
-    keys_text = text_kv[:, :, :320].reshape(-1, channels)
-    values_text = text_kv[:, :, 320:].reshape(-1, channels)
-    grad_after_ff_all = jnp.concatenate(z_pieces(after(grad_after_ff, qkv)), axis=0)
-
-    kv_all = jnp.concatenate(kv_pieces, axis=0)
-    keys_all, values_all = kv_all[:, :wide], kv_all[:, wide:]
-    attn_self, weights_self = soft_attend(queries, keys_all, values_all, key_valid, 5)
+    own_kv = qkv[:, wide:]
+    kv_pieces = [own_kv] + [flip(own_kv, j) for j in (1, 2, 3)]
+    text_sum, grad_here = after((text_sum, grad_after_ff), own_kv)
+    side_pieces = z_spread(jnp.concatenate([grad_here, folded(text_sum)], axis=0))
+    *kv_pieces, side_pieces = together(*kv_pieces, side_pieces)
+    attn_self, totals_self = small(
+        attend_kernel,
+        marks,
+        (qkv, *kv_pieces),
+        [(256, wide), (8, 256)],
+        [((1024, 256), jnp.float32)],
+    )
     self_part = mm(attn_self, out_self_full, 1, 1)
-    self_sum = z_collect(rows_of(self_part))
-    grad_ff_act = mm(after(grad_after_ff_all, self_part), ff_out_full, 1, 0)
-    residual_s = q_to_s(after(residual_q, self_part))
-    self_sum, grad_ff_act = together(self_sum, grad_ff_act)
+    self_pieces = z_received(rows_of(self_part))
+    self_sum = total_of(self_pieces)
+    event = self_pieces[1]
+    grad_after_ff_all, keys_text, values_text = small(
+        text_kernel,
+        marks,
+        (after(side_pieces, event),),
+        [(256, channels), (77, channels), (77, channels)],
+    )
+    grad_ff_act = mm(grad_after_ff_all, ff_out_full, 1, 0)
+    self_sum, grad_ff_act, keys_text, values_text = together(
+        self_sum, grad_ff_act, keys_text, values_text
+    )
     after_self = projected + self_sum
 
     normed_cross, centred_cross, inv_cross = layer_forward(after_self, gain_cross_full)
@@ -1326,15 +1641,17 @@
     grad_gate = grad_ff_act * value_half * slope
     grad_hidden_ff = jnp.concatenate([grad_value, grad_gate], axis=1)
     grad_normed_part = mm(grad_hidden_ff, ff_in_full, 1, 1)
-    grad_normed_ff = z_collect(rows_of(grad_normed_part))
-    ff_right = after(jnp.concatenate([grad_hidden_ff, ff_act], axis=1), grad_normed_part)
+    normed_pieces = z_received(rows_of(grad_normed_part))
+    grad_normed_ff = total_of(normed_pieces)
+    ff_right = jnp.concatenate(after([grad_hidden_ff, ff_act], normed_pieces[1]), axis=1)
     ff_grads = weight_grads(
         (((0, 1280, 0),), ((0, 1280, 0),), ((0, 1280, 1),)),
         (normed_ff_all, grad_after_ff_all),
         ff_right,
+        0,
+        5,
     )
     grad_normed_ff, ff_grads = together(grad_normed_ff, ff_grads)
-    ff_grads = scatter_plane(ff_grads)
 
     back_ff, grad_gain_ff = layer_grad(grad_normed_ff, centred_ff, inv_ff, gain_ff_full)
     grad_after_cross = grad_after_ff + back_ff
@@ -1348,42 +1665,57 @@
     )
     grad_after_self = grad_after_cross + back_cross
     grad_pieces = z_pieces(grad_after_self)
-    cross_right = after(
-        jnp.concatenate([grad_queries_cross, attn_cross], axis=1), grad_after_self
+    cross_right = after((grad_queries_cross, attn_cross), grad_pieces[1])
+    cross_right = jnp.concatenate(
+        [side[:, wide * k : wide * k + wide] for k in range(4) for side in cross_right], axis=1
     )
     cross_grads = weight_grads(
-        (((0, 1280, 0),), ((0, 1280, 1),)), (normed_cross, grad_after_cross), cross_right
-    )
-    *grad_pieces, cross_grads = together(*grad_pieces, cross_grads)
-    cross_grads = scatter_plane(cross_grads)
-    text_grads = jnp.concatenate(
-        [grad_keys_text.reshape(-1, 4, wide), grad_values_text.reshape(-1, 4, wide)], axis=2
-    )
+        (((0, 320, 0), (320, 320, 1), (640, 320, 0), (960, 320, 1)),) * 2,
+        (normed_cross, grad_after_cross),
+        cross_right,
+        3,
+        5,
+        ff_grads,
+    )
+    ff_here, grad_keys_text, grad_values_text = after(
+        (ff_act, grad_keys_text, grad_values_text), grad_pieces[1]
+    )
+    out_part = mm(ff_here, ff_out_full, 1, 1)
+    (side_grads,) = small(
+        text_grad_kernel,
+        marks,
+        (out_part, grad_keys_text, grad_values_text),
+        [(4, 104, channels)],
+    )
+    *grad_pieces, cross_grads, side_grads = together(*grad_pieces, cross_grads, side_grads)
+    side_grads = z_all(side_grads)
+    ff_grads = scatter_plane(cross_grads)
+    ff_grads, cross_grads = ff_grads[:, :3840], ff_grads[:, 3840:]
 
     grad_after_self_all = jnp.concatenate(grad_pieces, axis=0)
     grad_attn_self = mm(grad_after_self_all, out_self_full, 1, 0)
-    grad_queries, grad_keys_all, grad_values_all = soft_back(
-        queries, keys_all, values_all, 5, weights_self, attn_self, grad_attn_self
-    )
-    grad_kv_all = jnp.concatenate([grad_keys_all, grad_values_all], axis=1)
-    grad_kv = h_collect([grad_kv_all[256 * j : 256 * j + 256] for j in range(4)])
-    text_grads = after(text_grads, grad_kv_all)
-    text_grads = z_collect([pick(text_grads, lax.rem(t + j, 4), 1) for j in range(4)])
-    out_part = mm(after(ff_act, grad_kv_all), ff_out_full, 1, 1)
-    grad_kv, out_part = together(grad_kv, out_part)
-
+    grad_queries, *kv_pieces = small(
+        attend_back_kernel,
+        marks,
+        (qkv, *kv_pieces, totals_self, attn_self, grad_attn_self),
+        [(256, wide)] + [(256, 2 * wide)] * 4,
+    )
+    kv_pieces = kv_pieces[:1] + [flip(kv_pieces[j], j) for j in (1, 2, 3)]
+    grad_kv = total_of(kv_pieces)
     grad_qkv = jnp.concatenate([grad_queries, grad_kv], axis=1)
     grad_normed_part = mm(grad_qkv, qkv_full, 1, 1)
-    grad_normed_self = z_collect(rows_of(grad_normed_part))
-    text_grads = h_sum(after(text_grads, grad_normed_part))
-
+    normed_pieces = z_received(rows_of(grad_normed_part))
+    grad_normed_self = total_of(normed_pieces)
+    grad_normed_self, side_grads = together(grad_normed_self, side_grads)
     back_self, grad_gain_self = layer_grad(grad_normed_self, centred_self, inv_self, gain_self_full)
     grad_projected = grad_after_self + back_self
     grad_norm_three = mm(grad_projected, proj_in_full, 1, 0)
 
-    both_grads = s_to_q(
-        jnp.concatenate([grad_norm_three * gain_attn_full, grad_norm_three], axis=0)
-    )
+    (grad_three,) = small(pack_kernel, marks, (grad_norm_three,), [(8, 80, 128)])
+    grad_three_q = plane_exchange(grad_three)
+    side_grads = jnp.sum(after(side_grads, grad_three), axis=0)
+    out_sum, text_grads = side_grads[:64], side_grads[64:]
+    text_grads = text_grads + flip(text_grads, 1)
     attn_right = jnp.concatenate(
         [
             jnp.concatenate([grad_qkv, attn_self], axis=1),
@@ -1398,50 +1730,48 @@
             grad_after_self_all,
             jnp.pad(grad_projected, ((0, 192), (0, 0))),
         ),
-        after(attn_right, grad_norm_three),
-    )
-    both_grads, attn_grads = together(both_grads, attn_grads)
+        after(attn_right, grad_three),
+    )
+    grad_three_q, attn_grads, text_grads = together(grad_three_q, attn_grads, text_grads)
     attn_grads = scatter_plane(attn_grads)
-
-    scaled_three, grad_three = both_grads[:, :, :64] * q_valid, both_grads[:, :, 64:]
-    sums = z_sum(
-        jnp.stack(
-            [
-                strip_sums(scaled_three),
-                strip_sums(scaled_three * centred_three),
-                strip_sums(grad_three * centred_three),
-            ]
-        )
-    )
-    grad_gain_three = jnp.sum(sums[2], axis=0)
-    grad_residual_q = cot_q + spread(inv_three) * q_valid * (
-        scaled_three
-        - spread(group_sum(sums[0]) / counts)
-        - centred_three * spread(group_sum(sums[1]) / counts)
-    )
-
-    own_two, other_two, image_back = second_conv_back(
+    gain_block = lax.dynamic_slice_in_dim(gain_attn_full, block * width, width, 1)
+    (sums,) = small(
+        norm_sums_kernel, marks, (grad_three_q, residual_q, stats_three, gain_block), [(8, width)]
+    )
+    grad_residual_q, grad_gain_three = small(
+        norm_back_kernel,
         marks,
-        z_pieces(grad_residual_q.reshape(8, 64, width)),
-        conv_second.transpose(0, 1, 3, 2).reshape(9 * width, wide),
-    )
-    grad_act_two = plane_sum(own_two, other_two)
-    grad_conv_second = second_conv_weight(marks, image_two, after(image_back, own_two)).reshape(
-        3, 3, wide, width
-    )
-    after_ff = after_cross + z_collect(rows_of(after(out_part, own_two)))
-    after_ff_all = jnp.concatenate(z_pieces(after_ff), axis=0)
-    residual_cut = jnp.moveaxis(after(residual_s, own_two).reshape(64, 4, wide), 1, 0)
-    residual_all = jnp.concatenate(
-        z_exchange([pick(residual_cut, lax.rem(t + j, 4)) for j in range(4)]), axis=0
-    )
-    output = residual_all + mm(after_ff_all, proj_out_full, 1, 0)
-    output = jnp.concatenate([output, output], axis=0)
-    output = lax.dynamic_slice_in_dim(output, lax.rem(4 - t, 4) * 64, 256, 0) * own_valid
-    grad_proj_out = scatter_plane(mm(after_ff_all, cot_relative, 0, 0))
-    grad_text_weight = mm(text_own, text_grads, 0, 0) + mm(text_other, swap(text_grads), 0, 0)
-    gain_sums = z_sum(after(jnp.stack([grad_gain_self, grad_gain_cross, grad_gain_ff]), own_two))
-    *grad_act_two, grad_conv_second, output = together(*grad_act_two, grad_conv_second, output)
+        (grad_three_q, residual_q, stats_three, gain_block, cot_q, *z_pieces(sums)),
+        [(8, 80, 128), (8, width)],
+    )
+
+    residual_pieces = z_pieces(grad_residual_q)
+    text_grads = after(text_grads, grad_residual_q)
+    text_grads = text_grads + flip(text_grads, 2)
+    *residual_pieces, text_grads = together(*residual_pieces, text_grads)
+    own_two, other_two, image_back = second_conv_back(marks, residual_pieces, second_weight)
+    own_two = own_two + swap(other_two)
+    grad_act_two, part = plane_sum(own_two)
+    side = jnp.concatenate(
+        [
+            jnp.broadcast_to((after_cross + out_sum)[None], (4, 64, channels)),
+            jnp.moveaxis(residual_s.reshape(64, 4, wide), 1, 0),
+        ],
+        axis=2,
+    )
+    gain_rows = jnp.stack([grad_gain_self, grad_gain_cross, grad_gain_ff])
+    gain_rows = jnp.broadcast_to(jnp.pad(gain_rows, ((0, 5), (0, wide)))[None], (4, 8, 1600))
+    side = z_all(after(jnp.concatenate([side, gain_rows], axis=1), own_two))
+    side_here = after(side, part)
+    after_ff_all = side_here[:, :64, :channels].reshape(256, channels)
+    residual_all = side_here[:, :64, channels:].reshape(256, wide)
+    gain_sums = jnp.sum(side_here[:, 64:67, :channels], axis=0)
+    cross_cut = after(cross_grads, part)
+    cross_cut = jnp.stack([cross_cut[:, 640 * k : 640 * k + 640] for k in range(4)])
+    *grad_act_two, after_ff_all, gain_sums, residual_all, cross_cut = together(
+        *grad_act_two, after_ff_all, gain_sums, residual_all, cross_cut
+    )
+    cross_shares = z_all(cross_cut)
 
     *grad_act_one, image_grad, grad_tau, grad_gain_mid = first_conv_back(
         marks,
@@ -1449,91 +1779,103 @@
         strips_one,
         gain_mid[None, :],
         stats_two,
-        conv_first.transpose(0, 1, 3, 2).reshape(9 * wide, width),
-    )
-    grad_act_one_sum = z_collect(grad_act_one)
-    grad_conv_first = first_conv_weight(marks, image_one, after(image_grad, grad_act_one[0]))
-    grad_act_one_sum, grad_conv_first = together(grad_act_one_sum, grad_conv_first)
+        conv_first.reshape(9 * width, wide),
+    )
+    grad_act_pieces = z_received(grad_act_one)
+    image_grad, text_grads = after((image_grad, text_grads), grad_act_pieces[1])
+    text_other_grads = swap(text_grads)
+    grad_conv_first = conv_weight(marks, image_one, image_grad, 1)
+    cross_shares, after_ff_here = after((cross_shares, after_ff_all), grad_act_pieces[1])
+    cross_shares = jnp.sum(cross_shares, axis=0)
+    grad_proj_out = mm(after_ff_here, cot, 0, 0)
+    *grad_act_pieces, grad_conv_first, cross_shares, grad_proj_out, text_other_grads = together(
+        *grad_act_pieces, grad_conv_first, cross_shares, grad_proj_out, text_other_grads
+    )
+    text_grads, text_other_grads = unfolded(text_grads), unfolded(text_other_grads)
+    grad_proj_out = grad_proj_out.reshape(2, 4, width, wide)
+    grad_proj_own = pick(grad_proj_out, item) + swap(pick(grad_proj_out, 1 - item))
     grad_conv_first = grad_conv_first.reshape(3, 3, width, wide)
-    grad_time_weight = mm(own_features, grad_tau, 0, 0)
-
-    grad_act_one_sum = grad_act_one_sum.reshape(2, 4, 64, width)
-    stats_one = jnp.where(item == 0, stats_one, stats_one[::-1])
-    mean_one, inv_one = stats_one[:, 0], stats_one[:, 1]
-    centred_one_q = (quarter(source.reshape(2, 4, 256, width)) - spread(mean_one)) * (
-        spread(inv_one) * q_valid
-    )
-    norm_one_q = centred_one_q * gain_in
-    gate_one = jax.nn.sigmoid(norm_one_q)
-    grad_norm_one = grad_act_one_sum * gate_one * (1.0 + norm_one_q * (1.0 - gate_one))
-    scaled_one = grad_norm_one * gain_in
-    sums = z_sum(
-        jnp.stack(
-            [
-                strip_sums(scaled_one),
-                strip_sums(scaled_one * centred_one_q),
-                strip_sums(grad_norm_one * centred_one_q),
-            ]
-        )
-    )
-    grad_gain_in = jnp.sum(sums[2], axis=0)
-    grad_hidden = grad_residual_q + spread(inv_one) * q_valid * (
-        scaled_one
-        - spread(group_sum(sums[0]) / counts)
-        - centred_one_q * spread(group_sum(sums[1]) / counts)
-    )
     extra = jnp.concatenate(
         [
-            jnp.broadcast_to(grad_gain_three, (8, 1, width)),
+            jnp.broadcast_to(grad_gain_three[0], (8, 1, width)),
             jnp.moveaxis(gain_sums.reshape(3, 8, width), 1, 0),
-            jnp.zeros((8, 4, width), jnp.float32),
         ],
         axis=1,
     )
-    moved = jnp.concatenate([grad_hidden.reshape(8, 64, width), extra], axis=1)
-    moved = lax.all_to_all(moved, IH, 0, 0)
-    grad_hidden = jnp.moveaxis(moved[:, :64], 0, 1).reshape(64, channels)
-    grad_hidden = z_order(z_pieces(grad_hidden), 0).reshape(256, channels)
-    grad_gain_attn = lax.dynamic_slice_in_dim(
-        moved[:, 64].reshape(channels), t * wide, wide, 0
-    )
-    gain_sums = jnp.sum(moved[:, 65:68], axis=0)
-
-    grad_query_cross, grad_out_cross = z_shares(cross_grads, 2)
-    (grad_proj_in,) = z_shares(attn_grads[:, 1280:], 1)
+    extra = jnp.concatenate(
+        [extra[:, :, :128], jnp.pad(extra[:, :, 128:], ((0, 0), (0, 0), (0, 96)))], axis=1
+    )
+    grad_input_q, sums = small(
+        input_sums_kernel,
+        marks,
+        (source, gain_in[None, :], stats_one, *grad_act_pieces),
+        [(8, 80, 128), (8, width)],
+    )
+    moved, grad_gain_in = small(
+        input_back_kernel,
+        marks,
+        (
+            grad_input_q,
+            source,
+            gain_in[None, :],
+            stats_one,
+            grad_residual_q,
+            extra,
+            *z_pieces(sums),
+        ),
+        [(8, 88, 128), (8, width)],
+    )
+    received = plane_exchange(moved)
+    grad_proj_own, image_back = after((grad_proj_own, image_back), moved)
+    grad_conv_second = conv_weight(marks, image_back, image_two, -1)
+    grad_proj_out = h_collect([pick(grad_proj_own, h ^ j) for j in range(4)])
+    received, grad_conv_second, grad_proj_out = together(
+        received, grad_conv_second, grad_proj_out
+    )
+    grad_conv_second = grad_conv_second.reshape(3, 3, width, wide).transpose(0, 1, 3, 2)
+    attn_grads = after(attn_grads, received)
+    proj_cut = attn_grads[:, 1280:].reshape(width, 4, wide)
+    proj_pieces = z_received([pick(proj_cut, lax.rem(t + j, 4), 1) for j in range(4)])
+    (grad_hidden,) = small(unpack_kernel, marks, (received,), [(64, channels)])
+    hidden_pieces = z_pieces(grad_hidden)
+    text_own, text_other, own_features, after_ff_all = after(
+        (text_own, text_other, own_features, after_ff_all), hidden_pieces[1]
+    )
+    output = residual_all + mm(after_ff_all, proj_out_full, 1, 0)
+    output = output * own_valid
+    grad_text_weight = mm(text_own, text_grads, 0, 0) + mm(text_other, text_other_grads, 0, 0)
+    grad_time_weight = mm(own_features, grad_tau, 0, 0)
+    (grad_hidden,) = small(rows_kernel, marks, hidden_pieces, [(256, channels)])
+    proj_share = total_of(proj_pieces)
+    extra = jnp.concatenate([received[:, 80:84, :], received[:, 84:88, :32]], axis=2)
+    grad_gain_attn = lax.dynamic_slice_in_dim(extra[:, 0].reshape(channels), t * wide, wide, 0)
+    gain_sums = jnp.sum(extra[:, 1:], axis=0)
 
     return (
         output[None],
         grad_hidden[None],
-        grad_gain_in,
+        grad_gain_in[0],
         grad_conv_first,
         grad_time_weight,
         grad_gain_mid[0],
         grad_conv_second,
         grad_gain_attn,
-        grad_proj_in.T,
+        proj_share.T,
         gain_sums[0],
         attn_grads[:, :320],
         attn_grads[:, 320:640],
         attn_grads[:, 640:960],
         attn_grads[:, 960:1280].T,
         gain_sums[1],
-        grad_query_cross,
+        cross_shares[:, :320],
         grad_text_weight[:, :wide],
         grad_text_weight[:, wide:],
-        grad_out_cross.T,
+        cross_shares[:, 320:].T,
         gain_sums[2],
         ff_grads[:, :2560].reshape(width, 2, channels),
         ff_grads[:, 2560:].T,
         grad_proj_out,
     )
-
-
-def z_shares(columns, count):
-    t = lax.axis_index(T)
-    cut = columns.reshape(columns.shape[0], count, 4, 320)
-    own = z_collect([pick(cut, lax.rem(t + j, 4), 2) for j in range(4)])
-    return [own[:, k] for k in range(count)]
 
 
 def solution(mesh):

time: 1260 us -> 1060 us (0.84)
  waiting for transfers between devices: 476 us -> 356 us
  local copies, waits for them, and re-layouts: 156 us -> 86.3 us
  Pallas kernels: 151 us -> 218 us
  matrix products: 146 us -> 112 us
  starting transfers between devices: 246 us -> 218 us
  other arithmetic: 52.4 us -> 34.9 us
    ppermute x75 -> x45, waiting for transfers between devices: 302 us -> 134 us  [turn(): return lax.ppermute(values, T, [(s, (s + step) % 4) for s in range(4)])]
    ppermute x75 -> x45, starting transfers between devices: 194 us -> 128 us  [turn(): return lax.ppermute(values, T, [(s, (s + step) % 4) for s in range(4)])]
    pallas_call x6 -> x23, Pallas kernels: 122 us -> 184 us  [run_kernel(): pl.pallas_call(body, out_shape=[jax.ShapeDtypeStruct(shape, jnp.float32)...]
    ppermute x24 -> x25, waiting for transfers between devices: 145 us -> 185 us  [flip(): return lax.ppermute(values, H, [(s, s ^ step) for s in range(4)])]
    all_to_all x6 -> x10, starting transfers between devices: 24 us -> 58 us  [the longest x5 30.4 us: plane_exchange(): return lax.all_to_all(packed, IH, 0, 0)]
    dot_general x12 -> x6, matrix products: 36.7 us -> 8.52 us  [ein(): jnp.einsum(form, left, right, precision=high, preferred_element_type=jnp....]
    dynamic_update_slice x39 -> x0, local copies, waits for them, and re-layouts: 23.6 us -> none  [the longest x32 18.8 us: z_order(): lax.dynamic_update_index_in_dim(whole, pieces[j], lax.rem(t + j, 4), axis)]
    reshape x16 -> x2, local copies, waits for them, and re-layouts: 18.4 us -> 0.98 us  [the longest x1 0.69 us: fast_shards(): proj_cut = attn_grads[:, 1280:].reshape(width, 4, wide)]
  transfers between devices with their start and end apart: 126 -> 100, of which waited for: 58 -> 47; matrix products, arithmetic and copies ran while one was open for 22% -> 15% of each run, Pallas kernels for 12% -> 21%
where the time goes in v1:
time: 1060 us; the launch traced here: 1040 us
  waiting for transfers between devices  356 us (34%)
  starting transfers between devices  218 us (21%)
  Pallas kernels  218 us (21%)
  matrix products  112 us (11%)
  local copies, waits for them, and re-layouts  86.3 us (8%)
  other arithmetic  34.9 us (3%)
  between operations  17.8 us (2%)
    ppermute x25, waiting for transfers between devices, flip(): return lax.ppermute(values, H, [(s, s ^ step) for s in range(4)])  185 us
    pallas_call x23, Pallas kernels, run_kernel(): pl.pallas_call(body, out_shape=[jax.ShapeDtypeStruct(shape, jnp.float32)...  184 us
    ppermute x45, waiting for transfers between devices, turn(): return lax.ppermute(values, T, [(s, (s + step) % 4) for s in range(4)])  134 us
    ppermute x45, starting transfers between devices, turn(): return lax.ppermute(values, T, [(s, (s + step) % 4) for s in range(4)])  128 us
    dot_general x23, matrix products, mm(): lax.dot_general(left, right, (((left_dim,), (right_dim,)), ((), ())), pre...  103 us
    pallas_call x3, Pallas kernels, weight_grads(): pl.pallas_call(functools.partial(weight_kernel, plan), out_shape=jax.Shap...  33.7 us
    all_to_all x5, starting transfers between devices, plane_exchange(): return lax.all_to_all(packed, IH, 0, 0)  30.4 us
    ppermute x25, starting transfers between devices, flip(): return lax.ppermute(values, H, [(s, s ^ step) for s in range(4)])  29.8 us
  transfers between devices with their start and end apart: 100, of which 47 were waited for; matrix products, arithmetic and copies ran while one was open for 15% of the time, Pallas kernels for 21%

profile of v1, /device:TPU:0, one launch (start us, length us, event | category | flops | bytes accessed | tf_op | source)
XLA Modules:
  0.0 1042.9 jit_solution(5565867606693466973)
XLA Ops:
  32.0 19.1 %all-to-all-done.source = f32[8,320,128]{2,1,0:T(8,128)S(1)} async-done(((f32[8,320,128]{2,1,0:T(8,128)}), f32[8,320,128]{2,1,0:T(8,128)S(1)}, u32[]{:S(2)}, u32[]{:S(2)}) %all-to-all-start) | async-done | bytes 1310752 | tf_op jit(solution)/shard_map/all_to_all | solution.py:628
  52.2 19.1 %shard_map.426 = (f32[4,320,256]{2,1,0:T(8,128)}, f32[4,320,256]{2,1,0:T(8,128)}, f32[2,1152,160]{2,1,0:T(8,128)}, f32[2,8,160]{2,1,0:T(8,128)}) custom-call(s32[7]{0:T(128)} %stack.68.marks, f32[8,320,128]{2,1,0:T(8,128)} %copy-done.4, f32[1,160]{1,0:T(1,128)} %bitcast.212, f32[2,320]{1,0:T(2,128)} %fusion.94.tau, f32[1440,320]{1,0:T(8,128)} %bitcast.225), custom_call_target="tpu_custom_call" | custom-call | flops 5662310400 | bytes 10485760 | tf_op jit(solution)/shard_map/pallas_call | solution.py:1239
  71.3 15.7 %collective-permute-done.2.refs_2_ = f32[168,960]{1,0:T(8,128)} collective-permute-done((f32[168,960]{1,0:T(8,128)S(1)}, f32[168,960]{1,0:T(8,128)}, u32[]{:S(2)}, u32[]{:S(2)}) %collective-permute-start.2) | collective-permute-done | bytes 645152 | tf_op jit(solution)/shard_map/ppermute | solution.py:573
  132.9 14.4 %collective-permute-done.8.refs_1_.refs_9_ = f32[320,256]{1,0:T(8,128)} collective-permute-done((f32[320,256]{1,0:T(8,128)}, f32[320,256]{1,0:T(8,128)}, u32[]{:S(2)}, u32[]{:S(2)}) %collective-permute-start.8) | collective-permute-done | bytes 327712 | tf_op jit(solution)/shard_map/ppermute | solution.py:569
  148.8 12.6 %collective-permute-done.10.refs_3_.refs_11_ = f32[320,256]{1,0:T(8,128)} collective-permute-done((f32[320,256]{1,0:T(8,128)}, f32[320,256]{1,0:T(8,128)}, u32[]{:S(2)}, u32[]{:S(2)}) %collective-permute-start.10) | collective-permute-done | bytes 327712 | tf_op jit(solution)/shard_map/ppermute | solution.py:569
  168.2 21.4 %shard_map.427 = (f32[8,80,128]{2,1,0:T(8,128)}, f32[8,80,128]{2,1,0:T(8,128)}, f32[8,80,128]{2,1,0:T(8,128)}, f32[8,80,128]{2,1,0:T(8,128)}, f32[2,1152,320]{2,1,0:T(8,128)}, /*index=5*/f32[2,8,320]{2,1,0:T(8,128)}) custom-call(s32[7]{0:T(128)} %stack.68.marks, f32[320,256]{1,0:T(8,128)} %fusion.56.refs_0_.refs_8_, ...), custom_call_target="tpu_custom_call" | custom-call | flops 5662310400 | bytes 10485760 | tf_op jit(solution)/shard_map/pallas_call | solution.py:1239
  202.4 12.2 %collective-permute-done.16.third = f32[8,80,128]{2,1,0:T(8,128)S(1)} collective-permute-done((f32[8,80,128]{2,1,0:T(8,128)}, f32[8,80,128]{2,1,0:T(8,128)S(1)}, u32[]{:S(2)}, u32[]{:S(2)}) %collective-permute-start.16) | collective-permute-done | bytes 327712 | tf_op jit(solution)/shard_map/ppermute | solution.py:573
  234.2 13.3 %all-to-all-start.2 = ((f32[8,88,128]{2,1,0:T(8,128)}), f32[8,88,128]{2,1,0:T(8,128)S(1)}, u32[]{:S(2)}, u32[]{:S(2)}) async-start(f32[8,88,128]{2,1,0:T(8,128)} %get-tuple-element.198), calls=%async_computation.2 | async-start | bytes 720896 | tf_op jit(solution)/shard_map/all_to_all | solution.py:628
  249.5 9.5 all-to-all-done.2.packed
  280.5 10.0 collective-permute-done.27
  317.1 28.3 %collective-permute-done.28.refs_1_ = f32[256,640]{1,0:T(8,128)S(1)} collective-permute-done((f32[256,640]{1,0:T(8,128)}, f32[256,640]{1,0:T(8,128)S(1)}, u32[]{:S(2)}, u32[]{:S(2)}) %collective-permute-start.28) | collective-permute-done | bytes 655392 | tf_op jit(solution)/shard_map/ppermute | solution.py:569
  349.3 19.2 %collective-permute-done.30.refs_3_ = f32[256,640]{1,0:T(8,128)} collective-permute-done((f32[256,640]{1,0:T(8,128)}, f32[256,640]{1,0:T(8,128)}, u32[]{:S(2)}, u32[]{:S(2)}) %collective-permute-start.30) | collective-permute-done | bytes 655392 | tf_op jit(solution)/shard_map/ppermute | solution.py:569
  441.8 21.0 %collective-permute-done.35 = f32[64,1280]{1,0:T(8,128)} collective-permute-done((f32[64,1280]{1,0:T(8,128)S(1)}, f32[64,1280]{1,0:T(8,128)}, u32[]{:S(2)}, u32[]{:S(2)}) %collective-permute-start.35) | collective-permute-done | bytes 327712 | tf_op jit(solution)/shard_map/ppermute | solution.py:573
  462.8 9.2 fusion.2
  496.3 12.4 %shard_map.435.refs_3_ = f32[1280,6400]{1,0:T(8,128)} custom-call(f32[256,1280]{1,0:T(8,128)S(1)} %pad_maximum_fusion.6.refs_0_, f32[256,1280]{1,0:T(8,128)S(1)} %copy-done.2, f32[256,3840]{1,0:T(8,128)} %pad_maximum_fusion.refs_2_), custom_call_target="tpu_custom_call" | custom-call | flops 7549747200 | bytes 22020096 | tf_op jit(solution)/shard_map/pallas_call | solution.py:1285
  566.5 11.0 %shard_map.436 = f32[1280,6400]{1,0:T(8,128)} custom-call(f32[64,1280]{1,0:T(8,128)S(1)} %fusion.62.refs_0_, f32[64,1280]{1,0:T(8,128)S(1)} %multiply_add_fusion.2.refs_1_, f32[64,2560]{1,0:T(8,128)S(1)} %concatenate.86.refs_2_, f32[1280,6400]{1,0:T(8,128)} %shard_map.435.refs_3_), custom_call_target="tpu_custom_call", output_to_operand_aliasing={{}: (3, {})} | custom-call | flops 1258291200 | bytes 14680064 | tf_op jit(solution)/shard_map/pallas_call | solution.py:1285
  577.6 10.7 %all-to-all-start.5 = ((f32[4,104,1280]{2,1,0:T(8,128)}), f32[4,104,1280]{2,1,0:T(8,128)}, u32[]{:S(2)}, u32[]{:S(2)}) async-start(f32[4,104,1280]{2,1,0:T(8,128)} %shard_map.437), calls=%async_computation.5 | async-start | bytes 4259840 | tf_op jit(solution)/shard_map/all_to_all | solution.py:589
  596.4 11.9 %shard_map.438 = (f32[256,320]{1,0:T(8,128)}, f32[256,640]{1,0:T(8,128)}, f32[256,640]{1,0:T(8,128)}, f32[256,640]{1,0:T(8,128)}, f32[256,640]{1,0:T(8,128)}) custom-call(s32[7]{0:T(128)} %stack.68.marks, f32[256,960]{1,0:T(8,128)} %copy-done.5, f32[256,640]{1,0:T(8,128)} %slice.349.refs_0_, f32[256,640]{1,0:T(8,128)} %copy-done.31, ...), custom_call_target="tpu_custom_call" | custom-call | flops 4194304 | bytes 10485760 | tf_op jit(solution)/shard_map/pallas_call | solution.py:1239
  673.9 10.3 shard_map.440
  711.1 9.7 collective-permute-done.56
  721.5 13.2 %collective-permute-done.54.refs_2_ = f32[8,80,128]{2,1,0:T(8,128)S(1)} collective-permute-done((f32[8,80,128]{2,1,0:T(8,128)}, f32[8,80,128]{2,1,0:T(8,128)S(1)}, u32[]{:S(2)}, u32[]{:S(2)}) %collective-permute-start.54) | collective-permute-done | bytes 327712 | tf_op jit(solution)/shard_map/ppermute | solution.py:573
  736.1 19.6 %shard_map.443 = (f32[4,320,256]{2,1,0:T(8,128)}, f32[4,320,256]{2,1,0:T(8,128)}, f32[2,1152,160]{2,1,0:T(8,128)}) custom-call(s32[7]{0:T(128)} %stack.68.marks, f32[8,80,128]{2,1,0:T(8,128)} %get-tuple-element.265.refs_0_.base, f32[8,80,128]{2,1,0:T(8,128)} %copy-done.90, f32[8,80,128]{2,1,0:T(8,128)} %copy-done.91, f32[8,80,128]{2,1,0:T(8,128)} %copy-done.92, ...), custom_call_target="tpu_custom_call" | custom-call | flops 5662310400 | bytes 10485760 | tf_op jit(solution)/shard_map/pallas_call | solution.py:1239
  766.4 14.1 %collective-permute-done.58 = f32[320,256]{1,0:T(8,128)S(1)} collective-permute-done((f32[320,256]{1,0:T(8,128)S(1)}, f32[320,256]{1,0:T(8,128)S(1)}, u32[]{:S(2)}, u32[]{:S(2)}) %collective-permute-start.58) | collective-permute-done | bytes 327712 | tf_op jit(solution)/shard_map/ppermute | solution.py:569
  780.7 14.5 %collective-permute-done.60 = f32[320,256]{1,0:T(8,128)S(1)} collective-permute-done((f32[320,256]{1,0:T(8,128)S(1)}, f32[320,256]{1,0:T(8,128)S(1)}, u32[]{:S(2)}, u32[]{:S(2)}) %collective-permute-start.60) | collective-permute-done | bytes 327712 | tf_op jit(solution)/shard_map/ppermute | solution.py:569
  799.5 14.1 %collective-permute-done.61.refs_1_ = f32[320,256]{1,0:T(8,128)} collective-permute-done((f32[320,256]{1,0:T(8,128)}, f32[320,256]{1,0:T(8,128)}, u32[]{:S(2)}, u32[]{:S(2)}) %collective-permute-start.61) | collective-permute-done | bytes 327712 | tf_op jit(solution)/shard_map/ppermute | solution.py:569
  831.3 26.0 %shard_map.444 = (f32[8,80,128]{2,1,0:T(8,128)}, f32[8,80,128]{2,1,0:T(8,128)}, f32[8,80,128]{2,1,0:T(8,128)}, f32[8,80,128]{2,1,0:T(8,128)}, f32[2,1152,320]{2,...) custom-call(s32[7]{0:T(128)} %stack.68.marks, f32[320,256]{1,0:T(8,128)} %fusion.50.refs_0_, ...), custom_call_target="tpu_custom_call" | custom-call | flops 5662310400 | bytes 10485760 | tf_op jit(solution)/shard_map/pallas_call | solution.py:1239
  870.7 20.1 %shard_map.445 = f32[9,160,320]{2,1,0:T(8,128)} custom-call(s32[7]{0:T(128)} %stack.68.marks, f32[2,1152,160]{2,1,0:T(8,128)} %get-tuple-element.292.image, f32[2,1152,320]{2,1,0:T(8,128)} %get-tuple-element.295.cells), custom_call_target="tpu_custom_call" | custom-call | flops 5662310400 | bytes 10485760 | tf_op jit(solution)/shard_map/pallas_call | solution.py:1239
  905.8 9.1 collective-permute-start.72
  914.8 14.5 %collective-permute-start.73 = (f32[8,160]{1,0:T(8,128)}, f32[8,160]{1,0:T(8,128)S(1)}, u32[]{:S(2)}, u32[]{:S(2)}) collective-permute-start(f32[8,160]{1,0:T(8,128)} %get-tuple-element.307.refs_0_), channel_id=1, source_target_pairs={{0,2},{1,3},{2,0},{3,1},{4,6},{5,7},{6,4},{7,5},{8,10},{9,11},{10,... | collective-permute-start | bytes 15368 | tf_op jit(solution)/shard_map/ppermute | solution.py:573
  949.0 20.1 %shard_map.448 = f32[9,160,320]{2,1,0:T(8,128)} custom-call(s32[7]{0:T(128)} %stack.68.marks, f32[2,1152,160]{2,1,0:T(8,128)} %get-tuple-element.311.image, f32[2,1152,320]{2,1,0:T(8,128)} %get-tuple-element.312.cells), custom_call_target="tpu_custom_call" | custom-call | flops 5662310400 | bytes 10485760 | tf_op jit(solution)/shard_map/pallas_call | solution.py:1239
  985.5 12.8 %collective-permute-done.82 = f32[160,320]{1,0:T(8,128)S(1)} collective-permute-done((f32[160,320]{1,0:T(8,128)S(1)}, f32[160,320]{1,0:T(8,128)S(1)}, u32[]{:S(2)}, u32[]{:S(2)}) %collective-permute-start.82) | collective-permute-done | bytes 204832 | tf_op jit(solution)/shard_map/ppermute | solution.py:573
  998.3 16.5 %collective-permute-start.81 = (f32[64,1280]{1,0:T(8,128)}, f32[64,1280]{1,0:T(8,128)S(1)}, u32[]{:S(2)}, u32[]{:S(2)}) collective-permute-start(f32[64,1280]{1,0:T(8,128)} %shard_map.449.refs_0_), channel_id=1, source_target_pairs={{0,1},{1,2},{2,3},{3,0},{4,5},{5,6},{6,7},{7,4},{8,9},{9,10},{10,1... | collective-permute-start | bytes 983048 | tf_op jit(solution)/shard_map/ppermute | solution.py:573
  (569 shorter events, 539.7 us)
Async XLA Ops:
  7.2 112.8 %all-gather.4.cloned.1.call-start = ((), (), s32[]{:S(2)}) async-start(), calls=%async_computation.12 | async-start | bytes 10321920 | tf_op jit(solution)/shard_map/all_gather | solution.py:1445
  18.6 32.6 %all-to-all-start = ((f32[8,320,128]{2,1,0:T(8,128)}), f32[8,320,128]{2,1,0:T(8,128)S(1)}, u32[]{:S(2)}, u32[]{:S(2)}) async-start(f32[8,320,128]{2,1,0:T(8,128)} %shard_map.425), calls=%async_computation | async-start | bytes 2621440 | tf_op jit(solution)/shard_map/all_to_all | solution.py:628
  23.5 238.8 %all-gather.6.cloned.1.call-start = ((), (), s32[]{:S(2)}) async-start(), calls=%async_computation.13 | async-start | bytes 22118400 | tf_op jit(solution)/shard_map/all_gather | solution.py:1445
  23.8 47.4 %collective-permute-start.1 = (f32[168,960]{1,0:T(8,128)S(1)}, f32[168,960]{1,0:T(8,128)S(1)}, u32[]{:S(2)}, u32[]{:S(2)}) collective-permute-start(f32[168,960]{1,0:T(8,128)S(1)} %select_maximum_fusion.refs_0_), channel_id=1, source_target_pairs={{0,3},{1,0},{2,1},{3,2},{4,7},{5,4},{6,5},{7,6},{8,11},{9,8},{10,9... | collective-permute-start | bytes 1935368 | tf_op jit(solution)/shard_map/ppermute | solution.py:573
  27.5 59.6 %collective-permute-start.2 = (f32[168,960]{1,0:T(8,128)S(1)}, f32[168,960]{1,0:T(8,128)}, u32[]{:S(2)}, u32[]{:S(2)}) collective-permute-start(f32[168,960]{1,0:T(8,128)S(1)} %select_maximum_fusion.refs_0_), channel_id=1, source_target_pairs={{0,2},{1,3},{2,0},{3,1},{4,6},{5,7},{6,4},{7,5},{8,10},{9,11},{10,... | collective-permute-start | bytes 1935368 | tf_op jit(solution)/shard_map/ppermute | solution.py:573
  27.5 59.6 %collective-permute-start.3 = (f32[168,960]{1,0:T(8,128)S(1)}, f32[168,960]{1,0:T(8,128)}, u32[]{:S(2)}, u32[]{:S(2)}) collective-permute-start(f32[168,960]{1,0:T(8,128)S(1)} %select_maximum_fusion.refs_0_), channel_id=1, source_target_pairs={{0,1},{1,2},{2,3},{3,0},{4,5},{5,6},{6,7},{7,4},{8,9},{9,10},{10,1... | collective-permute-start | bytes 1935368 | tf_op jit(solution)/shard_map/ppermute | solution.py:573
  114.6 281.4 %all-gather.8.cloned.1.call-start = ((), (), s32[]{:S(2)}) async-start(), calls=%async_computation.14 | async-start | bytes 22118400 | tf_op jit(solution)/shard_map/all_gather | solution.py:1445
  125.3 42.9 %all-to-all-start.1 = ((f32[4,64,1600]{2,1,0:T(8,128)}), f32[4,64,1600]{2,1,0:T(8,128)S(1)}, u32[]{:S(2)}, u32[]{:S(2)}) async-start(f32[4,64,1600]{2,1,0:T(8,128)} %bitcast.181), calls=%async_computation.1 | async-start | bytes 3407872 | tf_op jit(solution)/shard_map/all_to_all | solution.py:589
  131.3 30.1 %collective-permute-start.10 = (f32[320,256]{1,0:T(8,128)}, f32[320,256]{1,0:T(8,128)}, u32[]{:S(2)}, u32[]{:S(2)}) collective-permute-start(f32[320,256]{1,0:T(8,128)} %fusion.56.refs_0_.refs_8_), channel_id=1, source_target_pairs={{0,12},{4,8},{8,4},{12,0},{1,13},{5,9},{9,5},{13,1},{2,14},{6,10},... | collective-permute-start | bytes 983048 | tf_op jit(solution)/shard_map/ppermute | solution.py:569
  132.9 31.2 %collective-permute-start.11 = (f32[320,256]{1,0:T(8,128)}, f32[320,256]{1,0:T(8,128)}, u32[]{:S(2)}, u32[]{:S(2)}) collective-permute-start(f32[320,256]{1,0:T(8,128)} %fusion.56.refs_0_.refs_8_), channel_id=1, source_target_pairs={{0,16},{16,0},{1,17},{17,1},{2,18},{18,2},{3,19},{19,3},{4,20},{20... | collective-permute-start | bytes 983048 | tf_op jit(solution)/shard_map/ppermute | solution.py:565
  194.8 52.7 %collective-permute-start.24 = (f32[77,256]{1,0:T(8,128)S(1)}, f32[77,256]{1,0:T(8,128)S(1)}, u32[]{:S(2)}, u32[]{:S(2)}) collective-permute-start(f32[77,256]{1,0:T(8,128)S(1)} %get-tuple-element.431), channel_id=1, source_target_pairs={{0,16},{16,0},{1,17},{17,1},{2,18},{18,2},{3,19},{19,3},{4,20},{20... | collective-permute-start | bytes 236552 | tf_op jit(solution)/shard_map/ppermute | solution.py:565
  309.0 59.4 %all-to-all-start.4 = ((f32[4,104,1280]{2,1,0:T(8,128)}), f32[4,104,1280]{2,1,0:T(8,128)}, u32[]{:S(2)}, u32[]{:S(2)}) async-start(f32[4,104,1280]{2,1,0:T(8,128)} %broadcast_in_dim.21), calls=%async_computation.4 | async-start | bytes 4259840 | tf_op jit(solution)/shard_map/all_to_all | solution.py:589
  313.5 508.4 %reduce-scatter.3.cloned.1.call-start = ((), (), s32[]{:S(2)}) async-start(), calls=%async_computation.15 | async-start | bytes 36864000 | tf_op jit(solution)/shard_map/reduce_scatter | solution.py:1449
  313.5 31.9 %collective-permute-start.28 = (f32[256,640]{1,0:T(8,128)}, f32[256,640]{1,0:T(8,128)S(1)}, u32[]{:S(2)}, u32[]{:S(2)}) collective-permute-start(f32[256,640]{1,0:T(8,128)} %slice.349.refs_0_), channel_id=1, source_target_pairs={{0,4},{4,0},{8,12},{12,8},{1,5},{5,1},{9,13},{13,9},{2,6},{6,2},{1... | collective-permute-start | bytes 1966088 | tf_op jit(solution)/shard_map/ppermute | solution.py:569
  315.3 34.0 %collective-permute-start.29 = (f32[256,640]{1,0:T(8,128)}, f32[256,640]{1,0:T(8,128)}, u32[]{:S(2)}, u32[]{:S(2)}) collective-permute-start(f32[256,640]{1,0:T(8,128)} %slice.349.refs_0_), channel_id=1, source_target_pairs={{0,8},{4,12},{8,0},{12,4},{1,9},{5,13},{9,1},{13,5},{2,10},{6,14},... | collective-permute-start | bytes 1966088 | tf_op jit(solution)/shard_map/ppermute | solution.py:569
  315.6 52.9 %collective-permute-start.30 = (f32[256,640]{1,0:T(8,128)}, f32[256,640]{1,0:T(8,128)}, u32[]{:S(2)}, u32[]{:S(2)}) collective-permute-start(f32[256,640]{1,0:T(8,128)} %slice.349.refs_0_), channel_id=1, source_target_pairs={{0,12},{4,8},{8,4},{12,0},{1,13},{5,9},{9,5},{13,1},{2,14},{6,10},... | collective-permute-start | bytes 1966088 | tf_op jit(solution)/shard_map/ppermute | solution.py:569
  535.1 42.4 %collective-permute-start.41 = (f32[64,1280]{1,0:T(8,128)}, f32[64,1280]{1,0:T(8,128)}, u32[]{:S(2)}, u32[]{:S(2)}) collective-permute-start(f32[64,1280]{1,0:T(8,128)} %multiply_add_fusion.1), channel_id=1, source_target_pairs={{0,2},{1,3},{2,0},{3,1},{4,6},{5,7},{6,4},{7,5},{8,10},{9,11},{10,... | collective-permute-start | bytes 983048 | tf_op jit(solution)/shard_map/ppermute | solution.py:573
  544.1 33.4 %collective-permute-start.42 = (f32[64,1280]{1,0:T(8,128)}, f32[64,1280]{1,0:T(8,128)}, u32[]{:S(2)}, u32[]{:S(2)}) collective-permute-start(f32[64,1280]{1,0:T(8,128)} %multiply_add_fusion.1), channel_id=1, source_target_pairs={{0,1},{1,2},{2,3},{3,0},{4,5},{5,6},{6,7},{7,4},{8,9},{9,10},{10,1... | collective-permute-start | bytes 983048 | tf_op jit(solution)/shard_map/ppermute | solution.py:573
  577.6 76.5 %all-to-all-start.5 = ((f32[4,104,1280]{2,1,0:T(8,128)}), f32[4,104,1280]{2,1,0:T(8,128)}, u32[]{:S(2)}, u32[]{:S(2)}) async-start(f32[4,104,1280]{2,1,0:T(8,128)} %shard_map.437), calls=%async_computation.5 | async-start | bytes 4259840 | tf_op jit(solution)/shard_map/all_to_all | solution.py:589
  668.5 304.9 %reduce-scatter.5.cloned.1.call-start = ((), (), s32[]{:S(2)}) async-start(), calls=%async_computation.16 | async-start | bytes 14745600 | tf_op jit(solution)/shard_map/reduce_scatter | solution.py:1449
  759.2 61.8 %all-to-all-start.7 = ((f32[4,72,1600]{2,1,0:T(8,128)}), f32[4,72,1600]{2,1,0:T(8,128)S(1)}, u32[]{:S(2)}, u32[]{:S(2)}) async-start(f32[4,72,1600]{2,1,0:T(8,128)} %pad_maximum_fusion.3), calls=%async_computation.7 | async-start | bytes 3833856 | tf_op jit(solution)/shard_map/all_to_all | solution.py:589
  765.0 30.2 %collective-permute-start.60 = (f32[320,256]{1,0:T(8,128)S(1)}, f32[320,256]{1,0:T(8,128)S(1)}, u32[]{:S(2)}, u32[]{:S(2)}) collective-permute-start(f32[320,256]{1,0:T(8,128)S(1)} %get-tuple-element.408), channel_id=1, source_target_pairs={{0,12},{4,8},{8,4},{12,0},{1,13},{5,9},{9,5},{13,1},{2,14},{6,10},... | collective-permute-start | bytes 983048 | tf_op jit(solution)/shard_map/ppermute | solution.py:569
  826.7 64.1 %all-to-all-start.8 = ((f32[4,160,640]{2,1,0:T(8,128)}), f32[4,160,640]{2,1,0:T(8,128)S(1)}, u32[]{:S(2)}, u32[]{:S(2)}) async-start(f32[4,160,640]{2,1,0:T(8,128)} %pad_maximum_fusion.5), calls=%async_computation.9 | async-start | bytes 3276800 | tf_op jit(solution)/shard_map/all_to_all | solution.py:589
  859.9 34.8 %collective-permute-start.69 = (f32[8,80,128]{2,1,0:T(8,128)}, f32[8,80,128]{2,1,0:T(8,128)}, u32[]{:S(2)}, u32[]{:S(2)}) collective-permute-start(f32[8,80,128]{2,1,0:T(8,128)} %get-tuple-element.290), channel_id=1, source_target_pairs={{0,2},{1,3},{2,0},{3,1},{4,6},{5,7},{6,4},{7,5},{8,10},{9,11},{10,... | collective-permute-start | bytes 983048 | tf_op jit(solution)/shard_map/ppermute | solution.py:573
  862.3 32.5 %collective-permute-start.70 = (f32[8,80,128]{2,1,0:T(8,128)}, f32[8,80,128]{2,1,0:T(8,128)}, u32[]{:S(2)}, u32[]{:S(2)}) collective-permute-start(f32[8,80,128]{2,1,0:T(8,128)} %get-tuple-element.291), channel_id=1, source_target_pairs={{0,3},{1,0},{2,1},{3,2},{4,7},{5,4},{6,5},{7,6},{8,11},{9,8},{10,9... | collective-permute-start | bytes 983048 | tf_op jit(solution)/shard_map/ppermute | solution.py:573
  898.3 45.8 %collective-permute-start.75 = (f32[4,160,320]{2,1,0:T(8,128)}, f32[4,160,320]{2,1,0:T(8,128)}, u32[]{:S(2)}, u32[]{:S(2)}) collective-permute-start(f32[4,160,320]{2,1,0:T(8,128)} %dynamic-slice_bitcast_fusion), channel_id=1, source_target_pairs={{0,16},{16,0},{1,17},{17,1},{2,18},{18,2},{3,19},{19,3},{4,20},{20... | collective-permute-start | bytes 2457608 | tf_op jit(solution)/shard_map/ppermute | solution.py:565
  938.5 31.4 %all-to-all-start.9 = ((f32[8,88,128]{2,1,0:T(8,128)}), f32[8,88,128]{2,1,0:T(8,128)}, u32[]{:S(2)}, u32[]{:S(2)}) async-start(f32[8,88,128]{2,1,0:T(8,128)} %get-tuple-element.308), calls=%async_computation.10 | async-start | bytes 720896 | tf_op jit(solution)/shard_map/all_to_all | solution.py:628
  975.9 48.2 %collective-permute-start.79 = (f32[64,1280]{1,0:T(8,128)}, f32[64,1280]{1,0:T(8,128)}, u32[]{:S(2)}, u32[]{:S(2)}) collective-permute-start(f32[64,1280]{1,0:T(8,128)} %shard_map.449.refs_0_), channel_id=1, source_target_pairs={{0,3},{1,0},{2,1},{3,2},{4,7},{5,4},{6,5},{7,6},{8,11},{9,8},{10,9... | collective-permute-start | bytes 983048 | tf_op jit(solution)/shard_map/ppermute | solution.py:573
  976.5 56.3 %collective-permute-start.80 = (f32[64,1280]{1,0:T(8,128)}, f32[64,1280]{1,0:T(8,128)}, u32[]{:S(2)}, u32[]{:S(2)}) collective-permute-start(f32[64,1280]{1,0:T(8,128)} %shard_map.449.refs_0_), channel_id=1, source_target_pairs={{0,2},{1,3},{2,0},{3,1},{4,6},{5,7},{6,4},{7,5},{8,10},{9,11},{10,... | collective-permute-start | bytes 983048 | tf_op jit(solution)/shard_map/ppermute | solution.py:573
  979.6 43.7 %collective-permute-start.83 = (f32[160,320]{1,0:T(8,128)S(1)}, f32[160,320]{1,0:T(8,128)S(1)}, u32[]{:S(2)}, u32[]{:S(2)}) collective-permute-start(f32[160,320]{1,0:T(8,128)S(1)} %bitcast.207), channel_id=1, source_target_pairs={{0,2},{1,3},{2,0},{3,1},{4,6},{5,7},{6,4},{7,5},{8,10},{9,11},{10,... | collective-permute-start | bytes 614408 | tf_op jit(solution)/shard_map/ppermute | solution.py:573
  982.6 40.7 %collective-permute-start.84 = (f32[160,320]{1,0:T(8,128)S(1)}, f32[160,320]{1,0:T(8,128)S(1)}, u32[]{:S(2)}, u32[]{:S(2)}) collective-permute-start(f32[160,320]{1,0:T(8,128)S(1)} %bitcast.209), channel_id=1, source_target_pairs={{0,3},{1,0},{2,1},{3,2},{4,7},{5,4},{6,5},{7,6},{8,11},{9,8},{10,9... | collective-permute-start | bytes 614408 | tf_op jit(solution)/shard_map/ppermute | solution.py:573
  998.3 34.4 %collective-permute-start.81 = (f32[64,1280]{1,0:T(8,128)}, f32[64,1280]{1,0:T(8,128)S(1)}, u32[]{:S(2)}, u32[]{:S(2)}) collective-permute-start(f32[64,1280]{1,0:T(8,128)} %shard_map.449.refs_0_), channel_id=1, source_target_pairs={{0,1},{1,2},{2,3},{3,0},{4,5},{5,6},{6,7},{7,4},{8,9},{9,10},{10,1... | collective-permute-start | bytes 983048 | tf_op jit(solution)/shard_map/ppermute | solution.py:573
  (163 other events, 2159.5 us)
Sparse Core Ops, SparseCore 0:
  10.7 74.4 all-gather.3
  114.7 115.5 all-gather.5
  232.2 139.7 all-gather.7
  577.7 237.1 reduce-scatter.2
  818.3 96.0 reduce-scatter.4

commit v2 on v1

--- a/solution.py
+++ b/solution.py
@@ -1079,16 +1079,19 @@
         values[40:77, lanes] = pieces[part, 64:101, 960:1280]
 
 
-def text_grad_kernel(marks, rows, keys, values, out):
-    for part in range(4):
-        at = pl.multiple_of(lax.rem(part - marks[6] + 4, 4) * 64, 8)
-        out[part, 0:64, :] = rows[pl.ds(at, 64), :]
-        lanes = slice(320 * part, 320 * part + 320)
-        out[part, 64:104, 0:320] = keys[0:40, lanes]
-        out[part, 64:104, 320:640] = values[0:40, lanes]
-        out[part, 64:101, 640:960] = keys[40:77, lanes]
-        out[part, 64:101, 960:1280] = values[40:77, lanes]
-        out[part, 101:104, 640:1280] = jnp.zeros((3, 640), jnp.float32)
+def text_grad_kernel(marks, keys, values, *outs):
+    for first in range(4):
+
+        @pl.when(marks[6] == first)
+        def _():
+            for j in range(4):
+                at = (first + j) % 4 * 320
+                lanes = slice(at, at + 320)
+                outs[j][:, 0:320] = keys[0:40, lanes]
+                outs[j][:, 320:640] = values[0:40, lanes]
+                outs[j][0:37, 640:960] = keys[40:77, lanes]
+                outs[j][0:37, 960:1280] = values[40:77, lanes]
+                outs[j][37:40, 640:1280] = jnp.zeros((3, 640), jnp.float32)
 
 
 def rows_kernel(marks, *refs):
@@ -1548,7 +1551,7 @@
     query_cross_full = third_full[:, 1280:2560]
     out_cross_full = third_full[:, 2560:]
     ff_block = jnp.concatenate([ff_in.reshape(160, 2560), ff_out.T], axis=1)
-    ff_full = gather_plane(after(ff_block, part))
+    ff_full = gather_plane(after(ff_block, third))
     ff_in_full = ff_full[:, :2560]
     ff_out_full = ff_full[:, 2560:]
     cot = after(cotangent[0] * own_valid, own_one)
@@ -1651,7 +1654,8 @@
         0,
         5,
     )
-    grad_normed_ff, ff_grads = together(grad_normed_ff, ff_grads)
+    out_part = mm(after(ff_act, normed_pieces[1]), ff_out_full, 1, 1)
+    grad_normed_ff, ff_grads, out_part = together(grad_normed_ff, ff_grads, out_part)
 
     back_ff, grad_gain_ff = layer_grad(grad_normed_ff, centred_ff, inv_ff, gain_ff_full)
     grad_after_cross = grad_after_ff + back_ff
@@ -1677,18 +1681,10 @@
         5,
         ff_grads,
     )
-    ff_here, grad_keys_text, grad_values_text = after(
-        (ff_act, grad_keys_text, grad_values_text), grad_pieces[1]
-    )
-    out_part = mm(ff_here, ff_out_full, 1, 1)
-    (side_grads,) = small(
-        text_grad_kernel,
-        marks,
-        (out_part, grad_keys_text, grad_values_text),
-        [(4, 104, channels)],
-    )
-    *grad_pieces, cross_grads, side_grads = together(*grad_pieces, cross_grads, side_grads)
-    side_grads = z_all(side_grads)
+    *grad_pieces, cross_grads = together(*grad_pieces, cross_grads)
+    out_turned = jnp.concatenate([out_part, out_part], axis=0)
+    out_turned = lax.dynamic_slice_in_dim(out_turned, lax.rem(4 - t, 4) * 64, 256, 0)
+    out_sum = z_all(after(out_turned, grad_after_self).reshape(4, 64, channels))
     ff_grads = scatter_plane(cross_grads)
     ff_grads, cross_grads = ff_grads[:, :3840], ff_grads[:, 3840:]
 
@@ -1706,16 +1702,21 @@
     grad_normed_part = mm(grad_qkv, qkv_full, 1, 1)
     normed_pieces = z_received(rows_of(grad_normed_part))
     grad_normed_self = total_of(normed_pieces)
-    grad_normed_self, side_grads = together(grad_normed_self, side_grads)
+    text_grads = small(
+        text_grad_kernel,
+        marks,
+        after((grad_keys_text, grad_values_text), normed_pieces[1]),
+        [(40, channels)] * 4,
+    )
+    grad_normed_self, out_sum, *text_grads = together(grad_normed_self, out_sum, *text_grads)
     back_self, grad_gain_self = layer_grad(grad_normed_self, centred_self, inv_self, gain_self_full)
     grad_projected = grad_after_self + back_self
     grad_norm_three = mm(grad_projected, proj_in_full, 1, 0)
 
     (grad_three,) = small(pack_kernel, marks, (grad_norm_three,), [(8, 80, 128)])
     grad_three_q = plane_exchange(grad_three)
-    side_grads = jnp.sum(after(side_grads, grad_three), axis=0)
-    out_sum, text_grads = side_grads[:64], side_grads[64:]
-    text_grads = text_grads + flip(text_grads, 1)
+    out_sum = jnp.sum(after(out_sum, grad_three), axis=0)
+    text_grads = total_of(z_received(text_grads))
     attn_right = jnp.concatenate(
         [
             jnp.concatenate([grad_qkv, attn_self], axis=1),
@@ -1747,7 +1748,7 @@
 
     residual_pieces = z_pieces(grad_residual_q)
     text_grads = after(text_grads, grad_residual_q)
-    text_grads = text_grads + flip(text_grads, 2)
+    text_grads = text_grads + flip(text_grads, 1)
     *residual_pieces, text_grads = together(*residual_pieces, text_grads)
     own_two, other_two, image_back = second_conv_back(marks, residual_pieces, second_weight)
     own_two = own_two + swap(other_two)
@@ -1783,17 +1784,12 @@
     )
     grad_act_pieces = z_received(grad_act_one)
     image_grad, text_grads = after((image_grad, text_grads), grad_act_pieces[1])
-    text_other_grads = swap(text_grads)
+    text_grads = text_grads + flip(text_grads, 2)
     grad_conv_first = conv_weight(marks, image_one, image_grad, 1)
-    cross_shares, after_ff_here = after((cross_shares, after_ff_all), grad_act_pieces[1])
-    cross_shares = jnp.sum(cross_shares, axis=0)
-    grad_proj_out = mm(after_ff_here, cot, 0, 0)
-    *grad_act_pieces, grad_conv_first, cross_shares, grad_proj_out, text_other_grads = together(
-        *grad_act_pieces, grad_conv_first, cross_shares, grad_proj_out, text_other_grads
-    )
-    text_grads, text_other_grads = unfolded(text_grads), unfolded(text_other_grads)
-    grad_proj_out = grad_proj_out.reshape(2, 4, width, wide)
-    grad_proj_own = pick(grad_proj_out, item) + swap(pick(grad_proj_out, 1 - item))
+    cross_shares = jnp.sum(after(cross_shares, grad_act_pieces[1]), axis=0)
+    *grad_act_pieces, grad_conv_first, cross_shares, text_grads = together(
+        *grad_act_pieces, grad_conv_first, cross_shares, text_grads
+    )
     grad_conv_first = grad_conv_first.reshape(3, 3, width, wide)
     extra = jnp.concatenate(
         [
@@ -1826,27 +1822,26 @@
         [(8, 88, 128), (8, width)],
     )
     received = plane_exchange(moved)
-    grad_proj_own, image_back = after((grad_proj_own, image_back), moved)
-    grad_conv_second = conv_weight(marks, image_back, image_two, -1)
-    grad_proj_out = h_collect([pick(grad_proj_own, h ^ j) for j in range(4)])
-    received, grad_conv_second, grad_proj_out = together(
-        received, grad_conv_second, grad_proj_out
-    )
-    grad_conv_second = grad_conv_second.reshape(3, 3, width, wide).transpose(0, 1, 3, 2)
-    attn_grads = after(attn_grads, received)
+    attn_grads, text_grads = after((attn_grads, text_grads), moved)
+    text_other_grads = swap(text_grads)
     proj_cut = attn_grads[:, 1280:].reshape(width, 4, wide)
-    proj_pieces = z_received([pick(proj_cut, lax.rem(t + j, 4), 1) for j in range(4)])
+    proj_share = total_of(z_received([pick(proj_cut, lax.rem(t + j, 4), 1) for j in range(4)]))
+    received, proj_share, text_other_grads = together(received, proj_share, text_other_grads)
+    text_grads, text_other_grads = unfolded(text_grads), unfolded(text_other_grads)
     (grad_hidden,) = small(unpack_kernel, marks, (received,), [(64, channels)])
     hidden_pieces = z_pieces(grad_hidden)
-    text_own, text_other, own_features, after_ff_all = after(
-        (text_own, text_other, own_features, after_ff_all), hidden_pieces[1]
-    )
+    after_ff_all, image_back = after((after_ff_all, image_back), grad_hidden)
+    grad_proj_out = mm(after_ff_all, cot, 0, 0).reshape(2, 4, width, wide)
+    grad_proj_own = pick(grad_proj_out, item) + swap(pick(grad_proj_out, 1 - item))
+    grad_proj_out = h_collect([pick(grad_proj_own, h ^ j) for j in range(4)])
+    grad_conv_second = conv_weight(marks, image_back, image_two, -1)
+    *hidden_pieces, grad_conv_second = together(*hidden_pieces, grad_conv_second)
+    grad_conv_second = grad_conv_second.reshape(3, 3, width, wide).transpose(0, 1, 3, 2)
     output = residual_all + mm(after_ff_all, proj_out_full, 1, 0)
     output = output * own_valid
     grad_text_weight = mm(text_own, text_grads, 0, 0) + mm(text_other, text_other_grads, 0, 0)
     grad_time_weight = mm(own_features, grad_tau, 0, 0)
     (grad_hidden,) = small(rows_kernel, marks, hidden_pieces, [(256, channels)])
-    proj_share = total_of(proj_pieces)
     extra = jnp.concatenate([received[:, 80:84, :], received[:, 84:88, :32]], axis=2)
     grad_gain_attn = lax.dynamic_slice_in_dim(extra[:, 0].reshape(channels), t * wide, wide, 0)
     gain_sums = jnp.sum(extra[:, 1:], axis=0)

time: 1060 us -> 1010 us (0.953)
  starting transfers between devices: 218 us -> 198 us
  waiting for transfers between devices: 356 us -> 338 us
    ppermute x45 -> x48, waiting for transfers between devices: 134 us -> 122 us  [turn(): return lax.ppermute(values, T, [(s, (s + step) % 4) for s in range(4)])]
    all_to_all x5, starting transfers between devices: 30.4 us -> 19.7 us  [plane_exchange(): return lax.all_to_all(packed, IH, 0, 0)]
    ppermute x45 -> x48, starting transfers between devices: 128 us -> 123 us  [turn(): return lax.ppermute(values, T, [(s, (s + step) % 4) for s in range(4)])]
    unnamed x203 -> x225, local copies, waits for them, and re-layouts: 28.6 us -> 25.1 us
  transfers between devices with their start and end apart: 100 -> 103, of which waited for: 47 -> 45; matrix products, arithmetic and copies ran while one was open for 15% -> 15% of each run, Pallas kernels for 21% -> 21%
where the time goes in v2:
time: 1010 us; the launch traced here: 1000 us
  waiting for transfers between devices  338 us (33%)
  Pallas kernels  217 us (21%)
  starting transfers between devices  198 us (20%)
  matrix products  110 us (11%)
  local copies, waits for them, and re-layouts  82.8 us (8%)
  other arithmetic  38.8 us (4%)
  between operations  17.6 us (2%)
    ppermute x25, waiting for transfers between devices, flip(): return lax.ppermute(values, H, [(s, s ^ step) for s in range(4)])  183 us
    pallas_call x23, Pallas kernels, run_kernel(): pl.pallas_call(body, out_shape=[jax.ShapeDtypeStruct(shape, jnp.float32)...  182 us
    ppermute x48, starting transfers between devices, turn(): return lax.ppermute(values, T, [(s, (s + step) % 4) for s in range(4)])  123 us
    ppermute x48, waiting for transfers between devices, turn(): return lax.ppermute(values, T, [(s, (s + step) % 4) for s in range(4)])  122 us
    dot_general x23, matrix products, mm(): lax.dot_general(left, right, (((left_dim,), (right_dim,)), ((), ())), pre...  103 us
    pallas_call x3, Pallas kernels, weight_grads(): pl.pallas_call(functools.partial(weight_kernel, plan), out_shape=jax.Shap...  34.3 us
    ppermute x25, starting transfers between devices, flip(): return lax.ppermute(values, H, [(s, s ^ step) for s in range(4)])  31.9 us
    unnamed x225, local copies, waits for them, and re-layouts  25.1 us
  transfers between devices with their start and end apart: 103, of which 45 were waited for; matrix products, arithmetic and copies ran while one was open for 15% of the time, Pallas kernels for 21%

profile of v2, /device:TPU:0, one launch (start us, length us, event | category | flops | bytes accessed | tf_op | source)
XLA Modules:
  0.0 1001.9 jit_solution(11365555507066524964)
XLA Ops:
  32.0 19.1 %all-to-all-done.source = f32[8,320,128]{2,1,0:T(8,128)S(1)} async-done(((f32[8,320,128]{2,1,0:T(8,128)}), f32[8,320,128]{2,1,0:T(8,128)S(1)}, u32[]{:S(2)}, u32[]{:S(2)}) %all-to-all-start) | async-done | bytes 1310752 | tf_op jit(solution)/shard_map/all_to_all | solution.py:628
  52.2 19.1 %shard_map.426 = (f32[4,320,256]{2,1,0:T(8,128)}, f32[4,320,256]{2,1,0:T(8,128)}, f32[2,1152,160]{2,1,0:T(8,128)}, f32[2,8,160]{2,1,0:T(8,128)}) custom-call(s32[7]{0:T(128)} %stack.68.marks, f32[8,320,128]{2,1,0:T(8,128)} %copy-done.5, f32[1,160]{1,0:T(1,128)} %bitcast.210, f32[2,320]{1,0:T(2,128)} %fusion.82.tau, f32[1440,320]{1,0:T(8,128)} %bitcast.223), custom_call_target="tpu_custom_call" | custom-call | flops 5662310400 | bytes 10485760 | tf_op jit(solution)/shard_map/pallas_call | solution.py:1242
  71.3 15.7 %collective-permute-done.2.refs_2_ = f32[168,960]{1,0:T(8,128)} collective-permute-done((f32[168,960]{1,0:T(8,128)S(1)}, f32[168,960]{1,0:T(8,128)}, u32[]{:S(2)}, u32[]{:S(2)}) %collective-permute-start.2) | collective-permute-done | bytes 645152 | tf_op jit(solution)/shard_map/ppermute | solution.py:573
  102.4 7.6 collective-permute-done.6
  132.9 14.4 %collective-permute-done.8.refs_1_.refs_9_ = f32[320,256]{1,0:T(8,128)} collective-permute-done((f32[320,256]{1,0:T(8,128)}, f32[320,256]{1,0:T(8,128)}, u32[]{:S(2)}, u32[]{:S(2)}) %collective-permute-start.8) | collective-permute-done | bytes 327712 | tf_op jit(solution)/shard_map/ppermute | solution.py:569
  148.8 12.6 %collective-permute-done.10.refs_3_.refs_11_ = f32[320,256]{1,0:T(8,128)} collective-permute-done((f32[320,256]{1,0:T(8,128)}, f32[320,256]{1,0:T(8,128)}, u32[]{:S(2)}, u32[]{:S(2)}) %collective-permute-start.10) | collective-permute-done | bytes 327712 | tf_op jit(solution)/shard_map/ppermute | solution.py:569
  168.1 21.4 %shard_map.427 = (f32[8,80,128]{2,1,0:T(8,128)}, f32[8,80,128]{2,1,0:T(8,128)}, f32[8,80,128]{2,1,0:T(8,128)}, f32[8,80,128]{2,1,0:T(8,128)}, f32[2,1152,320]{2,1,0:T(8,128)}, /*index=5*/f32[2,8,320]{2,1,0:T(8,128)}) custom-call(s32[7]{0:T(128)} %stack.68.marks, f32[320,256]{1,0:T(8,128)} %fusion.57.refs_0_.refs_8_, ...), custom_call_target="tpu_custom_call" | custom-call | flops 5662310400 | bytes 10485760 | tf_op jit(solution)/shard_map/pallas_call | solution.py:1242
  202.3 12.2 %collective-permute-done.16.third = f32[8,80,128]{2,1,0:T(8,128)S(1)} collective-permute-done((f32[8,80,128]{2,1,0:T(8,128)}, f32[8,80,128]{2,1,0:T(8,128)S(1)}, u32[]{:S(2)}, u32[]{:S(2)}) %collective-permute-start.16) | collective-permute-done | bytes 327712 | tf_op jit(solution)/shard_map/ppermute | solution.py:573
  268.3 11.6 %collective-permute-done.27 = f32[77,640]{1,0:T(8,128)S(1)} collective-permute-done((f32[77,640]{1,0:T(8,128)S(1)}, f32[77,640]{1,0:T(8,128)S(1)}, u32[]{:S(2)}, u32[]{:S(2)}) %collective-permute-start.27) | collective-permute-done | bytes 197152 | tf_op jit(solution)/shard_map/ppermute | solution.py:569
  302.5 28.3 %collective-permute-done.28.refs_1_ = f32[256,640]{1,0:T(8,128)S(1)} collective-permute-done((f32[256,640]{1,0:T(8,128)}, f32[256,640]{1,0:T(8,128)S(1)}, u32[]{:S(2)}, u32[]{:S(2)}) %collective-permute-start.28) | collective-permute-done | bytes 655392 | tf_op jit(solution)/shard_map/ppermute | solution.py:569
  333.9 25.4 %collective-permute-done.30.refs_3_ = f32[256,640]{1,0:T(8,128)} collective-permute-done((f32[256,640]{1,0:T(8,128)}, f32[256,640]{1,0:T(8,128)}, u32[]{:S(2)}, u32[]{:S(2)}) %collective-permute-start.30) | collective-permute-done | bytes 655392 | tf_op jit(solution)/shard_map/ppermute | solution.py:569
  400.1 7.6 fusion.10
  416.8 9.9 collective-permute-start.34
  438.5 16.0 %collective-permute-done.35 = f32[64,1280]{1,0:T(8,128)S(1)} collective-permute-done((f32[64,1280]{1,0:T(8,128)S(1)}, f32[64,1280]{1,0:T(8,128)S(1)}, u32[]{:S(2)}, u32[]{:S(2)}) %collective-permute-start.35) | collective-permute-done | bytes 327712 | tf_op jit(solution)/shard_map/ppermute | solution.py:573
  465.0 8.9 fusion
  479.7 8.1 collective-permute-done.37
  489.9 12.5 %shard_map.435.refs_3_ = f32[1280,6400]{1,0:T(8,128)} custom-call(f32[256,1280]{1,0:T(8,128)S(1)} %pad_maximum_fusion.6.refs_0_, f32[256,1280]{1,0:T(8,128)S(1)} %copy-done.2, f32[256,3840]{1,0:T(8,128)} %pad_maximum_fusion.refs_2_), custom_call_target="tpu_custom_call" | custom-call | flops 7549747200 | bytes 22020096 | tf_op jit(solution)/shard_map/pallas_call | solution.py:1288
  510.8 7.7 fusion.4
  528.5 12.5 %collective-permute-start.41 = (f32[64,1280]{1,0:T(8,128)S(1)}, f32[64,1280]{1,0:T(8,128)}, u32[]{:S(2)}, u32[]{:S(2)}) collective-permute-start(f32[64,1280]{1,0:T(8,128)S(1)} %multiply_add_fusion.1), channel_id=1, source_target_pairs={{0,2},{1,3},{2,0},{3,1},{4,6},{5,7},{6,4},{7,5},{8,10},{9,11},{10,... | collective-permute-start | bytes 983048 | tf_op jit(solution)/shard_map/ppermute | solution.py:573
  545.7 11.3 %shard_map.436 = f32[1280,6400]{1,0:T(8,128)} custom-call(f32[64,1280]{1,0:T(8,128)S(1)} %fusion.62.refs_0_, f32[64,1280]{1,0:T(8,128)S(1)} %multiply_add_fusion.2.refs_1_, f32[64,2560]{1,0:T(8,128)S(1)} %concatenate.89.refs_2_, f32[1280,6400]{1,0:T(8,128)} %shard_map.435.refs_3_), custom_call_target="tpu_custom_call", output_to_operand_aliasing={{}: (3, {})} | custom-call | flops 1258291200 | bytes 14680064 | tf_op jit(solution)/shard_map/pallas_call | solution.py:1288
  563.7 11.3 %shard_map.437 = (f32[256,320]{1,0:T(8,128)}, f32[256,640]{1,0:T(8,128)}, f32[256,640]{1,0:T(8,128)}, f32[256,640]{1,0:T(8,128)}, f32[256,640]{1,0:T(8,128)}) custom-call(s32[7]{0:T(128)} %stack.68.marks, f32[256,960]{1,0:T(8,128)} %copy-done.6, f32[256,640]{1,0:T(8,128)} %slice.341.refs_0_, f32[256,640]{1,0:T(8,128)} %copy-done.37, ...), custom_call_target="tpu_custom_call" | custom-call | flops 4194304 | bytes 10485760 | tf_op jit(solution)/shard_map/pallas_call | solution.py:1242
  661.3 10.5 %shard_map.440 = f32[1280,2560]{1,0:T(8,128)} custom-call(f32[256,1280]{1,0:T(8,128)S(1)} %constant_dynamic-update-slice_fusion.2.refs_0_, f32[256,1280]{1,0:T(8,128)S(1)} %constant_dynamic-update-slice_fusion.6.refs_1_, f32[256,1280]{1,0:T(8,128)S(1)} %copy-done.3, f32[256,2560]{1,0:T(8,128)} %concatenate.93.refs_3_), custom_call_target="tpu_custom_call" | custom-call | flops 5033164800 | bytes 14680064 | tf_op jit(solution)/shard_map/pallas_call | solution.py:1288
  691.8 9.6 collective-permute-done.58
  702.1 15.4 %collective-permute-done.56.refs_2_ = f32[8,80,128]{2,1,0:T(8,128)S(1)} collective-permute-done((f32[8,80,128]{2,1,0:T(8,128)}, f32[8,80,128]{2,1,0:T(8,128)S(1)}, u32[]{:S(2)}, u32[]{:S(2)}) %collective-permute-start.56) | collective-permute-done | bytes 327712 | tf_op jit(solution)/shard_map/ppermute | solution.py:573
  718.9 20.5 %shard_map.443 = (f32[4,320,256]{2,1,0:T(8,128)}, f32[4,320,256]{2,1,0:T(8,128)}, f32[2,1152,160]{2,1,0:T(8,128)}) custom-call(s32[7]{0:T(128)} %stack.68.marks, f32[8,80,128]{2,1,0:T(8,128)} %get-tuple-element.281.refs_0_.base, f32[8,80,128]{2,1,0:T(8,128)} %copy-done.101, f32[8,80,128]{2,1,0:T(8,128)} %copy-done.102, f32[8,80,128]{2,1,0:T(8,128)} %copy-done.103, ...), custom_call_target="tpu_custom_call" | custom-call | flops 5662310400 | bytes 10485760 | tf_op jit(solution)/shard_map/pallas_call | solution.py:1242
  750.8 14.1 %collective-permute-done.60 = f32[320,256]{1,0:T(8,128)S(1)} collective-permute-done((f32[320,256]{1,0:T(8,128)S(1)}, f32[320,256]{1,0:T(8,128)S(1)}, u32[]{:S(2)}, u32[]{:S(2)}) %collective-permute-start.60) | collective-permute-done | bytes 327712 | tf_op jit(solution)/shard_map/ppermute | solution.py:569
  766.9 13.0 %collective-permute-done.62 = f32[320,256]{1,0:T(8,128)S(1)} collective-permute-done((f32[320,256]{1,0:T(8,128)S(1)}, f32[320,256]{1,0:T(8,128)S(1)}, u32[]{:S(2)}, u32[]{:S(2)}) %collective-permute-start.62) | collective-permute-done | bytes 327712 | tf_op jit(solution)/shard_map/ppermute | solution.py:569
  810.9 24.4 %shard_map.444 = (f32[8,80,128]{2,1,0:T(8,128)}, f32[8,80,128]{2,1,0:T(8,128)}, f32[8,80,128]{2,1,0:T(8,128)}, f32[8,80,128]{2,1,0:T(8,128)}, f32[2,1152,320]{2,...) custom-call(s32[7]{0:T(128)} %stack.68.marks, f32[320,256]{1,0:T(8,128)} %fusion.51.refs_0_, ...), custom_call_target="tpu_custom_call" | custom-call | flops 5662310400 | bytes 10485760 | tf_op jit(solution)/shard_map/pallas_call | solution.py:1242
  849.8 20.1 %shard_map.445 = f32[9,160,320]{2,1,0:T(8,128)} custom-call(s32[7]{0:T(128)} %stack.68.marks, f32[2,1152,160]{2,1,0:T(8,128)} %get-tuple-element.311.image, f32[2,1152,320]{2,1,0:T(8,128)} %get-tuple-element.314.cells), custom_call_target="tpu_custom_call" | custom-call | flops 5662310400 | bytes 10485760 | tf_op jit(solution)/shard_map/pallas_call | solution.py:1242
  881.4 15.6 %collective-permute-start.75 = (f32[8,160]{1,0:T(8,128)}, f32[8,160]{1,0:T(8,128)S(1)}, u32[]{:S(2)}, u32[]{:S(2)}) collective-permute-start(f32[8,160]{1,0:T(8,128)} %get-tuple-element.325.refs_0_), channel_id=1, source_target_pairs={{0,2},{1,3},{2,0},{3,1},{4,6},{5,7},{6,4},{7,5},{8,10},{9,11},{10,... | collective-permute-start | bytes 15368 | tf_op jit(solution)/shard_map/ppermute | solution.py:573
  923.7 9.9 collective-permute-done.78
  958.0 20.1 %shard_map.449 = f32[9,160,320]{2,1,0:T(8,128)} custom-call(s32[7]{0:T(128)} %stack.68.marks, f32[2,1152,160]{2,1,0:T(8,128)} %get-tuple-element.333.image, f32[2,1152,320]{2,1,0:T(8,128)} %get-tuple-element.334.cells), custom_call_target="tpu_custom_call" | custom-call | flops 5662310400 | bytes 10485760 | tf_op jit(solution)/shard_map/pallas_call | solution.py:1242
  (596 shorter events, 518.3 us)
Async XLA Ops:
  7.2 112.8 %all-gather.4.cloned.1.call-start = ((), (), s32[]{:S(2)}) async-start(), calls=%async_computation.12 | async-start | bytes 10321920 | tf_op jit(solution)/shard_map/all_gather | solution.py:1448
  18.5 32.6 %all-to-all-start = ((f32[8,320,128]{2,1,0:T(8,128)}), f32[8,320,128]{2,1,0:T(8,128)S(1)}, u32[]{:S(2)}, u32[]{:S(2)}) async-start(f32[8,320,128]{2,1,0:T(8,128)} %shard_map.425), calls=%async_computation | async-start | bytes 2621440 | tf_op jit(solution)/shard_map/all_to_all | solution.py:628
  23.5 224.9 %all-gather.6.cloned.1.call-start = ((), (), s32[]{:S(2)}) async-start(), calls=%async_computation.13 | async-start | bytes 22118400 | tf_op jit(solution)/shard_map/all_gather | solution.py:1448
  23.8 47.5 %collective-permute-start.1 = (f32[168,960]{1,0:T(8,128)S(1)}, f32[168,960]{1,0:T(8,128)S(1)}, u32[]{:S(2)}, u32[]{:S(2)}) collective-permute-start(f32[168,960]{1,0:T(8,128)S(1)} %select_maximum_fusion.refs_0_), channel_id=1, source_target_pairs={{0,3},{1,0},{2,1},{3,2},{4,7},{5,4},{6,5},{7,6},{8,11},{9,8},{10,9... | collective-permute-start | bytes 1935368 | tf_op jit(solution)/shard_map/ppermute | solution.py:573
  27.4 59.6 %collective-permute-start.2 = (f32[168,960]{1,0:T(8,128)S(1)}, f32[168,960]{1,0:T(8,128)}, u32[]{:S(2)}, u32[]{:S(2)}) collective-permute-start(f32[168,960]{1,0:T(8,128)S(1)} %select_maximum_fusion.refs_0_), channel_id=1, source_target_pairs={{0,2},{1,3},{2,0},{3,1},{4,6},{5,7},{6,4},{7,5},{8,10},{9,11},{10,... | collective-permute-start | bytes 1935368 | tf_op jit(solution)/shard_map/ppermute | solution.py:573
  27.4 59.6 %collective-permute-start.3 = (f32[168,960]{1,0:T(8,128)S(1)}, f32[168,960]{1,0:T(8,128)}, u32[]{:S(2)}, u32[]{:S(2)}) collective-permute-start(f32[168,960]{1,0:T(8,128)S(1)} %select_maximum_fusion.refs_0_), channel_id=1, source_target_pairs={{0,1},{1,2},{2,3},{3,0},{4,5},{5,6},{6,7},{7,4},{8,9},{9,10},{10,1... | collective-permute-start | bytes 1935368 | tf_op jit(solution)/shard_map/ppermute | solution.py:573
  114.5 272.3 %all-gather.8.cloned.1.call-start = ((), (), s32[]{:S(2)}) async-start(), calls=%async_computation.14 | async-start | bytes 22118400 | tf_op jit(solution)/shard_map/all_gather | solution.py:1448
  125.2 42.9 %all-to-all-start.1 = ((f32[4,64,1600]{2,1,0:T(8,128)}), f32[4,64,1600]{2,1,0:T(8,128)S(1)}, u32[]{:S(2)}, u32[]{:S(2)}) async-start(f32[4,64,1600]{2,1,0:T(8,128)} %bitcast.175), calls=%async_computation.1 | async-start | bytes 3407872 | tf_op jit(solution)/shard_map/all_to_all | solution.py:589
  131.2 30.1 %collective-permute-start.10 = (f32[320,256]{1,0:T(8,128)}, f32[320,256]{1,0:T(8,128)}, u32[]{:S(2)}, u32[]{:S(2)}) collective-permute-start(f32[320,256]{1,0:T(8,128)} %fusion.57.refs_0_.refs_8_), channel_id=1, source_target_pairs={{0,12},{4,8},{8,4},{12,0},{1,13},{5,9},{9,5},{13,1},{2,14},{6,10},... | collective-permute-start | bytes 983048 | tf_op jit(solution)/shard_map/ppermute | solution.py:569
  132.9 31.5 %collective-permute-start.11 = (f32[320,256]{1,0:T(8,128)}, f32[320,256]{1,0:T(8,128)}, u32[]{:S(2)}, u32[]{:S(2)}) collective-permute-start(f32[320,256]{1,0:T(8,128)} %fusion.57.refs_0_.refs_8_), channel_id=1, source_target_pairs={{0,16},{16,0},{1,17},{17,1},{2,18},{18,2},{3,19},{19,3},{4,20},{20... | collective-permute-start | bytes 983048 | tf_op jit(solution)/shard_map/ppermute | solution.py:565
  194.7 43.1 %collective-permute-start.24 = (f32[77,256]{1,0:T(8,128)S(1)}, f32[77,256]{1,0:T(8,128)S(1)}, u32[]{:S(2)}, u32[]{:S(2)}) collective-permute-start(f32[77,256]{1,0:T(8,128)S(1)} %constant_dynamic-slice_fusion.5), channel_id=1, source_target_pairs={{0,16},{16,0},{1,17},{17,1},{2,18},{18,2},{3,19},{19,3},{4,20},{20... | collective-permute-start | bytes 236552 | tf_op jit(solution)/shard_map/ppermute | solution.py:565
  294.4 64.9 %all-to-all-start.4 = ((f32[4,104,1280]{2,1,0:T(8,128)}), f32[4,104,1280]{2,1,0:T(8,128)}, u32[]{:S(2)}, u32[]{:S(2)}) async-start(f32[4,104,1280]{2,1,0:T(8,128)} %broadcast_in_dim.21), calls=%async_computation.4 | async-start | bytes 4259840 | tf_op jit(solution)/shard_map/all_to_all | solution.py:589
  298.9 500.9 %reduce-scatter.3.cloned.1.call-start = ((), (), s32[]{:S(2)}) async-start(), calls=%async_computation.15 | async-start | bytes 36864000 | tf_op jit(solution)/shard_map/reduce_scatter | solution.py:1452
  298.9 31.9 %collective-permute-start.28 = (f32[256,640]{1,0:T(8,128)}, f32[256,640]{1,0:T(8,128)S(1)}, u32[]{:S(2)}, u32[]{:S(2)}) collective-permute-start(f32[256,640]{1,0:T(8,128)} %slice.341.refs_0_), channel_id=1, source_target_pairs={{0,4},{4,0},{8,12},{12,8},{1,5},{5,1},{9,13},{13,9},{2,6},{6,2},{1... | collective-permute-start | bytes 1966088 | tf_op jit(solution)/shard_map/ppermute | solution.py:569
  300.8 33.1 %collective-permute-start.29 = (f32[256,640]{1,0:T(8,128)}, f32[256,640]{1,0:T(8,128)}, u32[]{:S(2)}, u32[]{:S(2)}) collective-permute-start(f32[256,640]{1,0:T(8,128)} %slice.341.refs_0_), channel_id=1, source_target_pairs={{0,8},{4,12},{8,0},{12,4},{1,9},{5,13},{9,1},{13,5},{2,10},{6,14},... | collective-permute-start | bytes 1966088 | tf_op jit(solution)/shard_map/ppermute | solution.py:569
  301.5 57.8 %collective-permute-start.30 = (f32[256,640]{1,0:T(8,128)}, f32[256,640]{1,0:T(8,128)}, u32[]{:S(2)}, u32[]{:S(2)}) collective-permute-start(f32[256,640]{1,0:T(8,128)} %slice.341.refs_0_), channel_id=1, source_target_pairs={{0,12},{4,8},{8,4},{12,0},{1,13},{5,9},{9,5},{13,1},{2,14},{6,10},... | collective-permute-start | bytes 1966088 | tf_op jit(solution)/shard_map/ppermute | solution.py:569
  475.8 33.4 %collective-permute-start.38 = (f32[64,1280]{1,0:T(8,128)S(1)}, f32[64,1280]{1,0:T(8,128)S(1)}, u32[]{:S(2)}, u32[]{:S(2)}) collective-permute-start(f32[64,1280]{1,0:T(8,128)S(1)} %get-tuple-element.432), channel_id=1, source_target_pairs={{0,2},{1,3},{2,0},{3,1},{4,6},{5,7},{6,4},{7,5},{8,10},{9,11},{10,... | collective-permute-start | bytes 983048 | tf_op jit(solution)/shard_map/ppermute | solution.py:573
  476.1 33.1 %collective-permute-start.39 = (f32[64,1280]{1,0:T(8,128)S(1)}, f32[64,1280]{1,0:T(8,128)S(1)}, u32[]{:S(2)}, u32[]{:S(2)}) collective-permute-start(f32[64,1280]{1,0:T(8,128)S(1)} %get-tuple-element.431), channel_id=1, source_target_pairs={{0,3},{1,0},{2,1},{3,2},{4,7},{5,4},{6,5},{7,6},{8,11},{9,8},{10,9... | collective-permute-start | bytes 983048 | tf_op jit(solution)/shard_map/ppermute | solution.py:573
  584.4 49.2 %all-to-all-start.5 = ((f32[4,64,1280]{2,1,0:T(8,128)}), f32[4,64,1280]{2,1,0:T(8,128)}, u32[]{:S(2)}, u32[]{:S(2)}) async-start(f32[4,64,1280]{2,1,0:T(8,128)} %bitcast.185), calls=%async_computation.5 | async-start | bytes 2621440 | tf_op jit(solution)/shard_map/all_to_all | solution.py:589
  633.7 38.1 %collective-permute-start.49 = (f32[40,1280]{1,0:T(8,128)}, f32[40,1280]{1,0:T(8,128)S(1)}, u32[]{:S(2)}, u32[]{:S(2)}) collective-permute-start(f32[40,1280]{1,0:T(8,128)} %get-tuple-element.272), channel_id=1, source_target_pairs={{0,1},{1,2},{2,3},{3,0},{4,5},{5,6},{6,7},{7,4},{8,9},{9,10},{10,1... | collective-permute-start | bytes 614408 | tf_op jit(solution)/shard_map/ppermute | solution.py:573
  639.7 32.0 %collective-permute-start.50 = (f32[40,1280]{1,0:T(8,128)}, f32[40,1280]{1,0:T(8,128)}, u32[]{:S(2)}, u32[]{:S(2)}) collective-permute-start(f32[40,1280]{1,0:T(8,128)} %get-tuple-element.273), channel_id=1, source_target_pairs={{0,2},{1,3},{2,0},{3,1},{4,6},{5,7},{6,4},{7,5},{8,10},{9,11},{10,... | collective-permute-start | bytes 614408 | tf_op jit(solution)/shard_map/ppermute | solution.py:573
  641.8 30.6 %collective-permute-start.51 = (f32[40,1280]{1,0:T(8,128)}, f32[40,1280]{1,0:T(8,128)}, u32[]{:S(2)}, u32[]{:S(2)}) collective-permute-start(f32[40,1280]{1,0:T(8,128)} %get-tuple-element.274), channel_id=1, source_target_pairs={{0,3},{1,0},{2,1},{3,2},{4,7},{5,4},{6,5},{7,6},{8,11},{9,8},{10,9... | collective-permute-start | bytes 614408 | tf_op jit(solution)/shard_map/ppermute | solution.py:573
  659.7 250.5 %reduce-scatter.5.cloned.1.call-start = ((), (), s32[]{:S(2)}) async-start(), calls=%async_computation.16 | async-start | bytes 14745600 | tf_op jit(solution)/shard_map/reduce_scatter | solution.py:1452
  743.5 55.4 %all-to-all-start.7 = ((f32[4,72,1600]{2,1,0:T(8,128)}), f32[4,72,1600]{2,1,0:T(8,128)S(1)}, u32[]{:S(2)}, u32[]{:S(2)}) async-start(f32[4,72,1600]{2,1,0:T(8,128)} %pad_maximum_fusion.3), calls=%async_computation.7 | async-start | bytes 3833856 | tf_op jit(solution)/shard_map/all_to_all | solution.py:589
  750.5 29.4 %collective-permute-start.62 = (f32[320,256]{1,0:T(8,128)S(1)}, f32[320,256]{1,0:T(8,128)S(1)}, u32[]{:S(2)}, u32[]{:S(2)}) collective-permute-start(f32[320,256]{1,0:T(8,128)S(1)} %get-tuple-element.426), channel_id=1, source_target_pairs={{0,12},{4,8},{8,4},{12,0},{1,13},{5,9},{9,5},{13,1},{2,14},{6,10},... | collective-permute-start | bytes 983048 | tf_op jit(solution)/shard_map/ppermute | solution.py:569
  805.3 65.3 %all-to-all-start.8 = ((f32[4,160,640]{2,1,0:T(8,128)}), f32[4,160,640]{2,1,0:T(8,128)S(1)}, u32[]{:S(2)}, u32[]{:S(2)}) async-start(f32[4,160,640]{2,1,0:T(8,128)} %pad_maximum_fusion.5), calls=%async_computation.9 | async-start | bytes 3276800 | tf_op jit(solution)/shard_map/all_to_all | solution.py:589
  837.4 34.0 %collective-permute-start.71 = (f32[8,80,128]{2,1,0:T(8,128)}, f32[8,80,128]{2,1,0:T(8,128)}, u32[]{:S(2)}, u32[]{:S(2)}) collective-permute-start(f32[8,80,128]{2,1,0:T(8,128)} %get-tuple-element.309), channel_id=1, source_target_pairs={{0,2},{1,3},{2,0},{3,1},{4,6},{5,7},{6,4},{7,5},{8,10},{9,11},{10,... | collective-permute-start | bytes 983048 | tf_op jit(solution)/shard_map/ppermute | solution.py:573
  839.7 31.7 %collective-permute-start.72 = (f32[8,80,128]{2,1,0:T(8,128)}, f32[8,80,128]{2,1,0:T(8,128)}, u32[]{:S(2)}, u32[]{:S(2)}) collective-permute-start(f32[8,80,128]{2,1,0:T(8,128)} %get-tuple-element.310), channel_id=1, source_target_pairs={{0,3},{1,0},{2,1},{3,2},{4,7},{5,4},{6,5},{7,6},{8,11},{9,8},{10,9... | collective-permute-start | bytes 983048 | tf_op jit(solution)/shard_map/ppermute | solution.py:573
  938.0 44.7 %collective-permute-start.81 = (f32[64,1280]{1,0:T(8,128)}, f32[64,1280]{1,0:T(8,128)}, u32[]{:S(2)}, u32[]{:S(2)}) collective-permute-start(f32[64,1280]{1,0:T(8,128)} %shard_map.448.refs_0_), channel_id=1, source_target_pairs={{0,3},{1,0},{2,1},{3,2},{4,7},{5,4},{6,5},{7,6},{8,11},{9,8},{10,9... | collective-permute-start | bytes 983048 | tf_op jit(solution)/shard_map/ppermute | solution.py:573
  942.3 41.3 %collective-permute-start.82 = (f32[64,1280]{1,0:T(8,128)}, f32[64,1280]{1,0:T(8,128)}, u32[]{:S(2)}, u32[]{:S(2)}) collective-permute-start(f32[64,1280]{1,0:T(8,128)} %shard_map.448.refs_0_), channel_id=1, source_target_pairs={{0,2},{1,3},{2,0},{3,1},{4,6},{5,7},{6,4},{7,5},{8,10},{9,11},{10,... | collective-permute-start | bytes 983048 | tf_op jit(solution)/shard_map/ppermute | solution.py:573
  944.5 39.1 %collective-permute-start.83 = (f32[64,1280]{1,0:T(8,128)}, f32[64,1280]{1,0:T(8,128)}, u32[]{:S(2)}, u32[]{:S(2)}) collective-permute-start(f32[64,1280]{1,0:T(8,128)} %shard_map.448.refs_0_), channel_id=1, source_target_pairs={{0,1},{1,2},{2,3},{3,0},{4,5},{5,6},{6,7},{7,4},{8,9},{9,10},{10,1... | collective-permute-start | bytes 983048 | tf_op jit(solution)/shard_map/ppermute | solution.py:573
  947.9 30.2 %collective-permute-start.84 = (f32[4,160,320]{2,1,0:T(8,128)}, f32[4,160,320]{2,1,0:T(8,128)}, u32[]{:S(2)}, u32[]{:S(2)}) collective-permute-start(f32[4,160,320]{2,1,0:T(8,128)} %dynamic-slice_bitcast_fusion), channel_id=1, source_target_pairs={{0,16},{16,0},{1,17},{17,1},{2,18},{18,2},{3,19},{19,3},{4,20},{20... | collective-permute-start | bytes 2457608 | tf_op jit(solution)/shard_map/ppermute | solution.py:565
  (177 other events, 2403.1 us)
Sparse Core Ops, SparseCore 0:
  10.7 74.4 all-gather.3
  114.7 115.5 all-gather.5
  232.1 137.5 all-gather.7
  557.2 224.2 reduce-scatter.2
  784.9 95.1 reduce-scatter.4

commit v3 on v2

--- a/solution.py
+++ b/solution.py
@@ -1531,7 +1531,7 @@
     own_third = jnp.concatenate(
         [own_third, jnp.pad(gain_attn_norm[None, :], ((0, 7), (0, 640)))], axis=0
     )
-    third_pieces = z_pieces(own_third)
+    third_pieces = [own_third, turn(own_third, 3), turn(own_third[:, :512], 2), turn(own_third, 1)]
 
     features = jax.nn.silu(time_features(times, channels))
     own_features = lax.dynamic_slice_in_dim(features, block * width, width, 1)
@@ -1543,6 +1543,8 @@
     own_one, other_one, *third_pieces = together(own_one, other_one, *third_pieces)
     own_one = own_one + swap(other_one)
     strips_one, part = plane_sum(own_one)
+    third_rest = turn(own_third[:, 512:], 2)
+    third_pieces[2] = jnp.concatenate([third_pieces[2], third_rest], axis=1)
     third, gain_attn_full = small(
         third_kernel, marks, after(third_pieces, part), [(160, 3840), (1, channels)]
     )
@@ -1716,7 +1718,7 @@
     (grad_three,) = small(pack_kernel, marks, (grad_norm_three,), [(8, 80, 128)])
     grad_three_q = plane_exchange(grad_three)
     out_sum = jnp.sum(after(out_sum, grad_three), axis=0)
-    text_grads = total_of(z_received(text_grads))
+    text_grads = total_of(z_received(after(text_grads, grad_three)))
     attn_right = jnp.concatenate(
         [
             jnp.concatenate([grad_qkv, attn_self], axis=1),
@@ -1767,12 +1769,9 @@
     after_ff_all = side_here[:, :64, :channels].reshape(256, channels)
     residual_all = side_here[:, :64, channels:].reshape(256, wide)
     gain_sums = jnp.sum(side_here[:, 64:67, :channels], axis=0)
-    cross_cut = after(cross_grads, part)
-    cross_cut = jnp.stack([cross_cut[:, 640 * k : 640 * k + 640] for k in range(4)])
-    *grad_act_two, after_ff_all, gain_sums, residual_all, cross_cut = together(
-        *grad_act_two, after_ff_all, gain_sums, residual_all, cross_cut
-    )
-    cross_shares = z_all(cross_cut)
+    *grad_act_two, after_ff_all, gain_sums, residual_all = together(
+        *grad_act_two, after_ff_all, gain_sums, residual_all
+    )
 
     *grad_act_one, image_grad, grad_tau, grad_gain_mid = first_conv_back(
         marks,
@@ -1786,9 +1785,12 @@
     image_grad, text_grads = after((image_grad, text_grads), grad_act_pieces[1])
     text_grads = text_grads + flip(text_grads, 2)
     grad_conv_first = conv_weight(marks, image_one, image_grad, 1)
-    cross_shares = jnp.sum(after(cross_shares, grad_act_pieces[1]), axis=0)
-    *grad_act_pieces, grad_conv_first, cross_shares, text_grads = together(
-        *grad_act_pieces, grad_conv_first, cross_shares, text_grads
+    cross_cut = after(cross_grads, grad_act_pieces[1])
+    cross_cut = [
+        lax.dynamic_slice_in_dim(cross_cut, lax.rem(t + j, 4) * 640, 640, 1) for j in range(4)
+    ]
+    *grad_act_pieces, grad_conv_first, text_grads, cross_cut = together(
+        *grad_act_pieces, grad_conv_first, text_grads, cross_cut
     )
     grad_conv_first = grad_conv_first.reshape(3, 3, width, wide)
     extra = jnp.concatenate(
@@ -1807,6 +1809,7 @@
         (source, gain_in[None, :], stats_one, *grad_act_pieces),
         [(8, 80, 128), (8, width)],
     )
+    cross_shares = total_of(z_received(after(cross_cut, grad_input_q)))
     moved, grad_gain_in = small(
         input_back_kernel,
         marks,
@@ -1822,21 +1825,24 @@
         [(8, 88, 128), (8, width)],
     )
     received = plane_exchange(moved)
-    attn_grads, text_grads = after((attn_grads, text_grads), moved)
-    text_other_grads = swap(text_grads)
+    text_grads, image_back, after_ff_here, attn_grads = after(
+        (text_grads, image_back, after_ff_all, attn_grads), moved
+    )
     proj_cut = attn_grads[:, 1280:].reshape(width, 4, wide)
     proj_share = total_of(z_received([pick(proj_cut, lax.rem(t + j, 4), 1) for j in range(4)]))
-    received, proj_share, text_other_grads = together(received, proj_share, text_other_grads)
+    text_other_grads = swap(text_grads)
+    grad_proj_out = mm(after_ff_here, cot, 0, 0).reshape(2, 4, width, wide)
+    grad_proj_own = pick(grad_proj_out, item) + swap(pick(grad_proj_out, 1 - item))
+    grad_conv_second = conv_weight(marks, image_back, image_two, -1)
+    received, cross_shares, proj_share, text_other_grads, grad_proj_own, grad_conv_second = together(
+        received, cross_shares, proj_share, text_other_grads, grad_proj_own, grad_conv_second
+    )
+    grad_conv_second = grad_conv_second.reshape(3, 3, width, wide).transpose(0, 1, 3, 2)
     text_grads, text_other_grads = unfolded(text_grads), unfolded(text_other_grads)
     (grad_hidden,) = small(unpack_kernel, marks, (received,), [(64, channels)])
     hidden_pieces = z_pieces(grad_hidden)
-    after_ff_all, image_back = after((after_ff_all, image_back), grad_hidden)
-    grad_proj_out = mm(after_ff_all, cot, 0, 0).reshape(2, 4, width, wide)
-    grad_proj_own = pick(grad_proj_out, item) + swap(pick(grad_proj_out, 1 - item))
+    after_ff_all, grad_proj_own = after((after_ff_all, grad_proj_own), grad_hidden)
     grad_proj_out = h_collect([pick(grad_proj_own, h ^ j) for j in range(4)])
-    grad_conv_second = conv_weight(marks, image_back, image_two, -1)
-    *hidden_pieces, grad_conv_second = together(*hidden_pieces, grad_conv_second)
-    grad_conv_second = grad_conv_second.reshape(3, 3, width, wide).transpose(0, 1, 3, 2)
     output = residual_all + mm(after_ff_all, proj_out_full, 1, 0)
     output = output * own_valid
     grad_text_weight = mm(text_own, text_grads, 0, 0) + mm(text_other, text_other_grads, 0, 0)

time: 1010 us -> 985 us (0.975)
  waiting for transfers between devices: 338 us -> 312 us
    ppermute x25, waiting for transfers between devices: 183 us -> 161 us  [flip(): return lax.ppermute(values, H, [(s, s ^ step) for s in range(4)])]
    ppermute x48 -> x52, waiting for transfers between devices: 122 us -> 116 us  [turn(): return lax.ppermute(values, T, [(s, (s + step) % 4) for s in range(4)])]
    unnamed x225 -> x227, local copies, waits for them, and re-layouts: 25.1 us -> 29.5 us
    ppermute x48 -> x52, starting transfers between devices: 123 us -> 124 us  [turn(): return lax.ppermute(values, T, [(s, (s + step) % 4) for s in range(4)])]
    all_to_all x5 -> x4, starting transfers between devices: 21.8 us -> 22 us  [z_all(): return lax.all_to_all(values, T, 0, 0)]
  transfers between devices with their start and end apart: 103 -> 106, of which waited for: 45 -> 44; matrix products, arithmetic and copies ran while one was open for 15% -> 15% of each run, Pallas kernels for 21% -> 22%
where the time goes in v3:
time: 985 us; the launch traced here: 974 us
  waiting for transfers between devices  312 us (32%)
  Pallas kernels  218 us (22%)
  starting transfers between devices  199 us (20%)
  matrix products  108 us (11%)
  local copies, waits for them, and re-layouts  80.1 us (8%)
  other arithmetic  39.3 us (4%)
  between operations  17.7 us (2%)
    pallas_call x23, Pallas kernels, run_kernel(): pl.pallas_call(body, out_shape=[jax.ShapeDtypeStruct(shape, jnp.float32)...  184 us
    ppermute x25, waiting for transfers between devices, flip(): return lax.ppermute(values, H, [(s, s ^ step) for s in range(4)])  161 us
    ppermute x52, starting transfers between devices, turn(): return lax.ppermute(values, T, [(s, (s + step) % 4) for s in range(4)])  124 us
    ppermute x52, waiting for transfers between devices, turn(): return lax.ppermute(values, T, [(s, (s + step) % 4) for s in range(4)])  116 us
    dot_general x23, matrix products, mm(): lax.dot_general(left, right, (((left_dim,), (right_dim,)), ((), ())), pre...  101 us
    pallas_call x3, Pallas kernels, weight_grads(): pl.pallas_call(functools.partial(weight_kernel, plan), out_shape=jax.Shap...  34.1 us
    ppermute x25, starting transfers between devices, flip(): return lax.ppermute(values, H, [(s, s ^ step) for s in range(4)])  30.6 us
    unnamed x227, local copies, waits for them, and re-layouts  29.5 us
  transfers between devices with their start and end apart: 106, of which 44 were waited for; matrix products, arithmetic and copies ran while one was open for 15% of the time, Pallas kernels for 22%

profile of v3, /device:TPU:0, one launch (start us, length us, event | category | flops | bytes accessed | tf_op | source)
XLA Modules:
  0.0 973.5 jit_solution(4983260800543920406)
XLA Ops:
  32.9 18.3 %all-to-all-done.source = f32[8,320,128]{2,1,0:T(8,128)S(1)} async-done(((f32[8,320,128]{2,1,0:T(8,128)}), f32[8,320,128]{2,1,0:T(8,128)S(1)}, u32[]{:S(2)}, u32[]{:S(2)}) %all-to-all-start) | async-done | bytes 1310752 | tf_op jit(solution)/shard_map/all_to_all | solution.py:628
  52.2 19.1 %shard_map.426 = (f32[4,320,256]{2,1,0:T(8,128)}, f32[4,320,256]{2,1,0:T(8,128)}, f32[2,1152,160]{2,1,0:T(8,128)}, f32[2,8,160]{2,1,0:T(8,128)}) custom-call(s32[7]{0:T(128)} %stack.53.marks, f32[8,320,128]{2,1,0:T(8,128)} %copy-done.5, f32[1,160]{1,0:T(1,128)} %bitcast.202, f32[2,320]{1,0:T(2,128)} %fusion.82.tau, f32[1440,320]{1,0:T(8,128)} %bitcast.215), custom_call_target="tpu_custom_call" | custom-call | flops 5662310400 | bytes 10485760 | tf_op jit(solution)/shard_map/pallas_call | solution.py:1242
  80.7 10.5 %collective-permute-done.21 = f32[168,448]{1,0:T(8,128)S(1)} collective-permute-done((f32[168,448]{1,0:T(8,128)S(1)}, f32[168,448]{1,0:T(8,128)S(1)}, u32[]{:S(2)}, u32[]{:S(2)}) %collective-permute-start.21) | collective-permute-done | bytes 301088 | tf_op jit(solution)/shard_map/ppermute | solution.py:573
  121.6 14.4 %collective-permute-done.8.refs_1_.refs_9_ = f32[320,256]{1,0:T(8,128)} collective-permute-done((f32[320,256]{1,0:T(8,128)}, f32[320,256]{1,0:T(8,128)}, u32[]{:S(2)}, u32[]{:S(2)}) %collective-permute-start.8) | collective-permute-done | bytes 327712 | tf_op jit(solution)/shard_map/ppermute | solution.py:569
  136.7 12.6 %collective-permute-done.10.refs_3_.refs_11_ = f32[320,256]{1,0:T(8,128)} collective-permute-done((f32[320,256]{1,0:T(8,128)}, f32[320,256]{1,0:T(8,128)}, u32[]{:S(2)}, u32[]{:S(2)}) %collective-permute-start.10) | collective-permute-done | bytes 327712 | tf_op jit(solution)/shard_map/ppermute | solution.py:569
  157.8 21.6 %shard_map.427 = (f32[8,80,128]{2,1,0:T(8,128)}, f32[8,80,128]{2,1,0:T(8,128)}, f32[8,80,128]{2,1,0:T(8,128)}, f32[8,80,128]{2,1,0:T(8,128)}, f32[2,1152,320]{2,1,0:T(8,128)}, /*index=5*/f32[2,8,320]{2,1,0:T(8,128)}) custom-call(s32[7]{0:T(128)} %stack.53.marks, f32[320,256]{1,0:T(8,128)} %fusion.57.refs_0_.refs_8_, ...), custom_call_target="tpu_custom_call" | custom-call | flops 5662310400 | bytes 10485760 | tf_op jit(solution)/shard_map/pallas_call | solution.py:1242
  184.8 7.5 collective-permute-done.15.second
  192.2 12.0 %collective-permute-done.16.third = f32[8,80,128]{2,1,0:T(8,128)S(1)} collective-permute-done((f32[8,80,128]{2,1,0:T(8,128)}, f32[8,80,128]{2,1,0:T(8,128)S(1)}, u32[]{:S(2)}, u32[]{:S(2)}) %collective-permute-start.16) | collective-permute-done | bytes 327712 | tf_op jit(solution)/shard_map/ppermute | solution.py:573
  229.8 7.7 all-to-all-done.2.packed
  260.7 8.3 collective-permute-done.28
  292.9 28.1 %collective-permute-done.29.refs_1_ = f32[256,640]{1,0:T(8,128)S(1)} collective-permute-done((f32[256,640]{1,0:T(8,128)S(1)}, f32[256,640]{1,0:T(8,128)S(1)}, u32[]{:S(2)}, u32[]{:S(2)}) %collective-permute-start.29) | collective-permute-done | bytes 655392 | tf_op jit(solution)/shard_map/ppermute | solution.py:569
  325.4 22.7 %collective-permute-done.31.refs_3_ = f32[256,640]{1,0:T(8,128)} collective-permute-done((f32[256,640]{1,0:T(8,128)S(1)}, f32[256,640]{1,0:T(8,128)}, u32[]{:S(2)}, u32[]{:S(2)}) %collective-permute-start.31) | collective-permute-done | bytes 655392 | tf_op jit(solution)/shard_map/ppermute | solution.py:569
  387.4 7.6 fusion.10
  404.1 9.8 %collective-permute-start.35 = (f32[64,1280]{1,0:T(8,128)S(1)}, f32[64,1280]{1,0:T(8,128)S(1)}, u32[]{:S(2)}, u32[]{:S(2)}) collective-permute-start(f32[64,1280]{1,0:T(8,128)S(1)} %fusion.63), channel_id=1, source_target_pairs={{0,3},{1,0},{2,1},{3,2},{4,7},{5,4},{6,5},{7,6},{8,11},{9,8},{10,9... | collective-permute-start | bytes 983048 | tf_op jit(solution)/shard_map/ppermute | solution.py:573
  423.5 18.2 %collective-permute-done.36 = f32[64,1280]{1,0:T(8,128)S(1)} collective-permute-done((f32[64,1280]{1,0:T(8,128)S(1)}, f32[64,1280]{1,0:T(8,128)S(1)}, u32[]{:S(2)}, u32[]{:S(2)}) %collective-permute-start.36) | collective-permute-done | bytes 327712 | tf_op jit(solution)/shard_map/ppermute | solution.py:573
  452.3 8.9 fusion
  467.1 8.1 collective-permute-done.38
  477.4 12.5 %shard_map.435.refs_3_ = f32[1280,6400]{1,0:T(8,128)} custom-call(f32[256,1280]{1,0:T(8,128)S(1)} %pad_maximum_fusion.5.refs_0_, f32[256,1280]{1,0:T(8,128)S(1)} %copy-done.2, f32[256,3840]{1,0:T(8,128)} %pad_maximum_fusion.refs_2_), custom_call_target="tpu_custom_call" | custom-call | flops 7549747200 | bytes 22020096 | tf_op jit(solution)/shard_map/pallas_call | solution.py:1288
  498.1 7.6 fusion.4
  517.6 12.9 %collective-permute-start.42 = (f32[64,1280]{1,0:T(8,128)}, f32[64,1280]{1,0:T(8,128)}, u32[]{:S(2)}, u32[]{:S(2)}) collective-permute-start(f32[64,1280]{1,0:T(8,128)} %multiply_add_fusion.1), channel_id=1, source_target_pairs={{0,2},{1,3},{2,0},{3,1},{4,6},{5,7},{6,4},{7,5},{8,10},{9,11},{10,... | collective-permute-start | bytes 983048 | tf_op jit(solution)/shard_map/ppermute | solution.py:573
  534.1 11.2 %shard_map.436 = f32[1280,6400]{1,0:T(8,128)} custom-call(f32[64,1280]{1,0:T(8,128)S(1)} %fusion.62.refs_0_, f32[64,1280]{1,0:T(8,128)S(1)} %multiply_add_fusion.2.refs_1_, f32[64,2560]{1,0:T(8,128)S(1)} %concatenate.93.refs_2_, f32[1280,6400]{1,0:T(8,128)} %shard_map.435.refs_3_), custom_call_target="tpu_custom_call", output_to_operand_aliasing={{}: (3, {})} | custom-call | flops 1258291200 | bytes 14680064 | tf_op jit(solution)/shard_map/pallas_call | solution.py:1288
  552.9 11.3 %shard_map.437 = (f32[256,320]{1,0:T(8,128)}, f32[256,640]{1,0:T(8,128)}, f32[256,640]{1,0:T(8,128)}, f32[256,640]{1,0:T(8,128)}, f32[256,640]{1,0:T(8,128)}) custom-call(s32[7]{0:T(128)} %stack.53.marks, f32[256,960]{1,0:T(8,128)} %copy-done.6, f32[256,640]{1,0:T(8,128)} %copy-done.23, f32[256,640]{1,0:T(8,128)} %copy-done.36, f32[256,640]{1,0:T(8,128)} %copy-done.37, ...), custom_call_target="tpu_custom_call" | custom-call | flops 4194304 | bytes 10485760 | tf_op jit(solution)/shard_map/pallas_call | solution.py:1242
  646.3 10.4 %shard_map.440 = f32[1280,2560]{1,0:T(8,128)} custom-call(f32[256,1280]{1,0:T(8,128)S(1)} %constant_dynamic-update-slice_fusion.2.refs_0_, f32[256,1280]{1,0:T(8,128)S(1)} %constant_dynamic-update-slice_fusion.6.refs_1_, f32[256,1280]{1,0:T(8,128)S(1)} %copy-done.3, f32[256,2560]{1,0:T(8,128)} %concatenate.97.refs_3_), custom_call_target="tpu_custom_call" | custom-call | flops 5033164800 | bytes 14680064 | tf_op jit(solution)/shard_map/pallas_call | solution.py:1288
  682.6 9.5 collective-permute-done.59
  692.8 13.7 %collective-permute-done.57.refs_2_ = f32[8,80,128]{2,1,0:T(8,128)S(1)} collective-permute-done((f32[8,80,128]{2,1,0:T(8,128)}, f32[8,80,128]{2,1,0:T(8,128)S(1)}, u32[]{:S(2)}, u32[]{:S(2)}) %collective-permute-start.57) | collective-permute-done | bytes 327712 | tf_op jit(solution)/shard_map/ppermute | solution.py:573
  708.0 19.8 %shard_map.443 = (f32[4,320,256]{2,1,0:T(8,128)}, f32[4,320,256]{2,1,0:T(8,128)}, f32[2,1152,160]{2,1,0:T(8,128)}) custom-call(s32[7]{0:T(128)} %stack.53.marks, f32[8,80,128]{2,1,0:T(8,128)} %get-tuple-element.294.refs_0_.base, f32[8,80,128]{2,1,0:T(8,128)} %copy-done.102, f32[8,80,128]{2,1,0:T(8,128)} %copy-done.103, f32[8,80,128]{2,1,0:T(8,128)} %copy-done.104, ...), custom_call_target="tpu_custom_call" | custom-call | flops 5662310400 | bytes 10485760 | tf_op jit(solution)/shard_map/pallas_call | solution.py:1242
  739.3 14.1 %collective-permute-done.61 = f32[320,256]{1,0:T(8,128)S(1)} collective-permute-done((f32[320,256]{1,0:T(8,128)S(1)}, f32[320,256]{1,0:T(8,128)S(1)}, u32[]{:S(2)}, u32[]{:S(2)}) %collective-permute-start.61) | collective-permute-done | bytes 327712 | tf_op jit(solution)/shard_map/ppermute | solution.py:569
  755.2 12.6 %collective-permute-done.63 = f32[320,256]{1,0:T(8,128)S(1)} collective-permute-done((f32[320,256]{1,0:T(8,128)S(1)}, f32[320,256]{1,0:T(8,128)S(1)}, u32[]{:S(2)}, u32[]{:S(2)}) %collective-permute-start.63) | collective-permute-done | bytes 327712 | tf_op jit(solution)/shard_map/ppermute | solution.py:569
  789.8 26.1 %shard_map.444 = (f32[8,80,128]{2,1,0:T(8,128)}, f32[8,80,128]{2,1,0:T(8,128)}, f32[8,80,128]{2,1,0:T(8,128)}, f32[8,80,128]{2,1,0:T(8,128)}, f32[2,1152,320]{2,...) custom-call(s32[7]{0:T(128)} %stack.53.marks, f32[320,256]{1,0:T(8,128)} %fusion.51.refs_0_, ...), custom_call_target="tpu_custom_call" | custom-call | flops 5662310400 | bytes 10485760 | tf_op jit(solution)/shard_map/pallas_call | solution.py:1242
  829.5 20.2 %shard_map.445 = f32[9,160,320]{2,1,0:T(8,128)} custom-call(s32[7]{0:T(128)} %stack.53.marks, f32[2,1152,160]{2,1,0:T(8,128)} %get-tuple-element.321.image, f32[2,1152,320]{2,1,0:T(8,128)} %get-tuple-element.324.cells), custom_call_target="tpu_custom_call" | custom-call | flops 5662310400 | bytes 10485760 | tf_op jit(solution)/shard_map/pallas_call | solution.py:1242
  857.6 13.4 %collective-permute-start.76 = (f32[8,160]{1,0:T(8,128)}, f32[8,160]{1,0:T(8,128)S(1)}, u32[]{:S(2)}, u32[]{:S(2)}) collective-permute-start(f32[8,160]{1,0:T(8,128)} %get-tuple-element.335.refs_0_), channel_id=1, source_target_pairs={{0,2},{1,3},{2,0},{3,1},{4,6},{5,7},{6,4},{7,5},{8,10},{9,11},{10,... | collective-permute-start | bytes 15368 | tf_op jit(solution)/shard_map/ppermute | solution.py:573
  894.5 20.2 %shard_map.448 = f32[9,160,320]{2,1,0:T(8,128)} custom-call(s32[7]{0:T(128)} %stack.53.marks, f32[2,1152,160]{2,1,0:T(8,128)} %get-tuple-element.351.image, f32[2,1152,320]{2,1,0:T(8,128)} %get-tuple-element.352.cells), custom_call_target="tpu_custom_call" | custom-call | flops 5662310400 | bytes 10485760 | tf_op jit(solution)/shard_map/pallas_call | solution.py:1242
  (606 shorter events, 505.1 us)
Async XLA Ops:
  7.2 100.9 %all-gather.4.cloned.1.call-start = ((), (), s32[]{:S(2)}) async-start(), calls=%async_computation.11 | async-start | bytes 10321920 | tf_op jit(solution)/shard_map/all_gather | solution.py:1448
  18.6 32.5 %all-to-all-start = ((f32[8,320,128]{2,1,0:T(8,128)}), f32[8,320,128]{2,1,0:T(8,128)S(1)}, u32[]{:S(2)}, u32[]{:S(2)}) async-start(f32[8,320,128]{2,1,0:T(8,128)} %shard_map.425), calls=%async_computation | async-start | bytes 2621440 | tf_op jit(solution)/shard_map/all_to_all | solution.py:628
  23.6 217.0 %all-gather.6.cloned.1.call-start = ((), (), s32[]{:S(2)}) async-start(), calls=%async_computation.12 | async-start | bytes 22118400 | tf_op jit(solution)/shard_map/all_gather | solution.py:1448
  23.9 48.4 %collective-permute-start.1 = (f32[168,960]{1,0:T(8,128)S(1)}, f32[168,960]{1,0:T(8,128)S(1)}, u32[]{:S(2)}, u32[]{:S(2)}) collective-permute-start(f32[168,960]{1,0:T(8,128)S(1)} %select_maximum_fusion.refs_0_), channel_id=1, source_target_pairs={{0,3},{1,0},{2,1},{3,2},{4,7},{5,4},{6,5},{7,6},{8,11},{9,8},{10,9... | collective-permute-start | bytes 1935368 | tf_op jit(solution)/shard_map/ppermute | solution.py:573
  27.5 44.7 %collective-permute-start.3 = (f32[168,960]{1,0:T(8,128)S(1)}, f32[168,960]{1,0:T(8,128)}, u32[]{:S(2)}, u32[]{:S(2)}) collective-permute-start(f32[168,960]{1,0:T(8,128)S(1)} %select_maximum_fusion.refs_0_), channel_id=1, source_target_pairs={{0,1},{1,2},{2,3},{3,0},{4,5},{5,6},{6,7},{7,4},{8,9},{9,10},{10,1... | collective-permute-start | bytes 1935368 | tf_op jit(solution)/shard_map/ppermute | solution.py:573
  28.3 43.9 %collective-permute-start.2 = (f32[168,512]{1,0:T(8,128)}, f32[168,512]{1,0:T(8,128)S(1)}, u32[]{:S(2)}, u32[]{:S(2)}) collective-permute-start(f32[168,512]{1,0:T(8,128)} %slice.324), channel_id=1, source_target_pairs={{0,2},{1,3},{2,0},{3,1},{4,6},{5,7},{6,4},{7,5},{8,10},{9,11},{10,... | collective-permute-start | bytes 1032200 | tf_op jit(solution)/shard_map/ppermute | solution.py:573
  102.7 272.3 %all-gather.8.cloned.1.call-start = ((), (), s32[]{:S(2)}) async-start(), calls=%async_computation.13 | async-start | bytes 22118400 | tf_op jit(solution)/shard_map/all_gather | solution.py:1448
  113.4 44.5 %all-to-all-start.1 = ((f32[4,64,1600]{2,1,0:T(8,128)}), f32[4,64,1600]{2,1,0:T(8,128)S(1)}, u32[]{:S(2)}, u32[]{:S(2)}) async-start(f32[4,64,1600]{2,1,0:T(8,128)} %bitcast.167), calls=%async_computation.1 | async-start | bytes 3407872 | tf_op jit(solution)/shard_map/all_to_all | solution.py:589
  118.7 30.6 %collective-permute-start.10 = (f32[320,256]{1,0:T(8,128)}, f32[320,256]{1,0:T(8,128)}, u32[]{:S(2)}, u32[]{:S(2)}) collective-permute-start(f32[320,256]{1,0:T(8,128)} %fusion.57.refs_0_.refs_8_), channel_id=1, source_target_pairs={{0,12},{4,8},{8,4},{12,0},{1,13},{5,9},{9,5},{13,1},{2,14},{6,10},... | collective-permute-start | bytes 983048 | tf_op jit(solution)/shard_map/ppermute | solution.py:569
  121.6 30.8 %collective-permute-start.11 = (f32[320,256]{1,0:T(8,128)}, f32[320,256]{1,0:T(8,128)}, u32[]{:S(2)}, u32[]{:S(2)}) collective-permute-start(f32[320,256]{1,0:T(8,128)} %fusion.57.refs_0_.refs_8_), channel_id=1, source_target_pairs={{0,16},{16,0},{1,17},{17,1},{2,18},{18,2},{3,19},{19,3},{4,20},{20... | collective-permute-start | bytes 983048 | tf_op jit(solution)/shard_map/ppermute | solution.py:565
  184.7 43.1 %collective-permute-start.25 = (f32[77,256]{1,0:T(8,128)S(1)}, f32[77,256]{1,0:T(8,128)S(1)}, u32[]{:S(2)}, u32[]{:S(2)}) collective-permute-start(f32[77,256]{1,0:T(8,128)S(1)} %constant_dynamic-slice_fusion.9), channel_id=1, source_target_pairs={{0,16},{16,0},{1,17},{17,1},{2,18},{18,2},{3,19},{19,3},{4,20},{20... | collective-permute-start | bytes 236552 | tf_op jit(solution)/shard_map/ppermute | solution.py:565
  282.1 65.9 %all-to-all-start.4 = ((f32[4,104,1280]{2,1,0:T(8,128)}), f32[4,104,1280]{2,1,0:T(8,128)}, u32[]{:S(2)}, u32[]{:S(2)}) async-start(f32[4,104,1280]{2,1,0:T(8,128)} %broadcast_in_dim.21), calls=%async_computation.4 | async-start | bytes 4259840 | tf_op jit(solution)/shard_map/all_to_all | solution.py:589
  289.4 561.0 %reduce-scatter.3.cloned.1.call-start = ((), (), s32[]{:S(2)}) async-start(), calls=%async_computation.14 | async-start | bytes 36864000 | tf_op jit(solution)/shard_map/reduce_scatter | solution.py:1452
  289.4 31.6 %collective-permute-start.29 = (f32[256,640]{1,0:T(8,128)S(1)}, f32[256,640]{1,0:T(8,128)S(1)}, u32[]{:S(2)}, u32[]{:S(2)}) collective-permute-start(f32[256,640]{1,0:T(8,128)S(1)} %slice.335.refs_0_), channel_id=1, source_target_pairs={{0,4},{4,0},{8,12},{12,8},{1,5},{5,1},{9,13},{13,9},{2,6},{6,2},{1... | collective-permute-start | bytes 1966088 | tf_op jit(solution)/shard_map/ppermute | solution.py:569
  290.8 33.7 %collective-permute-start.30 = (f32[256,640]{1,0:T(8,128)S(1)}, f32[256,640]{1,0:T(8,128)S(1)}, u32[]{:S(2)}, u32[]{:S(2)}) collective-permute-start(f32[256,640]{1,0:T(8,128)S(1)} %slice.335.refs_0_), channel_id=1, source_target_pairs={{0,8},{4,12},{8,0},{12,4},{1,9},{5,13},{9,1},{13,5},{2,10},{6,14},... | collective-permute-start | bytes 1966088 | tf_op jit(solution)/shard_map/ppermute | solution.py:569
  290.8 57.2 %collective-permute-start.31 = (f32[256,640]{1,0:T(8,128)S(1)}, f32[256,640]{1,0:T(8,128)}, u32[]{:S(2)}, u32[]{:S(2)}) collective-permute-start(f32[256,640]{1,0:T(8,128)S(1)} %slice.335.refs_0_), channel_id=1, source_target_pairs={{0,12},{4,8},{8,4},{12,0},{1,13},{5,9},{9,5},{13,1},{2,14},{6,10},... | collective-permute-start | bytes 1966088 | tf_op jit(solution)/shard_map/ppermute | solution.py:569
  413.9 27.8 %collective-permute-start.36 = (f32[64,1280]{1,0:T(8,128)S(1)}, f32[64,1280]{1,0:T(8,128)S(1)}, u32[]{:S(2)}, u32[]{:S(2)}) collective-permute-start(f32[64,1280]{1,0:T(8,128)S(1)} %fusion.63), channel_id=1, source_target_pairs={{0,2},{1,3},{2,0},{3,1},{4,6},{5,7},{6,4},{7,5},{8,10},{9,11},{10,... | collective-permute-start | bytes 983048 | tf_op jit(solution)/shard_map/ppermute | solution.py:573
  463.2 33.4 %collective-permute-start.39 = (f32[64,1280]{1,0:T(8,128)S(1)}, f32[64,1280]{1,0:T(8,128)S(1)}, u32[]{:S(2)}, u32[]{:S(2)}) collective-permute-start(f32[64,1280]{1,0:T(8,128)S(1)} %get-tuple-element.450), channel_id=1, source_target_pairs={{0,2},{1,3},{2,0},{3,1},{4,6},{5,7},{6,4},{7,5},{8,10},{9,11},{10,... | collective-permute-start | bytes 983048 | tf_op jit(solution)/shard_map/ppermute | solution.py:573
  463.9 32.7 %collective-permute-start.40 = (f32[64,1280]{1,0:T(8,128)S(1)}, f32[64,1280]{1,0:T(8,128)S(1)}, u32[]{:S(2)}, u32[]{:S(2)}) collective-permute-start(f32[64,1280]{1,0:T(8,128)S(1)} %get-tuple-element.449), channel_id=1, source_target_pairs={{0,3},{1,0},{2,1},{3,2},{4,7},{5,4},{6,5},{7,6},{8,11},{9,8},{10,9... | collective-permute-start | bytes 983048 | tf_op jit(solution)/shard_map/ppermute | solution.py:573
  571.4 49.7 %all-to-all-start.5 = ((f32[4,64,1280]{2,1,0:T(8,128)}), f32[4,64,1280]{2,1,0:T(8,128)}, u32[]{:S(2)}, u32[]{:S(2)}) async-start(f32[4,64,1280]{2,1,0:T(8,128)} %bitcast.177), calls=%async_computation.5 | async-start | bytes 2621440 | tf_op jit(solution)/shard_map/all_to_all | solution.py:589
  635.1 254.5 %reduce-scatter.5.cloned.1.call-start = ((), (), s32[]{:S(2)}) async-start(), calls=%async_computation.15 | async-start | bytes 14745600 | tf_op jit(solution)/shard_map/reduce_scatter | solution.py:1452
  678.5 28.0 %collective-permute-start.57 = (f32[8,80,128]{2,1,0:T(8,128)}, f32[8,80,128]{2,1,0:T(8,128)S(1)}, u32[]{:S(2)}, u32[]{:S(2)}) collective-permute-start(f32[8,80,128]{2,1,0:T(8,128)} %get-tuple-element.294.refs_0_.base), channel_id=1, source_target_pairs={{0,2},{1,3},{2,0},{3,1},{4,6},{5,7},{6,4},{7,5},{8,10},{9,11},{10,... | collective-permute-start | bytes 983048 | tf_op jit(solution)/shard_map/ppermute | solution.py:573
  732.0 55.9 %all-to-all-start.7 = ((f32[4,72,1600]{2,1,0:T(8,128)}), f32[4,72,1600]{2,1,0:T(8,128)S(1)}, u32[]{:S(2)}, u32[]{:S(2)}) async-start(f32[4,72,1600]{2,1,0:T(8,128)} %pad_maximum_fusion.3), calls=%async_computation.7 | async-start | bytes 3833856 | tf_op jit(solution)/shard_map/all_to_all | solution.py:589
  738.4 29.4 %collective-permute-start.63 = (f32[320,256]{1,0:T(8,128)S(1)}, f32[320,256]{1,0:T(8,128)S(1)}, u32[]{:S(2)}, u32[]{:S(2)}) collective-permute-start(f32[320,256]{1,0:T(8,128)S(1)} %get-tuple-element.444), channel_id=1, source_target_pairs={{0,12},{4,8},{8,4},{12,0},{1,13},{5,9},{9,5},{13,1},{2,14},{6,10},... | collective-permute-start | bytes 983048 | tf_op jit(solution)/shard_map/ppermute | solution.py:569
  817.6 36.2 %collective-permute-start.72 = (f32[8,80,128]{2,1,0:T(8,128)}, f32[8,80,128]{2,1,0:T(8,128)}, u32[]{:S(2)}, u32[]{:S(2)}) collective-permute-start(f32[8,80,128]{2,1,0:T(8,128)} %get-tuple-element.319), channel_id=1, source_target_pairs={{0,2},{1,3},{2,0},{3,1},{4,6},{5,7},{6,4},{7,5},{8,10},{9,11},{10,... | collective-permute-start | bytes 983048 | tf_op jit(solution)/shard_map/ppermute | solution.py:573
  820.0 33.8 %collective-permute-start.73 = (f32[8,80,128]{2,1,0:T(8,128)}, f32[8,80,128]{2,1,0:T(8,128)}, u32[]{:S(2)}, u32[]{:S(2)}) collective-permute-start(f32[8,80,128]{2,1,0:T(8,128)} %get-tuple-element.320), channel_id=1, source_target_pairs={{0,3},{1,0},{2,1},{3,2},{4,7},{5,4},{6,5},{7,6},{8,11},{9,8},{10,9... | collective-permute-start | bytes 983048 | tf_op jit(solution)/shard_map/ppermute | solution.py:573
  873.0 52.8 %collective-permute-start.78 = (f32[160,640]{1,0:T(8,128)}, f32[160,640]{1,0:T(8,128)}, u32[]{:S(2)}, u32[]{:S(2)}) collective-permute-start(f32[160,640]{1,0:T(8,128)} %get-tuple-element.342), channel_id=1, source_target_pairs={{0,1},{1,2},{2,3},{3,0},{4,5},{5,6},{6,7},{7,4},{8,9},{9,10},{10,1... | collective-permute-start | bytes 1228808 | tf_op jit(solution)/shard_map/ppermute | solution.py:573
  873.2 52.6 %collective-permute-start.79 = (f32[160,640]{1,0:T(8,128)}, f32[160,640]{1,0:T(8,128)}, u32[]{:S(2)}, u32[]{:S(2)}) collective-permute-start(f32[160,640]{1,0:T(8,128)} %get-tuple-element.343), channel_id=1, source_target_pairs={{0,2},{1,3},{2,0},{3,1},{4,6},{5,7},{6,4},{7,5},{8,10},{9,11},{10,... | collective-permute-start | bytes 1228808 | tf_op jit(solution)/shard_map/ppermute | solution.py:573
  879.9 45.9 %collective-permute-start.80 = (f32[160,640]{1,0:T(8,128)}, f32[160,640]{1,0:T(8,128)}, u32[]{:S(2)}, u32[]{:S(2)}) collective-permute-start(f32[160,640]{1,0:T(8,128)} %get-tuple-element.344), channel_id=1, source_target_pairs={{0,3},{1,0},{2,1},{3,2},{4,7},{5,4},{6,5},{7,6},{8,11},{9,8},{10,9... | collective-permute-start | bytes 1228808 | tf_op jit(solution)/shard_map/ppermute | solution.py:573
  885.5 42.6 %all-to-all-start.8 = ((f32[8,88,128]{2,1,0:T(8,128)}), f32[8,88,128]{2,1,0:T(8,128)}, u32[]{:S(2)}, u32[]{:S(2)}) async-start(f32[8,88,128]{2,1,0:T(8,128)} %get-tuple-element.336), calls=%async_computation.9 | async-start | bytes 720896 | tf_op jit(solution)/shard_map/all_to_all | solution.py:628
  935.7 28.6 %collective-permute-start.87 = (f32[64,1280]{1,0:T(8,128)}, f32[64,1280]{1,0:T(8,128)}, u32[]{:S(2)}, u32[]{:S(2)}) collective-permute-start(f32[64,1280]{1,0:T(8,128)} %shard_map.449.refs_0_), channel_id=1, source_target_pairs={{0,2},{1,3},{2,0},{3,1},{4,6},{5,7},{6,4},{7,5},{8,10},{9,11},{10,... | collective-permute-start | bytes 983048 | tf_op jit(solution)/shard_map/ppermute | solution.py:573
  935.7 28.6 %collective-permute-start.88 = (f32[64,1280]{1,0:T(8,128)}, f32[64,1280]{1,0:T(8,128)}, u32[]{:S(2)}, u32[]{:S(2)}) collective-permute-start(f32[64,1280]{1,0:T(8,128)} %shard_map.449.refs_0_), channel_id=1, source_target_pairs={{0,1},{1,2},{2,3},{3,0},{4,5},{5,6},{6,7},{7,4},{8,9},{9,10},{10,1... | collective-permute-start | bytes 983048 | tf_op jit(solution)/shard_map/ppermute | solution.py:573
  (181 other events, 2385.0 us)
Sparse Core Ops, SparseCore 0:
  10.7 77.2 all-gather.3
  102.8 115.1 all-gather.5
  219.9 137.5 all-gather.7
  545.5 225.8 reduce-scatter.2
  774.9 99.5 reduce-scatter.4

commit v4 on v3

--- a/solution.py
+++ b/solution.py
@@ -1552,10 +1552,7 @@
     proj_in_full = third_full[:, :1280]
     query_cross_full = third_full[:, 1280:2560]
     out_cross_full = third_full[:, 2560:]
-    ff_block = jnp.concatenate([ff_in.reshape(160, 2560), ff_out.T], axis=1)
-    ff_full = gather_plane(after(ff_block, third))
-    ff_in_full = ff_full[:, :2560]
-    ff_out_full = ff_full[:, 2560:]
+    ff_out_full = gather_plane(after(ff_out.T, third))
     cot = after(cotangent[0] * own_valid, own_one)
     grad_ff_part = mm(cot, proj_out_full, 1, 1)
     cot_pieces = z_all(jnp.concatenate([grad_ff_part, cot], axis=1).reshape(4, 64, channels + wide))
@@ -1613,6 +1610,7 @@
         [(256, wide), (8, 256)],
         [((1024, 256), jnp.float32)],
     )
+    ff_in_full = gather_plane(after(ff_in.reshape(160, 2560), attn_self))
     self_part = mm(attn_self, out_self_full, 1, 1)
     self_pieces = z_received(rows_of(self_part))
     self_sum = total_of(self_pieces)
@@ -1719,6 +1717,21 @@
     grad_three_q = plane_exchange(grad_three)
     out_sum = jnp.sum(after(out_sum, grad_three), axis=0)
     text_grads = total_of(z_received(after(text_grads, grad_three)))
+    grad_three_q, text_grads = together(grad_three_q, text_grads)
+    gain_block = lax.dynamic_slice_in_dim(gain_attn_full, block * width, width, 1)
+    (sums,) = small(
+        norm_sums_kernel, marks, (grad_three_q, residual_q, stats_three, gain_block), [(8, width)]
+    )
+    grad_residual_q, grad_gain_three = small(
+        norm_back_kernel,
+        marks,
+        (grad_three_q, residual_q, stats_three, gain_block, cot_q, *z_pieces(sums)),
+        [(8, 80, 128), (8, width)],
+    )
+
+    residual_pieces = z_pieces(grad_residual_q)
+    text_grads = after(text_grads, grad_residual_q)
+    text_grads = text_grads + flip(text_grads, 1)
     attn_right = jnp.concatenate(
         [
             jnp.concatenate([grad_qkv, attn_self], axis=1),
@@ -1733,25 +1746,10 @@
             grad_after_self_all,
             jnp.pad(grad_projected, ((0, 192), (0, 0))),
         ),
-        after(attn_right, grad_three),
-    )
-    grad_three_q, attn_grads, text_grads = together(grad_three_q, attn_grads, text_grads)
+        after(attn_right, residual_pieces[1]),
+    )
+    *residual_pieces, text_grads, attn_grads = together(*residual_pieces, text_grads, attn_grads)
     attn_grads = scatter_plane(attn_grads)
-    gain_block = lax.dynamic_slice_in_dim(gain_attn_full, block * width, width, 1)
-    (sums,) = small(
-        norm_sums_kernel, marks, (grad_three_q, residual_q, stats_three, gain_block), [(8, width)]
-    )
-    grad_residual_q, grad_gain_three = small(
-        norm_back_kernel,
-        marks,
-        (grad_three_q, residual_q, stats_three, gain_block, cot_q, *z_pieces(sums)),
-        [(8, 80, 128), (8, width)],
-    )
-
-    residual_pieces = z_pieces(grad_residual_q)
-    text_grads = after(text_grads, grad_residual_q)
-    text_grads = text_grads + flip(text_grads, 1)
-    *residual_pieces, text_grads = together(*residual_pieces, text_grads)
     own_two, other_two, image_back = second_conv_back(marks, residual_pieces, second_weight)
     own_two = own_two + swap(other_two)
     grad_act_two, part = plane_sum(own_two)

time: 985 us -> 968 us (0.983)
  starting transfers between devices: 199 us -> 179 us
    ppermute x25, waiting for transfers between devices: 161 us -> 132 us  [flip(): return lax.ppermute(values, H, [(s, s ^ step) for s in range(4)])]
    all_to_all x4, waiting for transfers between devices: 5.48 us -> 23.3 us  [z_all(): return lax.all_to_all(values, T, 0, 0)]
    ppermute x52, starting transfers between devices: 124 us -> 109 us  [turn(): return lax.ppermute(values, T, [(s, (s + step) % 4) for s in range(4)])]
  transfers between devices with their start and end apart: 106 -> 107, of which waited for: 44 -> 46; matrix products, arithmetic and copies ran while one was open for 15% -> 18% of each run, Pallas kernels for 22% -> 22%
where the time goes in v4:
time: 968 us; the launch traced here: 957 us
  waiting for transfers between devices  313 us (32%)
  Pallas kernels  219 us (23%)
  starting transfers between devices  179 us (18%)
  matrix products  104 us (11%)
  local copies, waits for them, and re-layouts  82 us (8%)
  other arithmetic  41.4 us (4%)
  between operations  18.1 us (2%)
    pallas_call x23, Pallas kernels, run_kernel(): pl.pallas_call(body, out_shape=[jax.ShapeDtypeStruct(shape, jnp.float32)...  184 us
    ppermute x25, waiting for transfers between devices, flip(): return lax.ppermute(values, H, [(s, s ^ step) for s in range(4)])  132 us
    ppermute x52, waiting for transfers between devices, turn(): return lax.ppermute(values, T, [(s, (s + step) % 4) for s in range(4)])  123 us
    ppermute x52, starting transfers between devices, turn(): return lax.ppermute(values, T, [(s, (s + step) % 4) for s in range(4)])  109 us
    dot_general x23, matrix products, mm(): lax.dot_general(left, right, (((left_dim,), (right_dim,)), ((), ())), pre...  97.7 us
    pallas_call x3, Pallas kernels, weight_grads(): pl.pallas_call(functools.partial(weight_kernel, plan), out_shape=jax.Shap...  35.2 us
    all_to_all x5, waiting for transfers between devices, plane_exchange(): return lax.all_to_all(packed, IH, 0, 0)  30.9 us
    ppermute x25, starting transfers between devices, flip(): return lax.ppermute(values, H, [(s, s ^ step) for s in range(4)])  30.1 us
  transfers between devices with their start and end apart: 107, of which 46 were waited for; matrix products, arithmetic and copies ran while one was open for 18% of the time, Pallas kernels for 22%

profile of v4, /device:TPU:0, one launch (start us, length us, event | category | flops | bytes accessed | tf_op | source)
XLA Modules:
  0.0 956.6 jit_solution(11823160519289979873)
XLA Ops:
  32.9 18.3 %all-to-all-done.source = f32[8,320,128]{2,1,0:T(8,128)S(1)} async-done(((f32[8,320,128]{2,1,0:T(8,128)}), f32[8,320,128]{2,1,0:T(8,128)S(1)}, u32[]{:S(2)}, u32[]{:S(2)}) %all-to-all-start) | async-done | bytes 1310752 | tf_op jit(solution)/shard_map/all_to_all | solution.py:628
  52.2 19.2 %shard_map.426 = (f32[4,320,256]{2,1,0:T(8,128)}, f32[4,320,256]{2,1,0:T(8,128)}, f32[2,1152,160]{2,1,0:T(8,128)}, f32[2,8,160]{2,1,0:T(8,128)}) custom-call(s32[7]{0:T(128)} %stack.53.marks, f32[8,320,128]{2,1,0:T(8,128)} %copy-done.3, f32[1,160]{1,0:T(1,128)} %bitcast.210, f32[2,320]{1,0:T(2,128)} %fusion.74.tau, f32[1440,320]{1,0:T(8,128)} %bitcast.223), custom_call_target="tpu_custom_call" | custom-call | flops 5662310400 | bytes 10485760 | tf_op jit(solution)/shard_map/pallas_call | solution.py:1242
  80.7 10.5 %collective-permute-done.21 = f32[168,448]{1,0:T(8,128)S(1)} collective-permute-done((f32[168,448]{1,0:T(8,128)S(1)}, f32[168,448]{1,0:T(8,128)S(1)}, u32[]{:S(2)}, u32[]{:S(2)}) %collective-permute-start.21) | collective-permute-done | bytes 301088 | tf_op jit(solution)/shard_map/ppermute | solution.py:573
  116.9 14.4 %collective-permute-done.8.refs_1_.refs_9_ = f32[320,256]{1,0:T(8,128)} collective-permute-done((f32[320,256]{1,0:T(8,128)}, f32[320,256]{1,0:T(8,128)}, u32[]{:S(2)}, u32[]{:S(2)}) %collective-permute-start.8) | collective-permute-done | bytes 327712 | tf_op jit(solution)/shard_map/ppermute | solution.py:569
  132.3 12.5 %collective-permute-done.10.refs_3_.refs_11_ = f32[320,256]{1,0:T(8,128)} collective-permute-done((f32[320,256]{1,0:T(8,128)}, f32[320,256]{1,0:T(8,128)}, u32[]{:S(2)}, u32[]{:S(2)}) %collective-permute-start.10) | collective-permute-done | bytes 327712 | tf_op jit(solution)/shard_map/ppermute | solution.py:569
  153.1 21.4 %shard_map.427 = (f32[8,80,128]{2,1,0:T(8,128)}, f32[8,80,128]{2,1,0:T(8,128)}, f32[8,80,128]{2,1,0:T(8,128)}, f32[8,80,128]{2,1,0:T(8,128)}, f32[2,1152,320]{2,1,0:T(8,128)}, /*index=5*/f32[2,8,320]{2,1,0:T(8,128)}) custom-call(s32[7]{0:T(128)} %stack.53.marks, f32[320,256]{1,0:T(8,128)} %fusion.49.refs_0_.refs_8_, ...), custom_call_target="tpu_custom_call" | custom-call | flops 5662310400 | bytes 10485760 | tf_op jit(solution)/shard_map/pallas_call | solution.py:1242
  179.9 7.5 collective-permute-done.15.second
  187.4 12.2 %collective-permute-done.16.third = f32[8,80,128]{2,1,0:T(8,128)S(1)} collective-permute-done((f32[8,80,128]{2,1,0:T(8,128)}, f32[8,80,128]{2,1,0:T(8,128)S(1)}, u32[]{:S(2)}, u32[]{:S(2)}) %collective-permute-start.16) | collective-permute-done | bytes 327712 | tf_op jit(solution)/shard_map/ppermute | solution.py:573
  251.0 15.5 %collective-permute-done.28 = f32[77,640]{1,0:T(8,128)S(1)} collective-permute-done((f32[77,640]{1,0:T(8,128)S(1)}, f32[77,640]{1,0:T(8,128)S(1)}, u32[]{:S(2)}, u32[]{:S(2)}) %collective-permute-start.28) | collective-permute-done | bytes 197152 | tf_op jit(solution)/shard_map/ppermute | solution.py:569
  289.3 11.4 %collective-permute-done.29.refs_1_ = f32[256,640]{1,0:T(8,128)S(1)} collective-permute-done((f32[256,640]{1,0:T(8,128)S(1)}, f32[256,640]{1,0:T(8,128)S(1)}, u32[]{:S(2)}, u32[]{:S(2)}) %collective-permute-start.29) | collective-permute-done | bytes 655392 | tf_op jit(solution)/shard_map/ppermute | solution.py:569
  300.8 13.6 %collective-permute-done.30.refs_2_ = f32[256,640]{1,0:T(8,128)S(1)} collective-permute-done((f32[256,640]{1,0:T(8,128)S(1)}, f32[256,640]{1,0:T(8,128)S(1)}, u32[]{:S(2)}, u32[]{:S(2)}) %collective-permute-start.30) | collective-permute-done | bytes 655392 | tf_op jit(solution)/shard_map/ppermute | solution.py:569
  315.2 18.0 %all-to-all-done.4.pieces = f32[4,104,1280]{2,1,0:T(8,128)} async-done(((f32[4,104,1280]{2,1,0:T(8,128)}), f32[4,104,1280]{2,1,0:T(8,128)}, u32[]{:S(2)}, u32[]{:S(2)}) %all-to-all-start.4) | async-done | bytes 2129952 | tf_op jit(solution)/shard_map/all_to_all | solution.py:589
  349.9 8.5 collective-permute-done.32
  375.8 7.5 fusion.6
  406.2 22.2 %collective-permute-done.36 = f32[64,1280]{1,0:T(8,128)S(1)} collective-permute-done((f32[64,1280]{1,0:T(8,128)S(1)}, f32[64,1280]{1,0:T(8,128)S(1)}, u32[]{:S(2)}, u32[]{:S(2)}) %collective-permute-start.36) | collective-permute-done | bytes 327712 | tf_op jit(solution)/shard_map/ppermute | solution.py:573
  430.1 9.6 %fusion.81 = f32[256,2560]{1,0:T(8,128)S(1)} fusion(f32[1280,2560]{1,0:T(8,128)} %all-gather.11.cloned.1.call-done, f32[64,1280]{1,0:T(8,128)} %copy-done.54, f32[64,1280]{1,0:T(8,128)} %copy-done.53, f32[64,1280]{1,0:T(8,128)} %copy-done.52, f32[64,1280]{1,0:T(8,128)} %copy-done.31), kind=kOutput, calls=%fused_computation.208 | convolution fusion | flops 5034147840 | bytes 17039360 | tf_op jit(solution)/shard_map/dot_general | solution.py:555
  452.3 8.2 collective-permute-done.38
  462.8 13.2 %shard_map.435.refs_3_ = f32[1280,6400]{1,0:T(8,128)} custom-call(f32[256,1280]{1,0:T(8,128)S(1)} %pad_maximum_fusion.4.refs_0_, f32[256,1280]{1,0:T(8,128)S(1)} %copy-done.2, f32[256,3840]{1,0:T(8,128)} %pad_maximum_fusion.refs_2_), custom_call_target="tpu_custom_call" | custom-call | flops 7549747200 | bytes 22020096 | tf_op jit(solution)/shard_map/pallas_call | solution.py:1288
  481.7 7.6 fusion
  501.4 11.7 %collective-permute-start.42 = (f32[64,1280]{1,0:T(8,128)}, f32[64,1280]{1,0:T(8,128)}, u32[]{:S(2)}, u32[]{:S(2)}) collective-permute-start(f32[64,1280]{1,0:T(8,128)} %multiply_add_fusion.1), channel_id=1, source_target_pairs={{0,2},{1,3},{2,0},{3,1},{4,6},{5,7},{6,4},{7,5},{8,10},{9,11},{10,... | collective-permute-start | bytes 983048 | tf_op jit(solution)/shard_map/ppermute | solution.py:573
  520.5 11.5 %shard_map.436 = f32[1280,6400]{1,0:T(8,128)} custom-call(f32[64,1280]{1,0:T(8,128)S(1)} %fusion.54.refs_0_, f32[64,1280]{1,0:T(8,128)S(1)} %multiply_add_fusion.2.refs_1_, f32[64,2560]{1,0:T(8,128)S(1)} %concatenate.89.refs_2_, f32[1280,6400]{1,0:T(8,128)} %shard_map.435.refs_3_), custom_call_target="tpu_custom_call", output_to_operand_aliasing={{}: (3, {})} | custom-call | flops 1258291200 | bytes 14680064 | tf_op jit(solution)/shard_map/pallas_call | solution.py:1288
  540.0 11.9 %shard_map.437 = (f32[256,320]{1,0:T(8,128)}, f32[256,640]{1,0:T(8,128)}, f32[256,640]{1,0:T(8,128)}, f32[256,640]{1,0:T(8,128)}, f32[256,640]{1,0:T(8,128)}) custom-call(s32[7]{0:T(128)} %stack.53.marks, f32[256,960]{1,0:T(8,128)} %copy-done.4, f32[256,640]{1,0:T(8,128)} %slice.327.refs_0_, f32[256,640]{1,0:T(8,128)} %copy-done.37, f32[256,640]{1,0:T(8,128)} %copy-done.38, ...), custom_call_target="tpu_custom_call" | custom-call | flops 4194304 | bytes 10485760 | tf_op jit(solution)/shard_map/pallas_call | solution.py:1242
  599.7 7.5 collective-permute-done.48
  675.0 10.5 %shard_map.442 = f32[1280,2560]{1,0:T(8,128)} custom-call(f32[256,1280]{1,0:T(8,128)S(1)} %constant_dynamic-update-slice_fusion.2.refs_0_, f32[256,1280]{1,0:T(8,128)S(1)} %constant_dynamic-update-slice_fusion.6.refs_1_, f32[256,1280]{1,0:T(8,128)S(1)} %pad.30.refs_2_, f32[256,2560]{1,0:T(8,128)} %concatenate.93.refs_3_), custom_call_target="tpu_custom_call" | custom-call | flops 5033164800 | bytes 14680064 | tf_op jit(solution)/shard_map/pallas_call | solution.py:1288
  691.3 19.8 %shard_map.443 = (f32[4,320,256]{2,1,0:T(8,128)}, f32[4,320,256]{2,1,0:T(8,128)}, f32[2,1152,160]{2,1,0:T(8,128)}) custom-call(s32[7]{0:T(128)} %stack.53.marks, f32[8,80,128]{2,1,0:T(8,128)} %get-tuple-element.296.refs_0_.base, f32[8,80,128]{2,1,0:T(8,128)} %collective-permute-done.56.refs_1_, f32[8,80,128]{2,1,0:T(8,128)} %copy-done.98, ...), custom_call_target="tpu_custom_call" | custom-call | flops 5662310400 | bytes 10485760 | tf_op jit(solution)/shard_map/pallas_call | solution.py:1242
  723.1 14.1 %collective-permute-done.61 = f32[320,256]{1,0:T(8,128)S(1)} collective-permute-done((f32[320,256]{1,0:T(8,128)S(1)}, f32[320,256]{1,0:T(8,128)S(1)}, u32[]{:S(2)}, u32[]{:S(2)}) %collective-permute-start.61) | collective-permute-done | bytes 327712 | tf_op jit(solution)/shard_map/ppermute | solution.py:569
  740.2 11.1 %collective-permute-done.63 = f32[320,256]{1,0:T(8,128)S(1)} collective-permute-done((f32[320,256]{1,0:T(8,128)S(1)}, f32[320,256]{1,0:T(8,128)S(1)}, u32[]{:S(2)}, u32[]{:S(2)}) %collective-permute-start.63) | collective-permute-done | bytes 327712 | tf_op jit(solution)/shard_map/ppermute | solution.py:569
  755.6 7.5 collective-permute-done.64.refs_1_
  772.7 25.1 %shard_map.444 = (f32[8,80,128]{2,1,0:T(8,128)}, f32[8,80,128]{2,1,0:T(8,128)}, f32[8,80,128]{2,1,0:T(8,128)}, f32[8,80,128]{2,1,0:T(8,128)}, f32[2,1152,320]{2,...) custom-call(s32[7]{0:T(128)} %stack.53.marks, f32[320,256]{1,0:T(8,128)} %fusion.43.refs_0_, ...), custom_call_target="tpu_custom_call" | custom-call | flops 5662310400 | bytes 10485760 | tf_op jit(solution)/shard_map/pallas_call | solution.py:1242
  811.9 20.2 %shard_map.445 = f32[9,160,320]{2,1,0:T(8,128)} custom-call(s32[7]{0:T(128)} %stack.53.marks, f32[2,1152,160]{2,1,0:T(8,128)} %get-tuple-element.323.image, f32[2,1152,320]{2,1,0:T(8,128)} %get-tuple-element.326.cells), custom_call_target="tpu_custom_call" | custom-call | flops 5662310400 | bytes 10485760 | tf_op jit(solution)/shard_map/pallas_call | solution.py:1242
  841.0 12.7 %collective-permute-start.76 = (f32[8,160]{1,0:T(8,128)}, f32[8,160]{1,0:T(8,128)S(1)}, u32[]{:S(2)}, u32[]{:S(2)}) collective-permute-start(f32[8,160]{1,0:T(8,128)} %get-tuple-element.337.refs_0_), channel_id=1, source_target_pairs={{0,2},{1,3},{2,0},{3,1},{4,6},{5,7},{6,4},{7,5},{8,10},{9,11},{10,... | collective-permute-start | bytes 15368 | tf_op jit(solution)/shard_map/ppermute | solution.py:573
  877.0 20.4 %shard_map.448 = f32[9,160,320]{2,1,0:T(8,128)} custom-call(s32[7]{0:T(128)} %stack.53.marks, f32[2,1152,160]{2,1,0:T(8,128)} %get-tuple-element.353.image, f32[2,1152,320]{2,1,0:T(8,128)} %get-tuple-element.354.cells), custom_call_target="tpu_custom_call" | custom-call | flops 5662310400 | bytes 10485760 | tf_op jit(solution)/shard_map/pallas_call | solution.py:1242
  (610 shorter events, 503.5 us)
Async XLA Ops:
  7.2 96.7 %all-gather.5.cloned.1.call-start = ((), (), s32[]{:S(2)}) async-start(), calls=%async_computation.11 | async-start | bytes 10321920 | tf_op jit(solution)/shard_map/all_gather | solution.py:1448
  18.6 32.5 %all-to-all-start = ((f32[8,320,128]{2,1,0:T(8,128)}), f32[8,320,128]{2,1,0:T(8,128)S(1)}, u32[]{:S(2)}, u32[]{:S(2)}) async-start(f32[8,320,128]{2,1,0:T(8,128)} %shard_map.425), calls=%async_computation | async-start | bytes 2621440 | tf_op jit(solution)/shard_map/all_to_all | solution.py:628
  23.6 209.9 %all-gather.7.cloned.1.call-start = ((), (), s32[]{:S(2)}) async-start(), calls=%async_computation.12 | async-start | bytes 22118400 | tf_op jit(solution)/shard_map/all_gather | solution.py:1448
  23.9 48.4 %collective-permute-start.1 = (f32[168,960]{1,0:T(8,128)S(1)}, f32[168,960]{1,0:T(8,128)S(1)}, u32[]{:S(2)}, u32[]{:S(2)}) collective-permute-start(f32[168,960]{1,0:T(8,128)S(1)} %select_maximum_fusion.refs_0_), channel_id=1, source_target_pairs={{0,3},{1,0},{2,1},{3,2},{4,7},{5,4},{6,5},{7,6},{8,11},{9,8},{10,9... | collective-permute-start | bytes 1935368 | tf_op jit(solution)/shard_map/ppermute | solution.py:573
  27.5 44.7 %collective-permute-start.3 = (f32[168,960]{1,0:T(8,128)S(1)}, f32[168,960]{1,0:T(8,128)}, u32[]{:S(2)}, u32[]{:S(2)}) collective-permute-start(f32[168,960]{1,0:T(8,128)S(1)} %select_maximum_fusion.refs_0_), channel_id=1, source_target_pairs={{0,1},{1,2},{2,3},{3,0},{4,5},{5,6},{6,7},{7,4},{8,9},{9,10},{10,1... | collective-permute-start | bytes 1935368 | tf_op jit(solution)/shard_map/ppermute | solution.py:573
  28.3 43.9 %collective-permute-start.2 = (f32[168,512]{1,0:T(8,128)}, f32[168,512]{1,0:T(8,128)S(1)}, u32[]{:S(2)}, u32[]{:S(2)}) collective-permute-start(f32[168,512]{1,0:T(8,128)} %slice.316), channel_id=1, source_target_pairs={{0,2},{1,3},{2,0},{3,1},{4,6},{5,7},{6,4},{7,5},{8,10},{9,11},{10,... | collective-permute-start | bytes 1032200 | tf_op jit(solution)/shard_map/ppermute | solution.py:573
  102.6 259.0 %all-gather.9.cloned.1.call-start = ((), (), s32[]{:S(2)}) async-start(), calls=%async_computation.13 | async-start | bytes 7372800 | tf_op jit(solution)/shard_map/all_gather | solution.py:1448
  108.6 44.5 %all-to-all-start.1 = ((f32[4,64,1600]{2,1,0:T(8,128)}), f32[4,64,1600]{2,1,0:T(8,128)S(1)}, u32[]{:S(2)}, u32[]{:S(2)}) async-start(f32[4,64,1600]{2,1,0:T(8,128)} %bitcast.175), calls=%async_computation.1 | async-start | bytes 3407872 | tf_op jit(solution)/shard_map/all_to_all | solution.py:589
  114.5 30.3 %collective-permute-start.10 = (f32[320,256]{1,0:T(8,128)}, f32[320,256]{1,0:T(8,128)}, u32[]{:S(2)}, u32[]{:S(2)}) collective-permute-start(f32[320,256]{1,0:T(8,128)} %fusion.49.refs_0_.refs_8_), channel_id=1, source_target_pairs={{0,12},{4,8},{8,4},{12,0},{1,13},{5,9},{9,5},{13,1},{2,14},{6,10},... | collective-permute-start | bytes 983048 | tf_op jit(solution)/shard_map/ppermute | solution.py:569
  116.9 30.9 %collective-permute-start.11 = (f32[320,256]{1,0:T(8,128)}, f32[320,256]{1,0:T(8,128)}, u32[]{:S(2)}, u32[]{:S(2)}) collective-permute-start(f32[320,256]{1,0:T(8,128)} %fusion.49.refs_0_.refs_8_), channel_id=1, source_target_pairs={{0,16},{16,0},{1,17},{17,1},{2,18},{18,2},{3,19},{19,3},{4,20},{20... | collective-permute-start | bytes 983048 | tf_op jit(solution)/shard_map/ppermute | solution.py:565
  179.8 43.1 %collective-permute-start.25 = (f32[77,256]{1,0:T(8,128)S(1)}, f32[77,256]{1,0:T(8,128)S(1)}, u32[]{:S(2)}, u32[]{:S(2)}) collective-permute-start(f32[77,256]{1,0:T(8,128)S(1)} %constant_dynamic-slice_fusion.9), channel_id=1, source_target_pairs={{0,16},{16,0},{1,17},{17,1},{2,18},{18,2},{3,19},{19,3},{4,20},{20... | collective-permute-start | bytes 236552 | tf_op jit(solution)/shard_map/ppermute | solution.py:565
  278.0 55.2 %all-to-all-start.4 = ((f32[4,104,1280]{2,1,0:T(8,128)}), f32[4,104,1280]{2,1,0:T(8,128)}, u32[]{:S(2)}, u32[]{:S(2)}) async-start(f32[4,104,1280]{2,1,0:T(8,128)} %broadcast_in_dim.21), calls=%async_computation.4 | async-start | bytes 4259840 | tf_op jit(solution)/shard_map/all_to_all | solution.py:589
  283.1 146.9 %all-gather.11.cloned.1.call-start = ((), (), s32[]{:S(2)}) async-start(), calls=%async_computation.14 | async-start | bytes 14745600 | tf_op jit(solution)/shard_map/all_gather | solution.py:1448
  284.3 30.1 %collective-permute-start.30 = (f32[256,640]{1,0:T(8,128)S(1)}, f32[256,640]{1,0:T(8,128)S(1)}, u32[]{:S(2)}, u32[]{:S(2)}) collective-permute-start(f32[256,640]{1,0:T(8,128)S(1)} %copy-done.18), channel_id=1, source_target_pairs={{0,8},{4,12},{8,0},{12,4},{1,9},{5,13},{9,1},{13,5},{2,10},{6,14},... | collective-permute-start | bytes 1966088 | tf_op jit(solution)/shard_map/ppermute | solution.py:569
  284.6 30.6 %collective-permute-start.31 = (f32[256,640]{1,0:T(8,128)S(1)}, f32[256,640]{1,0:T(8,128)}, u32[]{:S(2)}, u32[]{:S(2)}) collective-permute-start(f32[256,640]{1,0:T(8,128)S(1)} %copy-done.18), channel_id=1, source_target_pairs={{0,12},{4,8},{8,4},{12,0},{1,13},{5,9},{9,5},{13,1},{2,14},{6,10},... | collective-permute-start | bytes 1966088 | tf_op jit(solution)/shard_map/ppermute | solution.py:569
  340.2 492.6 %reduce-scatter.3.cloned.1.call-start = ((), (), s32[]{:S(2)}) async-start(), calls=%async_computation.15 | async-start | bytes 36864000 | tf_op jit(solution)/shard_map/reduce_scatter | solution.py:1452
  397.6 30.8 %collective-permute-start.36 = (f32[64,1280]{1,0:T(8,128)S(1)}, f32[64,1280]{1,0:T(8,128)S(1)}, u32[]{:S(2)}, u32[]{:S(2)}) collective-permute-start(f32[64,1280]{1,0:T(8,128)S(1)} %fusion.55), channel_id=1, source_target_pairs={{0,2},{1,3},{2,0},{3,1},{4,6},{5,7},{6,4},{7,5},{8,10},{9,11},{10,... | collective-permute-start | bytes 983048 | tf_op jit(solution)/shard_map/ppermute | solution.py:573
  448.0 32.0 %collective-permute-start.39 = (f32[64,1280]{1,0:T(8,128)}, f32[64,1280]{1,0:T(8,128)S(1)}, u32[]{:S(2)}, u32[]{:S(2)}) collective-permute-start(f32[64,1280]{1,0:T(8,128)} %get-tuple-element.452), channel_id=1, source_target_pairs={{0,2},{1,3},{2,0},{3,1},{4,6},{5,7},{6,4},{7,5},{8,10},{9,11},{10,... | collective-permute-start | bytes 983048 | tf_op jit(solution)/shard_map/ppermute | solution.py:573
  448.3 31.8 %collective-permute-start.40 = (f32[64,1280]{1,0:T(8,128)}, f32[64,1280]{1,0:T(8,128)}, u32[]{:S(2)}, u32[]{:S(2)}) collective-permute-start(f32[64,1280]{1,0:T(8,128)} %get-tuple-element.451), channel_id=1, source_target_pairs={{0,3},{1,0},{2,1},{3,2},{4,7},{5,4},{6,5},{7,6},{8,11},{9,8},{10,9... | collective-permute-start | bytes 983048 | tf_op jit(solution)/shard_map/ppermute | solution.py:573
  501.4 30.6 %collective-permute-start.42 = (f32[64,1280]{1,0:T(8,128)}, f32[64,1280]{1,0:T(8,128)}, u32[]{:S(2)}, u32[]{:S(2)}) collective-permute-start(f32[64,1280]{1,0:T(8,128)} %multiply_add_fusion.1), channel_id=1, source_target_pairs={{0,2},{1,3},{2,0},{3,1},{4,6},{5,7},{6,4},{7,5},{8,10},{9,11},{10,... | collective-permute-start | bytes 983048 | tf_op jit(solution)/shard_map/ppermute | solution.py:573
  558.2 51.0 %all-to-all-start.5 = ((f32[4,64,1280]{2,1,0:T(8,128)}), f32[4,64,1280]{2,1,0:T(8,128)}, u32[]{:S(2)}, u32[]{:S(2)}) async-start(f32[4,64,1280]{2,1,0:T(8,128)} %bitcast.185), calls=%async_computation.5 | async-start | bytes 2621440 | tf_op jit(solution)/shard_map/all_to_all | solution.py:589
  636.7 235.3 %reduce-scatter.5.cloned.1.call-start = ((), (), s32[]{:S(2)}) async-start(), calls=%async_computation.16 | async-start | bytes 14745600 | tf_op jit(solution)/shard_map/reduce_scatter | solution.py:1452
  715.5 55.4 %all-to-all-start.7 = ((f32[4,72,1600]{2,1,0:T(8,128)}), f32[4,72,1600]{2,1,0:T(8,128)S(1)}, u32[]{:S(2)}, u32[]{:S(2)}) async-start(f32[4,72,1600]{2,1,0:T(8,128)} %pad_maximum_fusion.2), calls=%async_computation.7 | async-start | bytes 3833856 | tf_op jit(solution)/shard_map/all_to_all | solution.py:589
  721.5 29.7 %collective-permute-start.63 = (f32[320,256]{1,0:T(8,128)S(1)}, f32[320,256]{1,0:T(8,128)S(1)}, u32[]{:S(2)}, u32[]{:S(2)}) collective-permute-start(f32[320,256]{1,0:T(8,128)S(1)} %get-tuple-element.446), channel_id=1, source_target_pairs={{0,12},{4,8},{8,4},{12,0},{1,13},{5,9},{9,5},{13,1},{2,14},{6,10},... | collective-permute-start | bytes 983048 | tf_op jit(solution)/shard_map/ppermute | solution.py:569
  799.7 36.9 %collective-permute-start.72 = (f32[8,80,128]{2,1,0:T(8,128)}, f32[8,80,128]{2,1,0:T(8,128)}, u32[]{:S(2)}, u32[]{:S(2)}) collective-permute-start(f32[8,80,128]{2,1,0:T(8,128)} %get-tuple-element.321), channel_id=1, source_target_pairs={{0,2},{1,3},{2,0},{3,1},{4,6},{5,7},{6,4},{7,5},{8,10},{9,11},{10,... | collective-permute-start | bytes 983048 | tf_op jit(solution)/shard_map/ppermute | solution.py:573
  802.1 34.5 %collective-permute-start.73 = (f32[8,80,128]{2,1,0:T(8,128)}, f32[8,80,128]{2,1,0:T(8,128)}, u32[]{:S(2)}, u32[]{:S(2)}) collective-permute-start(f32[8,80,128]{2,1,0:T(8,128)} %get-tuple-element.322), channel_id=1, source_target_pairs={{0,3},{1,0},{2,1},{3,2},{4,7},{5,4},{6,5},{7,6},{8,11},{9,8},{10,9... | collective-permute-start | bytes 983048 | tf_op jit(solution)/shard_map/ppermute | solution.py:573
  855.7 52.8 %collective-permute-start.78 = (f32[160,640]{1,0:T(8,128)}, f32[160,640]{1,0:T(8,128)}, u32[]{:S(2)}, u32[]{:S(2)}) collective-permute-start(f32[160,640]{1,0:T(8,128)} %get-tuple-element.344), channel_id=1, source_target_pairs={{0,1},{1,2},{2,3},{3,0},{4,5},{5,6},{6,7},{7,4},{8,9},{9,10},{10,1... | collective-permute-start | bytes 1228808 | tf_op jit(solution)/shard_map/ppermute | solution.py:573
  855.7 52.8 %collective-permute-start.79 = (f32[160,640]{1,0:T(8,128)}, f32[160,640]{1,0:T(8,128)}, u32[]{:S(2)}, u32[]{:S(2)}) collective-permute-start(f32[160,640]{1,0:T(8,128)} %get-tuple-element.345), channel_id=1, source_target_pairs={{0,2},{1,3},{2,0},{3,1},{4,6},{5,7},{6,4},{7,5},{8,10},{9,11},{10,... | collective-permute-start | bytes 1228808 | tf_op jit(solution)/shard_map/ppermute | solution.py:573
  862.4 46.1 %collective-permute-start.80 = (f32[160,640]{1,0:T(8,128)}, f32[160,640]{1,0:T(8,128)}, u32[]{:S(2)}, u32[]{:S(2)}) collective-permute-start(f32[160,640]{1,0:T(8,128)} %get-tuple-element.346), channel_id=1, source_target_pairs={{0,3},{1,0},{2,1},{3,2},{4,7},{5,4},{6,5},{7,6},{8,11},{9,8},{10,9... | collective-permute-start | bytes 1228808 | tf_op jit(solution)/shard_map/ppermute | solution.py:573
  868.0 42.8 %all-to-all-start.8 = ((f32[8,88,128]{2,1,0:T(8,128)}), f32[8,88,128]{2,1,0:T(8,128)}, u32[]{:S(2)}, u32[]{:S(2)}) async-start(f32[8,88,128]{2,1,0:T(8,128)} %get-tuple-element.338), calls=%async_computation.9 | async-start | bytes 720896 | tf_op jit(solution)/shard_map/all_to_all | solution.py:628
  918.5 28.5 %collective-permute-start.87 = (f32[64,1280]{1,0:T(8,128)}, f32[64,1280]{1,0:T(8,128)}, u32[]{:S(2)}, u32[]{:S(2)}) collective-permute-start(f32[64,1280]{1,0:T(8,128)} %shard_map.449.refs_0_), channel_id=1, source_target_pairs={{0,2},{1,3},{2,0},{3,1},{4,6},{5,7},{6,4},{7,5},{8,10},{9,11},{10,... | collective-permute-start | bytes 983048 | tf_op jit(solution)/shard_map/ppermute | solution.py:573
  918.5 28.5 %collective-permute-start.88 = (f32[64,1280]{1,0:T(8,128)}, f32[64,1280]{1,0:T(8,128)}, u32[]{:S(2)}, u32[]{:S(2)}) collective-permute-start(f32[64,1280]{1,0:T(8,128)} %shard_map.449.refs_0_), channel_id=1, source_target_pairs={{0,1},{1,2},{2,3},{3,0},{4,5},{5,6},{6,7},{7,4},{8,9},{9,10},{10,1... | collective-permute-start | bytes 983048 | tf_op jit(solution)/shard_map/ppermute | solution.py:573
  (182 other events, 2241.4 us)
Sparse Core Ops, SparseCore 0:
  10.7 77.2 all-gather.4
  102.8 115.1 all-gather.6
  219.9 54.7 all-gather.8
  340.3 71.1 all-gather.10
  532.2 220.7 reduce-scatter.2
  756.4 99.4 reduce-scatter.4

commit v5 on v4

--- a/solution.py
+++ b/solution.py
@@ -1807,7 +1807,7 @@
         (source, gain_in[None, :], stats_one, *grad_act_pieces),
         [(8, 80, 128), (8, width)],
     )
-    cross_shares = total_of(z_received(after(cross_cut, grad_input_q)))
+    cross_received = z_received(after(cross_cut, grad_input_q))
     moved, grad_gain_in = small(
         input_back_kernel,
         marks,
@@ -1832,13 +1832,14 @@
     grad_proj_out = mm(after_ff_here, cot, 0, 0).reshape(2, 4, width, wide)
     grad_proj_own = pick(grad_proj_out, item) + swap(pick(grad_proj_out, 1 - item))
     grad_conv_second = conv_weight(marks, image_back, image_two, -1)
-    received, cross_shares, proj_share, text_other_grads, grad_proj_own, grad_conv_second = together(
-        received, cross_shares, proj_share, text_other_grads, grad_proj_own, grad_conv_second
+    received, text_other_grads, grad_proj_own, grad_conv_second = together(
+        received, text_other_grads, grad_proj_own, grad_conv_second
     )
     grad_conv_second = grad_conv_second.reshape(3, 3, width, wide).transpose(0, 1, 3, 2)
     text_grads, text_other_grads = unfolded(text_grads), unfolded(text_other_grads)
     (grad_hidden,) = small(unpack_kernel, marks, (received,), [(64, channels)])
     hidden_pieces = z_pieces(grad_hidden)
+    cross_shares = total_of(after(cross_received, hidden_pieces[1]))
     after_ff_all, grad_proj_own = after((after_ff_all, grad_proj_own), grad_hidden)
     grad_proj_out = h_collect([pick(grad_proj_own, h ^ j) for j in range(4)])
     output = residual_all + mm(after_ff_all, proj_out_full, 1, 0)

time: 968 us -> 990 us (1.023)
  waiting for transfers between devices: 313 us -> 324 us
    ppermute x52, waiting for transfers between devices: 123 us -> 135 us  [turn(): return lax.ppermute(values, T, [(s, (s + step) % 4) for s in range(4)])]
    unnamed x227 -> x243, local copies, waits for them, and re-layouts: 28.1 us -> 29.2 us
  transfers between devices with their start and end apart: 107 -> 107, of which waited for: 46 -> 47; matrix products, arithmetic and copies ran while one was open for 18% -> 19% of each run, Pallas kernels for 22% -> 22%
where the time goes in v5:
time: 990 us; the launch traced here: 979 us
  waiting for transfers between devices  324 us (33%)
  Pallas kernels  219 us (22%)
  starting transfers between devices  178 us (18%)
  matrix products  106 us (11%)
  local copies, waits for them, and re-layouts  90.3 us (9%)
  other arithmetic  42.9 us (4%)
  between operations  18 us (2%)
    pallas_call x23, Pallas kernels, run_kernel(): pl.pallas_call(body, out_shape=[jax.ShapeDtypeStruct(shape, jnp.float32)...  184 us
    ppermute x52, waiting for transfers between devices, turn(): return lax.ppermute(values, T, [(s, (s + step) % 4) for s in range(4)])  135 us
    ppermute x25, waiting for transfers between devices, flip(): return lax.ppermute(values, H, [(s, s ^ step) for s in range(4)])  132 us
    ppermute x52, starting transfers between devices, turn(): return lax.ppermute(values, T, [(s, (s + step) % 4) for s in range(4)])  106 us
    dot_general x23, matrix products, mm(): lax.dot_general(left, right, (((left_dim,), (right_dim,)), ((), ())), pre...  99.5 us
    pallas_call x3, Pallas kernels, weight_grads(): pl.pallas_call(functools.partial(weight_kernel, plan), out_shape=jax.Shap...  35.2 us
    all_to_all x5, waiting for transfers between devices, plane_exchange(): return lax.all_to_all(packed, IH, 0, 0)  30.9 us
    ppermute x25, starting transfers between devices, flip(): return lax.ppermute(values, H, [(s, s ^ step) for s in range(4)])  30.7 us
  transfers between devices with their start and end apart: 107, of which 47 were waited for; matrix products, arithmetic and copies ran while one was open for 19% of the time, Pallas kernels for 22%

profile of v5, /device:TPU:0, one launch (start us, length us, event | category | flops | bytes accessed | tf_op | source)
XLA Modules:
  0.0 978.6 jit_solution(8052430505968823978)
XLA Ops:
  32.8 18.3 %all-to-all-done.source = f32[8,320,128]{2,1,0:T(8,128)S(1)} async-done(((f32[8,320,128]{2,1,0:T(8,128)}), f32[8,320,128]{2,1,0:T(8,128)S(1)}, u32[]{:S(2)}, u32[]{:S(2)}) %all-to-all-start) | async-done | bytes 1310752 | tf_op jit(solution)/shard_map/all_to_all | solution.py:628
  52.2 19.1 %shard_map.426 = (f32[4,320,256]{2,1,0:T(8,128)}, f32[4,320,256]{2,1,0:T(8,128)}, f32[2,1152,160]{2,1,0:T(8,128)}, f32[2,8,160]{2,1,0:T(8,128)}) custom-call(s32[7]{0:T(128)} %stack.53.marks, f32[8,320,128]{2,1,0:T(8,128)} %copy-done.3, f32[1,160]{1,0:T(1,128)} %bitcast.212, f32[2,320]{1,0:T(2,128)} %fusion.75.tau, f32[1440,320]{1,0:T(8,128)} %bitcast.225), custom_call_target="tpu_custom_call" | custom-call | flops 5662310400 | bytes 10485760 | tf_op jit(solution)/shard_map/pallas_call | solution.py:1242
  80.6 10.5 %collective-permute-done.21 = f32[168,448]{1,0:T(8,128)S(1)} collective-permute-done((f32[168,448]{1,0:T(8,128)S(1)}, f32[168,448]{1,0:T(8,128)S(1)}, u32[]{:S(2)}, u32[]{:S(2)}) %collective-permute-start.21) | collective-permute-done | bytes 301088 | tf_op jit(solution)/shard_map/ppermute | solution.py:573
  116.9 14.4 %collective-permute-done.8.refs_1_.refs_9_ = f32[320,256]{1,0:T(8,128)} collective-permute-done((f32[320,256]{1,0:T(8,128)}, f32[320,256]{1,0:T(8,128)}, u32[]{:S(2)}, u32[]{:S(2)}) %collective-permute-start.8) | collective-permute-done | bytes 327712 | tf_op jit(solution)/shard_map/ppermute | solution.py:569
  132.3 12.5 %collective-permute-done.10.refs_3_.refs_11_ = f32[320,256]{1,0:T(8,128)} collective-permute-done((f32[320,256]{1,0:T(8,128)}, f32[320,256]{1,0:T(8,128)}, u32[]{:S(2)}, u32[]{:S(2)}) %collective-permute-start.10) | collective-permute-done | bytes 327712 | tf_op jit(solution)/shard_map/ppermute | solution.py:569
  153.2 21.4 %shard_map.427 = (f32[8,80,128]{2,1,0:T(8,128)}, f32[8,80,128]{2,1,0:T(8,128)}, f32[8,80,128]{2,1,0:T(8,128)}, f32[8,80,128]{2,1,0:T(8,128)}, f32[2,1152,320]{2,1,0:T(8,128)}, /*index=5*/f32[2,8,320]{2,1,0:T(8,128)}) custom-call(s32[7]{0:T(128)} %stack.53.marks, f32[320,256]{1,0:T(8,128)} %fusion.49.refs_0_.refs_8_, ...), custom_call_target="tpu_custom_call" | custom-call | flops 5662310400 | bytes 10485760 | tf_op jit(solution)/shard_map/pallas_call | solution.py:1242
  179.8 7.5 collective-permute-done.15.second
  187.4 12.2 %collective-permute-done.16.third = f32[8,80,128]{2,1,0:T(8,128)S(1)} collective-permute-done((f32[8,80,128]{2,1,0:T(8,128)}, f32[8,80,128]{2,1,0:T(8,128)S(1)}, u32[]{:S(2)}, u32[]{:S(2)}) %collective-permute-start.16) | collective-permute-done | bytes 327712 | tf_op jit(solution)/shard_map/ppermute | solution.py:573
  251.0 15.5 %collective-permute-done.28 = f32[77,640]{1,0:T(8,128)S(1)} collective-permute-done((f32[77,640]{1,0:T(8,128)S(1)}, f32[77,640]{1,0:T(8,128)S(1)}, u32[]{:S(2)}, u32[]{:S(2)}) %collective-permute-start.28) | collective-permute-done | bytes 197152 | tf_op jit(solution)/shard_map/ppermute | solution.py:569
  289.3 11.4 %collective-permute-done.29.refs_1_ = f32[256,640]{1,0:T(8,128)S(1)} collective-permute-done((f32[256,640]{1,0:T(8,128)S(1)}, f32[256,640]{1,0:T(8,128)S(1)}, u32[]{:S(2)}, u32[]{:S(2)}) %collective-permute-start.29) | collective-permute-done | bytes 655392 | tf_op jit(solution)/shard_map/ppermute | solution.py:569
  300.7 13.6 %collective-permute-done.30.refs_2_ = f32[256,640]{1,0:T(8,128)S(1)} collective-permute-done((f32[256,640]{1,0:T(8,128)S(1)}, f32[256,640]{1,0:T(8,128)S(1)}, u32[]{:S(2)}, u32[]{:S(2)}) %collective-permute-start.30) | collective-permute-done | bytes 655392 | tf_op jit(solution)/shard_map/ppermute | solution.py:569
  315.2 17.9 %all-to-all-done.4.pieces = f32[4,104,1280]{2,1,0:T(8,128)} async-done(((f32[4,104,1280]{2,1,0:T(8,128)}), f32[4,104,1280]{2,1,0:T(8,128)}, u32[]{:S(2)}, u32[]{:S(2)}) %all-to-all-start.4) | async-done | bytes 2129952 | tf_op jit(solution)/shard_map/all_to_all | solution.py:589
  349.8 8.5 collective-permute-done.32
  375.6 7.5 fusion.6
  406.1 22.2 %collective-permute-done.36 = f32[64,1280]{1,0:T(8,128)S(1)} collective-permute-done((f32[64,1280]{1,0:T(8,128)S(1)}, f32[64,1280]{1,0:T(8,128)S(1)}, u32[]{:S(2)}, u32[]{:S(2)}) %collective-permute-start.36) | collective-permute-done | bytes 327712 | tf_op jit(solution)/shard_map/ppermute | solution.py:573
  430.0 9.6 fusion.82
  452.2 8.2 collective-permute-done.38
  462.7 13.3 %shard_map.435.refs_3_ = f32[1280,6400]{1,0:T(8,128)} custom-call(f32[256,1280]{1,0:T(8,128)S(1)} %pad_maximum_fusion.4.refs_0_, f32[256,1280]{1,0:T(8,128)S(1)} %copy-done.2, f32[256,3840]{1,0:T(8,128)} %pad_maximum_fusion.refs_2_), custom_call_target="tpu_custom_call" | custom-call | flops 7549747200 | bytes 22020096 | tf_op jit(solution)/shard_map/pallas_call | solution.py:1288
  481.6 7.6 fusion
  501.3 11.7 %collective-permute-start.42 = (f32[64,1280]{1,0:T(8,128)}, f32[64,1280]{1,0:T(8,128)}, u32[]{:S(2)}, u32[]{:S(2)}) collective-permute-start(f32[64,1280]{1,0:T(8,128)} %multiply_add_fusion.1), channel_id=1, source_target_pairs={{0,2},{1,3},{2,0},{3,1},{4,6},{5,7},{6,4},{7,5},{8,10},{9,11},{10,... | collective-permute-start | bytes 983048 | tf_op jit(solution)/shard_map/ppermute | solution.py:573
  520.4 11.5 %shard_map.436 = f32[1280,6400]{1,0:T(8,128)} custom-call(f32[64,1280]{1,0:T(8,128)S(1)} %fusion.55.refs_0_, f32[64,1280]{1,0:T(8,128)S(1)} %multiply_add_fusion.2.refs_1_, f32[64,2560]{1,0:T(8,128)S(1)} %concatenate.89.refs_2_, f32[1280,6400]{1,0:T(8,128)} %shard_map.435.refs_3_), custom_call_target="tpu_custom_call", output_to_operand_aliasing={{}: (3, {})} | custom-call | flops 1258291200 | bytes 14680064 | tf_op jit(solution)/shard_map/pallas_call | solution.py:1288
  539.9 11.9 %shard_map.437 = (f32[256,320]{1,0:T(8,128)}, f32[256,640]{1,0:T(8,128)}, f32[256,640]{1,0:T(8,128)}, f32[256,640]{1,0:T(8,128)}, f32[256,640]{1,0:T(8,128)}) custom-call(s32[7]{0:T(128)} %stack.53.marks, f32[256,960]{1,0:T(8,128)} %copy-done.4, f32[256,640]{1,0:T(8,128)} %slice.327.refs_0_, f32[256,640]{1,0:T(8,128)} %copy-done.37, f32[256,640]{1,0:T(8,128)} %copy-done.38, ...), custom_call_target="tpu_custom_call" | custom-call | flops 4194304 | bytes 10485760 | tf_op jit(solution)/shard_map/pallas_call | solution.py:1242
  599.6 7.5 collective-permute-done.48
  675.0 10.5 %shard_map.442 = f32[1280,2560]{1,0:T(8,128)} custom-call(f32[256,1280]{1,0:T(8,128)S(1)} %constant_dynamic-update-slice_fusion.2.refs_0_, f32[256,1280]{1,0:T(8,128)S(1)} %constant_dynamic-update-slice_fusion.6.refs_1_, f32[256,1280]{1,0:T(8,128)S(1)} %pad.30.refs_2_, f32[256,2560]{1,0:T(8,128)} %concatenate.93.refs_3_), custom_call_target="tpu_custom_call" | custom-call | flops 5033164800 | bytes 14680064 | tf_op jit(solution)/shard_map/pallas_call | solution.py:1288
  691.2 19.7 %shard_map.443 = (f32[4,320,256]{2,1,0:T(8,128)}, f32[4,320,256]{2,1,0:T(8,128)}, f32[2,1152,160]{2,1,0:T(8,128)}) custom-call(s32[7]{0:T(128)} %stack.53.marks, f32[8,80,128]{2,1,0:T(8,128)} %get-tuple-element.298.refs_0_.base, f32[8,80,128]{2,1,0:T(8,128)} %collective-permute-done.56.refs_1_, f32[8,80,128]{2,1,0:T(8,128)} %copy-done.106, ...), custom_call_target="tpu_custom_call" | custom-call | flops 5662310400 | bytes 10485760 | tf_op jit(solution)/shard_map/pallas_call | solution.py:1242
  723.0 14.1 %collective-permute-done.61 = f32[320,256]{1,0:T(8,128)S(1)} collective-permute-done((f32[320,256]{1,0:T(8,128)S(1)}, f32[320,256]{1,0:T(8,128)S(1)}, u32[]{:S(2)}, u32[]{:S(2)}) %collective-permute-start.61) | collective-permute-done | bytes 327712 | tf_op jit(solution)/shard_map/ppermute | solution.py:569
  740.1 11.2 %collective-permute-done.63 = f32[320,256]{1,0:T(8,128)S(1)} collective-permute-done((f32[320,256]{1,0:T(8,128)S(1)}, f32[320,256]{1,0:T(8,128)S(1)}, u32[]{:S(2)}, u32[]{:S(2)}) %collective-permute-start.63) | collective-permute-done | bytes 327712 | tf_op jit(solution)/shard_map/ppermute | solution.py:569
  772.7 25.1 %shard_map.444 = (f32[8,80,128]{2,1,0:T(8,128)}, f32[8,80,128]{2,1,0:T(8,128)}, f32[8,80,128]{2,1,0:T(8,128)}, f32[8,80,128]{2,1,0:T(8,128)}, f32[2,1152,320]{2,...) custom-call(s32[7]{0:T(128)} %stack.53.marks, f32[320,256]{1,0:T(8,128)} %fusion.43.refs_0_, ...), custom_call_target="tpu_custom_call" | custom-call | flops 5662310400 | bytes 10485760 | tf_op jit(solution)/shard_map/pallas_call | solution.py:1242
  811.8 20.2 %shard_map.445 = f32[9,160,320]{2,1,0:T(8,128)} custom-call(s32[7]{0:T(128)} %stack.53.marks, f32[2,1152,160]{2,1,0:T(8,128)} %get-tuple-element.325.image, f32[2,1152,320]{2,1,0:T(8,128)} %get-tuple-element.328.cells), custom_call_target="tpu_custom_call" | custom-call | flops 5662310400 | bytes 10485760 | tf_op jit(solution)/shard_map/pallas_call | solution.py:1242
  840.9 12.7 %collective-permute-start.76 = (f32[8,160]{1,0:T(8,128)}, f32[8,160]{1,0:T(8,128)S(1)}, u32[]{:S(2)}, u32[]{:S(2)}) collective-permute-start(f32[8,160]{1,0:T(8,128)} %get-tuple-element.339.refs_0_), channel_id=1, source_target_pairs={{0,2},{1,3},{2,0},{3,1},{4,6},{5,7},{6,4},{7,5},{8,10},{9,11},{10,... | collective-permute-start | bytes 15368 | tf_op jit(solution)/shard_map/ppermute | solution.py:573
  885.2 20.5 %shard_map.448 = f32[9,160,320]{2,1,0:T(8,128)} custom-call(s32[7]{0:T(128)} %stack.53.marks, f32[2,1152,160]{2,1,0:T(8,128)} %get-tuple-element.346.image, f32[2,1152,320]{2,1,0:T(8,128)} %get-tuple-element.347.cells), custom_call_target="tpu_custom_call" | custom-call | flops 5662310400 | bytes 10485760 | tf_op jit(solution)/shard_map/pallas_call | solution.py:1242
  946.0 21.6 %collective-permute-done.81.refs_2_ = f32[64,1280]{1,0:T(8,128)S(1)} collective-permute-done((f32[64,1280]{1,0:T(8,128)S(1)}, f32[64,1280]{1,0:T(8,128)S(1)}, u32[]{:S(2)}, u32[]{:S(2)}) %collective-permute-start.81) | collective-permute-done | bytes 327712 | tf_op jit(solution)/shard_map/ppermute | solution.py:573
  (625 shorter events, 511.3 us)
Async XLA Ops:
  7.2 96.7 %all-gather.5.cloned.1.call-start = ((), (), s32[]{:S(2)}) async-start(), calls=%async_computation.11 | async-start | bytes 10321920 | tf_op jit(solution)/shard_map/all_gather | solution.py:1448
  18.6 32.6 %all-to-all-start = ((f32[8,320,128]{2,1,0:T(8,128)}), f32[8,320,128]{2,1,0:T(8,128)S(1)}, u32[]{:S(2)}, u32[]{:S(2)}) async-start(f32[8,320,128]{2,1,0:T(8,128)} %shard_map.425), calls=%async_computation | async-start | bytes 2621440 | tf_op jit(solution)/shard_map/all_to_all | solution.py:628
  23.5 209.9 %all-gather.7.cloned.1.call-start = ((), (), s32[]{:S(2)}) async-start(), calls=%async_computation.12 | async-start | bytes 22118400 | tf_op jit(solution)/shard_map/all_gather | solution.py:1448
  23.8 48.4 %collective-permute-start.1 = (f32[168,960]{1,0:T(8,128)S(1)}, f32[168,960]{1,0:T(8,128)S(1)}, u32[]{:S(2)}, u32[]{:S(2)}) collective-permute-start(f32[168,960]{1,0:T(8,128)S(1)} %select_maximum_fusion.refs_0_), channel_id=1, source_target_pairs={{0,3},{1,0},{2,1},{3,2},{4,7},{5,4},{6,5},{7,6},{8,11},{9,8},{10,9... | collective-permute-start | bytes 1935368 | tf_op jit(solution)/shard_map/ppermute | solution.py:573
  27.5 44.7 %collective-permute-start.3 = (f32[168,960]{1,0:T(8,128)S(1)}, f32[168,960]{1,0:T(8,128)}, u32[]{:S(2)}, u32[]{:S(2)}) collective-permute-start(f32[168,960]{1,0:T(8,128)S(1)} %select_maximum_fusion.refs_0_), channel_id=1, source_target_pairs={{0,1},{1,2},{2,3},{3,0},{4,5},{5,6},{6,7},{7,4},{8,9},{9,10},{10,1... | collective-permute-start | bytes 1935368 | tf_op jit(solution)/shard_map/ppermute | solution.py:573
  28.2 43.9 %collective-permute-start.2 = (f32[168,512]{1,0:T(8,128)}, f32[168,512]{1,0:T(8,128)S(1)}, u32[]{:S(2)}, u32[]{:S(2)}) collective-permute-start(f32[168,512]{1,0:T(8,128)} %slice.316), channel_id=1, source_target_pairs={{0,2},{1,3},{2,0},{3,1},{4,6},{5,7},{6,4},{7,5},{8,10},{9,11},{10,... | collective-permute-start | bytes 1032200 | tf_op jit(solution)/shard_map/ppermute | solution.py:573
  102.6 258.9 %all-gather.9.cloned.1.call-start = ((), (), s32[]{:S(2)}) async-start(), calls=%async_computation.13 | async-start | bytes 7372800 | tf_op jit(solution)/shard_map/all_gather | solution.py:1448
  108.6 44.5 %all-to-all-start.1 = ((f32[4,64,1600]{2,1,0:T(8,128)}), f32[4,64,1600]{2,1,0:T(8,128)S(1)}, u32[]{:S(2)}, u32[]{:S(2)}) async-start(f32[4,64,1600]{2,1,0:T(8,128)} %bitcast.178), calls=%async_computation.1 | async-start | bytes 3407872 | tf_op jit(solution)/shard_map/all_to_all | solution.py:589
  114.5 30.2 %collective-permute-start.10 = (f32[320,256]{1,0:T(8,128)}, f32[320,256]{1,0:T(8,128)}, u32[]{:S(2)}, u32[]{:S(2)}) collective-permute-start(f32[320,256]{1,0:T(8,128)} %fusion.49.refs_0_.refs_8_), channel_id=1, source_target_pairs={{0,12},{4,8},{8,4},{12,0},{1,13},{5,9},{9,5},{13,1},{2,14},{6,10},... | collective-permute-start | bytes 983048 | tf_op jit(solution)/shard_map/ppermute | solution.py:569
  116.9 30.9 %collective-permute-start.11 = (f32[320,256]{1,0:T(8,128)}, f32[320,256]{1,0:T(8,128)}, u32[]{:S(2)}, u32[]{:S(2)}) collective-permute-start(f32[320,256]{1,0:T(8,128)} %fusion.49.refs_0_.refs_8_), channel_id=1, source_target_pairs={{0,16},{16,0},{1,17},{17,1},{2,18},{18,2},{3,19},{19,3},{4,20},{20... | collective-permute-start | bytes 983048 | tf_op jit(solution)/shard_map/ppermute | solution.py:565
  179.8 43.1 %collective-permute-start.25 = (f32[77,256]{1,0:T(8,128)S(1)}, f32[77,256]{1,0:T(8,128)S(1)}, u32[]{:S(2)}, u32[]{:S(2)}) collective-permute-start(f32[77,256]{1,0:T(8,128)S(1)} %constant_dynamic-slice_fusion.9), channel_id=1, source_target_pairs={{0,16},{16,0},{1,17},{17,1},{2,18},{18,2},{3,19},{19,3},{4,20},{20... | collective-permute-start | bytes 236552 | tf_op jit(solution)/shard_map/ppermute | solution.py:565
  278.0 55.1 %all-to-all-start.4 = ((f32[4,104,1280]{2,1,0:T(8,128)}), f32[4,104,1280]{2,1,0:T(8,128)}, u32[]{:S(2)}, u32[]{:S(2)}) async-start(f32[4,104,1280]{2,1,0:T(8,128)} %broadcast_in_dim.21), calls=%async_computation.4 | async-start | bytes 4259840 | tf_op jit(solution)/shard_map/all_to_all | solution.py:589
  283.0 146.9 %all-gather.11.cloned.1.call-start = ((), (), s32[]{:S(2)}) async-start(), calls=%async_computation.14 | async-start | bytes 14745600 | tf_op jit(solution)/shard_map/all_gather | solution.py:1448
  284.2 30.1 %collective-permute-start.30 = (f32[256,640]{1,0:T(8,128)S(1)}, f32[256,640]{1,0:T(8,128)S(1)}, u32[]{:S(2)}, u32[]{:S(2)}) collective-permute-start(f32[256,640]{1,0:T(8,128)S(1)} %copy-done.17), channel_id=1, source_target_pairs={{0,8},{4,12},{8,0},{12,4},{1,9},{5,13},{9,1},{13,5},{2,10},{6,14},... | collective-permute-start | bytes 1966088 | tf_op jit(solution)/shard_map/ppermute | solution.py:569
  284.6 30.6 %collective-permute-start.31 = (f32[256,640]{1,0:T(8,128)S(1)}, f32[256,640]{1,0:T(8,128)}, u32[]{:S(2)}, u32[]{:S(2)}) collective-permute-start(f32[256,640]{1,0:T(8,128)S(1)} %copy-done.17), channel_id=1, source_target_pairs={{0,12},{4,8},{8,4},{12,0},{1,13},{5,9},{9,5},{13,1},{2,14},{6,10},... | collective-permute-start | bytes 1966088 | tf_op jit(solution)/shard_map/ppermute | solution.py:569
  340.1 492.7 %reduce-scatter.3.cloned.1.call-start = ((), (), s32[]{:S(2)}) async-start(), calls=%async_computation.15 | async-start | bytes 36864000 | tf_op jit(solution)/shard_map/reduce_scatter | solution.py:1452
  397.5 30.8 %collective-permute-start.36 = (f32[64,1280]{1,0:T(8,128)S(1)}, f32[64,1280]{1,0:T(8,128)S(1)}, u32[]{:S(2)}, u32[]{:S(2)}) collective-permute-start(f32[64,1280]{1,0:T(8,128)S(1)} %fusion.56), channel_id=1, source_target_pairs={{0,2},{1,3},{2,0},{3,1},{4,6},{5,7},{6,4},{7,5},{8,10},{9,11},{10,... | collective-permute-start | bytes 983048 | tf_op jit(solution)/shard_map/ppermute | solution.py:573
  447.9 32.0 %collective-permute-start.39 = (f32[64,1280]{1,0:T(8,128)}, f32[64,1280]{1,0:T(8,128)S(1)}, u32[]{:S(2)}, u32[]{:S(2)}) collective-permute-start(f32[64,1280]{1,0:T(8,128)} %get-tuple-element.456), channel_id=1, source_target_pairs={{0,2},{1,3},{2,0},{3,1},{4,6},{5,7},{6,4},{7,5},{8,10},{9,11},{10,... | collective-permute-start | bytes 983048 | tf_op jit(solution)/shard_map/ppermute | solution.py:573
  448.2 31.8 %collective-permute-start.40 = (f32[64,1280]{1,0:T(8,128)}, f32[64,1280]{1,0:T(8,128)}, u32[]{:S(2)}, u32[]{:S(2)}) collective-permute-start(f32[64,1280]{1,0:T(8,128)} %get-tuple-element.455), channel_id=1, source_target_pairs={{0,3},{1,0},{2,1},{3,2},{4,7},{5,4},{6,5},{7,6},{8,11},{9,8},{10,9... | collective-permute-start | bytes 983048 | tf_op jit(solution)/shard_map/ppermute | solution.py:573
  501.3 30.6 %collective-permute-start.42 = (f32[64,1280]{1,0:T(8,128)}, f32[64,1280]{1,0:T(8,128)}, u32[]{:S(2)}, u32[]{:S(2)}) collective-permute-start(f32[64,1280]{1,0:T(8,128)} %multiply_add_fusion.1), channel_id=1, source_target_pairs={{0,2},{1,3},{2,0},{3,1},{4,6},{5,7},{6,4},{7,5},{8,10},{9,11},{10,... | collective-permute-start | bytes 983048 | tf_op jit(solution)/shard_map/ppermute | solution.py:573
  558.2 51.0 %all-to-all-start.5 = ((f32[4,64,1280]{2,1,0:T(8,128)}), f32[4,64,1280]{2,1,0:T(8,128)}, u32[]{:S(2)}, u32[]{:S(2)}) async-start(f32[4,64,1280]{2,1,0:T(8,128)} %bitcast.188), calls=%async_computation.5 | async-start | bytes 2621440 | tf_op jit(solution)/shard_map/all_to_all | solution.py:589
  636.7 231.5 %reduce-scatter.5.cloned.1.call-start = ((), (), s32[]{:S(2)}) async-start(), calls=%async_computation.16 | async-start | bytes 14745600 | tf_op jit(solution)/shard_map/reduce_scatter | solution.py:1452
  715.4 55.4 %all-to-all-start.7 = ((f32[4,72,1600]{2,1,0:T(8,128)}), f32[4,72,1600]{2,1,0:T(8,128)S(1)}, u32[]{:S(2)}, u32[]{:S(2)}) async-start(f32[4,72,1600]{2,1,0:T(8,128)} %pad_maximum_fusion.2), calls=%async_computation.7 | async-start | bytes 3833856 | tf_op jit(solution)/shard_map/all_to_all | solution.py:589
  799.7 36.9 %collective-permute-start.72 = (f32[8,80,128]{2,1,0:T(8,128)}, f32[8,80,128]{2,1,0:T(8,128)}, u32[]{:S(2)}, u32[]{:S(2)}) collective-permute-start(f32[8,80,128]{2,1,0:T(8,128)} %get-tuple-element.323), channel_id=1, source_target_pairs={{0,2},{1,3},{2,0},{3,1},{4,6},{5,7},{6,4},{7,5},{8,10},{9,11},{10,... | collective-permute-start | bytes 983048 | tf_op jit(solution)/shard_map/ppermute | solution.py:573
  802.1 34.5 %collective-permute-start.73 = (f32[8,80,128]{2,1,0:T(8,128)}, f32[8,80,128]{2,1,0:T(8,128)}, u32[]{:S(2)}, u32[]{:S(2)}) collective-permute-start(f32[8,80,128]{2,1,0:T(8,128)} %get-tuple-element.324), channel_id=1, source_target_pairs={{0,3},{1,0},{2,1},{3,2},{4,7},{5,4},{6,5},{7,6},{8,11},{9,8},{10,9... | collective-permute-start | bytes 983048 | tf_op jit(solution)/shard_map/ppermute | solution.py:573
  855.6 86.6 %collective-permute-start.86 = (f32[160,640]{1,0:T(8,128)}, f32[160,640]{1,0:T(8,128)}, u32[]{:S(2)}, u32[]{:S(2)}) collective-permute-start(f32[160,640]{1,0:T(8,128)} %get-tuple-element.362), channel_id=1, source_target_pairs={{0,1},{1,2},{2,3},{3,0},{4,5},{5,6},{6,7},{7,4},{8,9},{9,10},{10,1... | collective-permute-start | bytes 1228808 | tf_op jit(solution)/shard_map/ppermute | solution.py:573
  864.1 52.6 %all-to-all-start.8 = ((f32[8,88,128]{2,1,0:T(8,128)}), f32[8,88,128]{2,1,0:T(8,128)}, u32[]{:S(2)}, u32[]{:S(2)}) async-start(f32[8,88,128]{2,1,0:T(8,128)} %get-tuple-element.340), calls=%async_computation.9 | async-start | bytes 720896 | tf_op jit(solution)/shard_map/all_to_all | solution.py:628
  871.5 42.9 %collective-permute-start.79 = (f32[4,160,320]{2,1,0:T(8,128)}, f32[4,160,320]{2,1,0:T(8,128)}, u32[]{:S(2)}, u32[]{:S(2)}) collective-permute-start(f32[4,160,320]{2,1,0:T(8,128)} %dynamic-slice_bitcast_fusion), channel_id=1, source_target_pairs={{0,16},{16,0},{1,17},{17,1},{2,18},{18,2},{3,19},{19,3},{4,20},{20... | collective-permute-start | bytes 2457608 | tf_op jit(solution)/shard_map/ppermute | solution.py:565
  879.7 30.5 %collective-permute-start.83 = (f32[160,320]{1,0:T(8,128)S(1)}, f32[160,320]{1,0:T(8,128)S(1)}, u32[]{:S(2)}, u32[]{:S(2)}) collective-permute-start(f32[160,320]{1,0:T(8,128)S(1)} %bitcast.209), channel_id=1, source_target_pairs={{0,1},{1,2},{2,3},{3,0},{4,5},{5,6},{6,7},{7,4},{8,9},{9,10},{10,1... | collective-permute-start | bytes 614408 | tf_op jit(solution)/shard_map/ppermute | solution.py:573
  880.3 30.4 %collective-permute-start.84 = (f32[160,320]{1,0:T(8,128)S(1)}, f32[160,320]{1,0:T(8,128)S(1)}, u32[]{:S(2)}, u32[]{:S(2)}) collective-permute-start(f32[160,320]{1,0:T(8,128)S(1)} %bitcast.208), channel_id=1, source_target_pairs={{0,2},{1,3},{2,0},{3,1},{4,6},{5,7},{6,4},{7,5},{8,10},{9,11},{10,... | collective-permute-start | bytes 614408 | tf_op jit(solution)/shard_map/ppermute | solution.py:573
  910.2 33.5 %collective-permute-start.87 = (f32[160,640]{1,0:T(8,128)}, f32[160,640]{1,0:T(8,128)}, u32[]{:S(2)}, u32[]{:S(2)}) collective-permute-start(f32[160,640]{1,0:T(8,128)} %get-tuple-element.363), channel_id=1, source_target_pairs={{0,2},{1,3},{2,0},{3,1},{4,6},{5,7},{6,4},{7,5},{8,10},{9,11},{10,... | collective-permute-start | bytes 1228808 | tf_op jit(solution)/shard_map/ppermute | solution.py:573
  910.8 33.0 %collective-permute-start.88 = (f32[160,640]{1,0:T(8,128)}, f32[160,640]{1,0:T(8,128)}, u32[]{:S(2)}, u32[]{:S(2)}) collective-permute-start(f32[160,640]{1,0:T(8,128)} %get-tuple-element.364), channel_id=1, source_target_pairs={{0,3},{1,0},{2,1},{3,2},{4,7},{5,4},{6,5},{7,6},{8,11},{9,8},{10,9... | collective-permute-start | bytes 1228808 | tf_op jit(solution)/shard_map/ppermute | solution.py:573
  (189 other events, 2319.4 us)
Sparse Core Ops, SparseCore 0:
  10.7 77.3 all-gather.4
  102.8 115.1 all-gather.6
  219.9 54.7 all-gather.8
  340.2 71.2 all-gather.10
  532.1 220.7 reduce-scatter.2
  756.3 99.4 reduce-scatter.4
